TPU v7x, 1024 devices: a whole 4x4x32 slice. The times are simulated.
1024 devices in a mesh: dp: 256 (over x, z, y_hi), pipe: 4 (over y_lo, core).
Axes of the slice: x: 4, y: 4 (y_hi: 2, y_lo: 2; y = y_hi * 2 + y_lo), z: 32, core: 2. Of those that a mesh axis runs over, the one named last changes fastest.
Arguments:
- text_states: bfloat16 [4, 16384, 4096], P('pipe', 'dp')
- image_states: bfloat16 [4, 16384, 4096], P(None, ('dp', 'pipe'))
- image_start: int32 [4, 256], P(None, 'dp'), may hold values from 0 to 31
- w_query: bfloat16 [4, 4096, 512], P('pipe')
- w_key: bfloat16 [4, 4096, 128], P('pipe', 'dp')
- w_value: bfloat16 [4, 4096, 128], P('pipe', 'dp'), may hold values from -0.09375 to 0.09375
- w_out: bfloat16 [4, 512, 4096], P('pipe'), may hold values from -0.25 to 0.25
- query_gain: float32 [4, 128], P('pipe'), may hold values from 1 to 2.5
- key_gain: float32 [4, 128], P('pipe'), may hold values from 1 to 2
- cross_gate: float32 [4], P('pipe'), may hold values from 0.3 to 1.2
Outputs:
- final_states: bfloat16 [4, 16384, 4096], P('pipe', 'dp')
All inputs are finite; a program needn't handle non-finite values.
Results may differ from a plain program's by a relative error of at most 0.013.
Values may be sent and summed in bfloat16 or wider, within the bound.
No kernel may reach another device: no remote copies, remote signals or barrier semaphores. Data moves between devices by JAX's collectives and lax.ppermute only.
A program may use at most 64 MiB of HBM per device.

v0:
```python
import math

import jax
import jax.numpy as jnp
from jax import lax
from jax.sharding import PartitionSpec as P

epsilon = 1e-06


def shifted(block, axis, distance):
    devices = range(lax.axis_size(axis))
    route = [((i - distance) % len(devices), i) for i in devices]
    return lax.ppermute(block, axis, route)


def normalized(projected, scales):
    mean_square = jnp.mean(projected * projected, axis=-1, keepdims=True)
    return projected * lax.rsqrt(mean_square + epsilon) * scales


def keep_state(current, holding):
    return current


def local(
    text_states,
    image_states,
    image_start,
    w_query,
    w_key,
    w_value,
    w_out,
    query_gain,
    key_gain,
    cross_gate,
):
    sections = lax.axis_size("pipe")
    section_index = lax.axis_index("pipe")
    pictures = lax.all_gather(image_states, "pipe", axis=1, tiled=True)
    batches, image_rows, width = pictures.shape
    flattened = pictures.reshape(batches * image_rows, width)
    head_size = w_key.shape[2]
    head_count = w_query.shape[2] // head_size
    key_full, value_full = (
        lax.all_gather(w_key, "dp", axis=1, tiled=True),
        lax.all_gather(w_value, "dp", axis=1, tiled=True),
    )
    key_sums = jnp.dot(flattened, key_full[0], preferred_element_type=jnp.float32)
    value_sums = jnp.dot(flattened, value_full[0], preferred_element_type=jnp.float32)
    key_rows = (
        normalized(key_sums, key_gain[0])
        .astype(jnp.bfloat16)
        .reshape(batches, image_rows, head_size)
    )
    value_rows = value_sums.astype(jnp.bfloat16).reshape(batches, image_rows, head_size)
    query_weight = w_query[0]
    out_weight = w_out[0]
    factor = jnp.tanh(cross_gate[0])
    tok_rows = text_states.shape[1]
    positions = jnp.arange(tok_rows, dtype=jnp.int32)
    root_size = math.sqrt(head_size)

    def apply_layer(current, holding):
        own_keys = lax.dynamic_index_in_dim(key_rows, holding, 0, keepdims=False)
        own_values = lax.dynamic_index_in_dim(value_rows, holding, 0, keepdims=False)
        query_sums = jnp.dot(current, query_weight, preferred_element_type=jnp.float32)
        query_sums = query_sums.reshape(tok_rows * head_count, head_size)
        queries = normalized(query_sums, query_gain[0]).astype(jnp.bfloat16)
        scores = jnp.dot(queries, own_keys.T, preferred_element_type=jnp.float32) / root_size
        exponent = jnp.exp(scores)
        probs = (exponent / jnp.sum(exponent, axis=-1, keepdims=True)).astype(jnp.bfloat16)
        attended = jnp.dot(probs, own_values, preferred_element_type=jnp.float32).astype(
            jnp.bfloat16
        )
        attended = attended.reshape(tok_rows, head_count * head_size)
        update = jnp.dot(attended, out_weight, preferred_element_type=jnp.float32)
        first_seen = lax.dynamic_index_in_dim(image_start[:, 0], holding, 0, keepdims=False)
        seen = (positions >= first_seen).astype(jnp.float32)[:, None]
        return (current.astype(jnp.float32) + factor * seen * update).astype(jnp.bfloat16)

    current = text_states[0]
    for moment in range(sections):
        holding = jnp.mod(section_index - moment, sections)
        current = lax.cond(moment <= section_index, apply_layer, keep_state, current, holding)
        current = shifted(current, "pipe", 1)
    return current[None]


def solution(mesh):
    placed = (
        P("pipe", "dp", None),
        P(None, ("dp", "pipe"), None),
        P(None, "dp"),
        P("pipe", None, None),
        P("pipe", "dp", None),
        P("pipe", "dp", None),
        P("pipe", None, None),
        P("pipe", None),
        P("pipe", None),
        P("pipe"),
    )
    return jax.shard_map(
        local, mesh=mesh, in_specs=placed, out_specs=P("pipe", "dp", None), check_vma=False
    )
```

profile of v0, /device:TPU:2, one launch (start us, length us, event | category | flops | bytes accessed | tf_op | source)
XLA Modules:
  0.0 884.1 jit_solution(17323513968056919281)
XLA Ops:
  6.5 0.0 copy-start
  6.5 0.0 copy-start.3
  6.5 0.0 copy-start.1
  6.5 0.0 copy-start.2
  6.5 0.0 all-gather.6.cloned.1.call-start
  6.6 0.7 all-gather.6.cloned.1.call-update
  7.3 0.0 all-gather.4.cloned.1.call-start
  7.3 0.7 all-gather.4.cloned.1.call-update
  8.0 0.0 all-gather.8.cloned.1.call-start
  8.1 0.7 all-gather.8.cloned.1.call-update
  9.4 381.0 %all-gather.6.cloned.1.call-done = bf16[1,4096,128]{2,1,0:T(8,128)(2,1)} async-done(((bf16[1,16,128]{2,1,0:T(8,128)(2,1)}), bf16[1,4096,128]{2,1,0:T(8,128)(2,1)}) %all-gather.6.cloned.1.call-update) | async-done | bytes 1048592 | tf_op jit(solution)/shard_map/all_gather | solution.py:46
  390.4 38.8 %all-gather.4.cloned.1.call-done = bf16[4,64,4096]{2,1,0:T(8,128)(2,1)} async-done(((bf16[4,16,4096]{2,1,0:T(8,128)(2,1)}), bf16[4,64,4096]{2,1,0:T(8,128)(2,1)}) %all-gather.4.cloned.1.call-update) | async-done | bytes 2097168 | tf_op jit(solution)/shard_map/all_gather | solution.py:40
  429.2 2.6 multiply_reduce_fusion
  431.8 0.0 copy-done.2
  431.9 0.1 multiply_convert_fusion
  432.0 374.1 %all-gather.8.cloned.1.call-done = bf16[1,4096,128]{2,1,0:T(8,128)(2,1)} async-done(((bf16[1,16,128]{2,1,0:T(8,128)(2,1)}), bf16[1,4096,128]{2,1,0:T(8,128)(2,1)}) %all-gather.8.cloned.1.call-update) | async-done | bytes 1048592 | tf_op jit(solution)/shard_map/all_gather | solution.py:47
  806.0 2.5 convolution_convert_fusion.4
  808.6 0.0 copy-done
  808.6 0.0 copy-done.3
  808.6 0.0 copy-done.1
  808.6 8.2 conditional.4
  808.7 3.0 fusion.51
  811.7 0.1 reduce_sum.88
  811.8 0.1 rsqrt.52
  812.0 0.1 mul.200
  812.1 0.1 convert_element_type.106
  812.2 0.2 fusion.52
  812.4 0.2 convolution_convert_fusion
  812.6 0.1 reshape.179
  812.6 0.6 constant_dynamic-slice_fusion
  813.2 0.6 compare_select_fusion
  813.8 3.1 fusion.1
  816.9 1.9 collective-permute-start
  818.8 8.6 collective-permute-done
  827.4 8.6 collective-permute-start.1
  836.0 7.8 collective-permute-done.1
  843.8 2.6 collective-permute-start.2
  846.5 13.8 %collective-permute-done.2 = bf16[64,4096]{1,0:T(8,128)(2,1)S(1)} collective-permute-done((bf16[64,4096]{1,0:T(8,128)(2,1)S(1)}, bf16[64,4096]{1,0:T(8,128)(2,1)S(1)}, u32[]{:S(2)}, u32[]{:S(2)}) %collective-permute-start.2) | collective-permute-done | bytes 524320 | tf_op jit(solution)/shard_map/ppermute | solution.py:14
  860.3 5.1 collective-permute-start.3
  865.4 11.3 %collective-permute-done.3 = bf16[64,4096]{1,0:T(8,128)(2,1)S(1)} collective-permute-done((bf16[64,4096]{1,0:T(8,128)(2,1)S(1)}, bf16[64,4096]{1,0:T(8,128)(2,1)S(1)}, u32[]{:S(2)}, u32[]{:S(2)}) %collective-permute-start.3) | collective-permute-done | bytes 524320 | tf_op jit(solution)/shard_map/ppermute | solution.py:14
  876.7 0.8 copy.31
  (12 shorter events, 0.1 us)
Async XLA Ops:
  6.5 802.1 %copy-start = (bf16[1,64,4096]{2,1,0:T(8,128)(2,1)S(1)}, bf16[1,64,4096]{2,1,0:T(8,128)(2,1)}, u32[]{:S(2)}) copy-start(bf16[1,64,4096]{2,1,0:T(8,128)(2,1)} %param.18) | copy-start | bytes 1572868
  6.5 802.1 %copy-start.3 = (s32[4,1]{0,1:T(1,128)S(1)}, s32[4,1]{0,1:T(1,128)}, u32[]{:S(2)}) copy-start(s32[4,1]{0,1:T(1,128)} %param.20) | copy-start | bytes 52
  6.5 802.1 %copy-start.1 = (f32[1,128]{1,0:T(1,128)S(1)}, f32[1,128]{1,0:T(1,128)}, u32[]{:S(2)}) copy-start(f32[1,128]{1,0:T(1,128)} %param.25) | copy-start | bytes 1540
  6.5 425.3 %copy-start.2 = (f32[1,128]{1,0:T(1,128)S(1)}, f32[1,128]{1,0:T(1,128)}, u32[]{:S(2)}) copy-start(f32[1,128]{1,0:T(1,128)} %param.26) | copy-start | bytes 1540
  6.5 383.9 %all-gather.6.cloned.1.call-start = ((), (), s32[]{:S(2)}) async-start(), calls=%async_computation.1 | async-start | bytes 1052672 | tf_op jit(solution)/shard_map/all_gather | solution.py:46
  7.3 421.9 %all-gather.4.cloned.1.call-start = ((), (), s32[]{:S(2)}) async-start(), calls=%async_computation | async-start | bytes 2621440 | tf_op jit(solution)/shard_map/all_gather | solution.py:40
  8.0 798.0 %all-gather.8.cloned.1.call-start = ((), (), s32[]{:S(2)}) async-start(), calls=%async_computation.2 | async-start | bytes 1052672 | tf_op jit(solution)/shard_map/all_gather | solution.py:47
  816.9 10.5 %collective-permute-start = (bf16[64,4096]{1,0:T(8,128)(2,1)S(1)}, bf16[64,4096]{1,0:T(8,128)(2,1)S(1)}, u32[]{:S(2)}, u32[]{:S(2)}) collective-permute-start(bf16[64,4096]{1,0:T(8,128)(2,1)S(1)} %get-tuple-element.553), channel_id=1, source_target_pairs={{3,0},{0,1},{1,2},{2,3},{7,4},{4,5},{5,6},{6,7},{11,8},{8,9},{9,10... | collective-permute-start | bytes 1572872 | tf_op jit(solution)/shard_map/ppermute | solution.py:14
  827.4 16.4 %collective-permute-start.1 = (bf16[64,4096]{1,0:T(8,128)(2,1)S(1)}, bf16[64,4096]{1,0:T(8,128)(2,1)S(1)}, u32[]{:S(2)}, u32[]{:S(2)}) collective-permute-start(bf16[64,4096]{1,0:T(8,128)(2,1)S(1)} %get-tuple-element.554), channel_id=1, source_target_pairs={{3,0},{0,1},{1,2},{2,3},{7,4},{4,5},{5,6},{6,7},{11,8},{8,9},{9,10... | collective-permute-start | bytes 1572872 | tf_op jit(solution)/shard_map/ppermute | solution.py:14
  843.8 16.4 %collective-permute-start.2 = (bf16[64,4096]{1,0:T(8,128)(2,1)S(1)}, bf16[64,4096]{1,0:T(8,128)(2,1)S(1)}, u32[]{:S(2)}, u32[]{:S(2)}) collective-permute-start(bf16[64,4096]{1,0:T(8,128)(2,1)S(1)} %get-tuple-element.555), channel_id=1, source_target_pairs={{3,0},{0,1},{1,2},{2,3},{7,4},{4,5},{5,6},{6,7},{11,8},{8,9},{9,10... | collective-permute-start | bytes 1572872 | tf_op jit(solution)/shard_map/ppermute | solution.py:14
  860.3 16.4 %collective-permute-start.3 = (bf16[64,4096]{1,0:T(8,128)(2,1)S(1)}, bf16[64,4096]{1,0:T(8,128)(2,1)S(1)}, u32[]{:S(2)}, u32[]{:S(2)}) collective-permute-start(bf16[64,4096]{1,0:T(8,128)(2,1)S(1)} %get-tuple-element.556), channel_id=1, source_target_pairs={{3,0},{0,1},{1,2},{2,3},{7,4},{4,5},{5,6},{6,7},{11,8},{8,9},{9,10... | collective-permute-start | bytes 1572872 | tf_op jit(solution)/shard_map/ppermute | solution.py:14
Sparse Core Ops, SparseCore 0:
  13.2 377.2 all-gather.5
  393.1 36.0 all-gather.3
  435.0 370.9 all-gather.7
where the time goes:
time: 885 us; the launch traced here: 884 us
  waiting for transfers between devices  837 us (95%)
  starting transfers between devices  18.4 us (2%)
  between operations  13.9 us (2%)
  matrix products  11.7 us (1%)
    all_gather x1, waiting for transfers between devices, local(): lax.all_gather(w_key, 'dp', axis=1, tiled=True)  381 us
    all_gather x1, waiting for transfers between devices, local(): lax.all_gather(w_value, 'dp', axis=1, tiled=True)  374 us
    ppermute x4, waiting for transfers between devices, shifted(): return lax.ppermute(block, axis, route)  41.5 us
    all_gather x1, waiting for transfers between devices, local(): pictures = lax.all_gather(image_states, 'pipe', axis=1, tiled=True)  38.8 us
    ppermute x4, starting transfers between devices, shifted(): return lax.ppermute(block, axis, route)  18.3 us
  transfers between devices with their start and end apart: 7, of which 7 were waited for; matrix products, arithmetic and copies ran while one was open for 0% of the time, Pallas kernels for 0%

commit v1 on v0

--- a/solution.py
+++ b/solution.py
@@ -3,6 +3,7 @@
 import jax
 import jax.numpy as jnp
 from jax import lax
+from jax.sharding import Mesh
 from jax.sharding import PartitionSpec as P
 
 epsilon = 1e-06
@@ -23,6 +24,47 @@
     return current
 
 
+def exchanged(block, axis, distance):
+    devices = range(lax.axis_size(axis))
+    return lax.ppermute(block, axis, [(i, i ^ distance) for i in devices])
+
+
+def doubled(known, axis, distance, where):
+    other = exchanged(known, axis, distance)
+    upper = (lax.axis_index(axis) & distance) != 0
+    first = jnp.where(upper, other, known)
+    second = jnp.where(upper, known, other)
+    return jnp.stack([first, second], axis=where)
+
+
+def gathered_rows(shard):
+    rows, columns = shard.shape
+    known = doubled(shard[None], "yh", 1, 1)
+    distance = lax.axis_size("z") // 2
+    while distance >= 1:
+        known = doubled(known, "z", distance, 1)
+        known = known.reshape((-1,) + known.shape[2:])
+        distance //= 2
+    return known.reshape(-1, columns)
+
+
+def column_slices(image_states):
+    batches, rows, width = image_states.shape
+    parts = lax.axis_size("x")
+    own = lax.axis_index("x")
+    cut = jnp.moveaxis(image_states.reshape(batches, rows, parts, width // parts), 2, 0)
+    blocks = [
+        exchanged(lax.dynamic_index_in_dim(cut, own ^ distance, 0, keepdims=False), "x", distance)
+        if distance
+        else lax.dynamic_index_in_dim(cut, own, 0, keepdims=False)
+        for distance in range(parts)
+    ]
+    ordered = jnp.stack(blocks)
+    ordered = jnp.take(ordered, own ^ jnp.arange(parts), axis=0)
+    halves = doubled(ordered, "pipe", 2, 0)
+    return doubled(halves, "pipe", 1, 1).reshape((-1,) + ordered.shape)
+
+
 def local(
     text_states,
     image_states,
@@ -37,23 +79,23 @@
 ):
     sections = lax.axis_size("pipe")
     section_index = lax.axis_index("pipe")
-    pictures = lax.all_gather(image_states, "pipe", axis=1, tiled=True)
-    batches, image_rows, width = pictures.shape
-    flattened = pictures.reshape(batches * image_rows, width)
     head_size = w_key.shape[2]
     head_count = w_query.shape[2] // head_size
-    key_full, value_full = (
-        lax.all_gather(w_key, "dp", axis=1, tiled=True),
-        lax.all_gather(w_value, "dp", axis=1, tiled=True),
-    )
-    key_sums = jnp.dot(flattened, key_full[0], preferred_element_type=jnp.float32)
-    value_sums = jnp.dot(flattened, value_full[0], preferred_element_type=jnp.float32)
-    key_rows = (
-        normalized(key_sums, key_gain[0])
-        .astype(jnp.bfloat16)
-        .reshape(batches, image_rows, head_size)
-    )
-    value_rows = value_sums.astype(jnp.bfloat16).reshape(batches, image_rows, head_size)
+    weights = gathered_rows(jnp.concatenate([w_key[0], w_value[0]], axis=1))
+    pictures = column_slices(image_states)
+    parts, depth = lax.axis_size("x"), weights.shape[0]
+    sums = jnp.dot(pictures.reshape(-1, depth), weights, preferred_element_type=jnp.float32)
+    sums = sums.reshape(pictures.shape[:-1] + (2 * head_size,))
+    own = lax.axis_index("x")
+    total = lax.dynamic_index_in_dim(sums, own, 1, keepdims=False)
+    rounded = sums.astype(jnp.bfloat16)
+    for distance in range(1, parts):
+        block = lax.dynamic_index_in_dim(rounded, own ^ distance, 1, keepdims=False)
+        total = total + exchanged(block, "x", distance).astype(jnp.float32)
+    total = jnp.swapaxes(total, 0, 1)
+    total = total.reshape(total.shape[0], -1, 2 * head_size)
+    key_rows = normalized(total[..., :head_size], key_gain[0]).astype(jnp.bfloat16)
+    value_rows = total[..., head_size:].astype(jnp.bfloat16)
     query_weight = w_query[0]
     out_weight = w_out[0]
     factor = jnp.tanh(cross_gate[0])
@@ -88,18 +130,23 @@
 
 
 def solution(mesh):
+    sections = mesh.shape["pipe"]
+    planes, far = 4, 2
+    groups = mesh.shape["dp"] // (planes * far)
+    mesh = Mesh(mesh.devices.reshape(planes, groups, far, sections), ("x", "z", "yh", "pipe"))
+    replicas = ("x", "z", "yh")
     placed = (
-        P("pipe", "dp", None),
-        P(None, ("dp", "pipe"), None),
-        P(None, "dp"),
+        P("pipe", replicas, None),
+        P(None, replicas + ("pipe",), None),
+        P(None, replicas),
         P("pipe", None, None),
-        P("pipe", "dp", None),
-        P("pipe", "dp", None),
+        P("pipe", replicas, None),
+        P("pipe", replicas, None),
         P("pipe", None, None),
         P("pipe", None),
         P("pipe", None),
         P("pipe"),
     )
     return jax.shard_map(
-        local, mesh=mesh, in_specs=placed, out_specs=P("pipe", "dp", None), check_vma=False
+        local, mesh=mesh, in_specs=placed, out_specs=P("pipe", replicas, None), check_vma=False
     )

time: 885 us -> 185 us (0.21)
  the two profiles are of different devices: /device:TPU:2 before, /device:TPU:1 now
where the time goes in v1:
time: 185 us; the launch traced here: 184 us
  starting transfers between devices  112 us (61%)
  waiting for transfers between devices  45.6 us (25%)
  matrix products  13.7 us (7%)
  local copies, waits for them, and re-layouts  6.42 us (3%)
  other arithmetic  4.44 us (2%)
    ppermute x14, starting transfers between devices, exchanged(): return lax.ppermute(block, axis, [(i, i ^ distance) for i in devices])  81.3 us
    ppermute x4, starting transfers between devices, shifted(): return lax.ppermute(block, axis, route)  31.2 us
    ppermute x4, waiting for transfers between devices, shifted(): return lax.ppermute(block, axis, route)  24.4 us
    ppermute x14, waiting for transfers between devices, exchanged(): return lax.ppermute(block, axis, [(i, i ^ distance) for i in devices])  21.2 us
    dot_general x2, matrix products, apply_layer(): update = jnp.dot(attended, out_weight, preferred_element_type=jnp.float32)  6.19 us
    dot_general x2, matrix products, apply_layer(): jnp.dot(current, query_weight, preferred_element_type=jnp.float32)  6.05 us
  transfers between devices with their start and end apart: 18, of which 9 were waited for; matrix products, arithmetic and copies ran while one was open for 2% of the time, Pallas kernels for 0%

profile of v1, /device:TPU:1, one launch (start us, length us, event | category | flops | bytes accessed | tf_op | source)
XLA Modules:
  0.0 184.2 jit_solution(15271923987978421978)
XLA Ops:
  0.0 0.8 maximum_bitcast_fusion.1
  0.8 5.6 %collective-permute-start.5 = (bf16[1,16,256]{2,1,0:T(8,128)(2,1)S(1)}, bf16[1,16,256]{2,1,0:T(8,128)(2,1)S(1)}, u32[]{:S(2)}, u32[]{:S(2)}) collective-permute-start(bf16[1,16,256]{2,1,0:T(8,128)(2,1)S(1)} %maximum_bitcast_fusion.1), channel_id=1, source_target_pairs={{0,4},{4,0},{1,5},{5,1},{2,6},{6,2},{3,7},{7,3},{8,12},{12,8},{9,1... | collective-permute-start | bytes 24584 | tf_op jit(solution)/shard_map/ppermute | solution.py:29
  6.4 1.4 reshape.227
  7.9 1.1 constant_dynamic-slice_fusion.7
  9.0 4.4 %collective-permute-start.2 = (bf16[4,16,1024]{2,1,0:T(8,128)(2,1)S(1)}, bf16[4,16,1024]{2,1,0:T(8,128)(2,1)S(1)}, u32[]{:S(2)}, u32[]{:S(2)}) collective-permute-start(bf16[4,16,1024]{2,1,0:T(8,128)(2,1)S(1)} %bitcast.225), channel_id=1, source_target_pairs={{0,768},{256,512},{512,256},{768,0},{1,769},{257,513},{513,257},{7... | collective-permute-start | bytes 393224 | tf_op jit(solution)/shard_map/ppermute | solution.py:29
  13.5 1.9 %collective-permute-start = (bf16[4,16,1024]{2,1,0:T(8,128)(2,1)S(1)}, bf16[4,16,1024]{2,1,0:T(8,128)(2,1)S(1)}, u32[]{:S(2)}, u32[]{:S(2)}) collective-permute-start(bf16[4,16,1024]{2,1,0:T(8,128)(2,1)S(1)} %bitcast.226), channel_id=1, source_target_pairs={{0,256},{256,0},{512,768},{768,512},{1,257},{257,1},{513,769},{769... | collective-permute-start | bytes 393224 | tf_op jit(solution)/shard_map/ppermute | solution.py:29
  15.5 3.3 %collective-permute-start.1 = (bf16[4,16,1024]{2,1,0:T(8,128)(2,1)S(1)}, bf16[4,16,1024]{2,1,0:T(8,128)(2,1)S(1)}, u32[]{:S(2)}, u32[]{:S(2)}) collective-permute-start(bf16[4,16,1024]{2,1,0:T(8,128)(2,1)S(1)} %bitcast.227), channel_id=1, source_target_pairs={{0,512},{256,768},{512,0},{768,256},{1,513},{257,769},{513,1},{769... | collective-permute-start | bytes 393224 | tf_op jit(solution)/shard_map/ppermute | solution.py:29
  18.8 28.7 %collective-permute-start.6 = (bf16[1,2,16,256]{3,2,1,0:T(8,128)(2,1)S(1)}, bf16[1,2,16,256]{3,2,1,0:T(8,128)(2,1)S(1)}, u32[]{:S(2)}, u32[]{:S(2)}) collective-permute-start(bf16[1,2,16,256]{3,2,1,0:T(8,128)(2,1)S(1)} %pad_maximum_fusion.7), channel_id=1, source_target_pairs={{0,128},{8,136},{16,144},{24,152},{32,160},{40,168},{48,176},{56,1... | collective-permute-start | bytes 49160 | tf_op jit(solution)/shard_map/ppermute | solution.py:29
  47.5 1.1 collective-permute-done.6
  48.7 8.4 %collective-permute-start.7 = (bf16[2,2,16,256]{3,2,1,0:T(8,128)(2,1)S(1)}, bf16[2,2,16,256]{3,2,1,0:T(8,128)(2,1)S(1)}, u32[]{:S(2)}, u32[]{:S(2)}) collective-permute-start(bf16[2,2,16,256]{3,2,1,0:T(8,128)(2,1)S(1)} %maximum_bitcast_fusion), channel_id=1, source_target_pairs={{0,64},{8,72},{16,80},{24,88},{32,96},{40,104},{48,112},{56,120},{... | collective-permute-start | bytes 98312 | tf_op jit(solution)/shard_map/ppermute | solution.py:29
  57.2 4.9 %collective-permute-done.7 = bf16[2,2,16,256]{3,2,1,0:T(8,128)(2,1)S(1)} collective-permute-done((bf16[2,2,16,256]{3,2,1,0:T(8,128)(2,1)S(1)}, bf16[2,2,16,256]{3,2,1,0:T(8,128)(2,1)S(1)}, u32[]{:S(2)}, u32[]{:S(2)}) %collective-permute-start.7) | collective-permute-done | bytes 32800 | tf_op jit(solution)/shard_map/ppermute | solution.py:29
  62.1 0.1 pad_maximum_fusion.2
  62.2 0.6 gather_fusion
  62.7 0.1 broadcast_select_fusion
  62.9 2.3 %collective-permute-start.3 = (bf16[4,4,16,1024]{3,2,1,0:T(8,128)(2,1)S(1)}, bf16[4,4,16,1024]{3,2,1,0:T(8,128)(2,1)S(1)}, u32[]{:S(2)}, u32[]{:S(2)}) collective-permute-start(bf16[4,4,16,1024]{3,2,1,0:T(8,128)(2,1)S(1)} %broadcast_select_fusion), channel_id=1, source_target_pairs={{0,2},{1,3},{2,0},{3,1},{4,6},{5,7},{6,4},{7,5},{8,10},{9,11},{10,... | collective-permute-start | bytes 1572872 | tf_op jit(solution)/shard_map/ppermute | solution.py:29
  65.2 5.2 %collective-permute-start.8 = (bf16[4,2,16,256]{3,2,1,0:T(8,128)(2,1)S(1)}, bf16[4,2,16,256]{3,2,1,0:T(8,128)(2,1)S(1)}, u32[]{:S(2)}, u32[]{:S(2)}) collective-permute-start(bf16[4,2,16,256]{3,2,1,0:T(8,128)(2,1)S(1)} %bitcast.224), channel_id=1, source_target_pairs={{0,32},{8,40},{16,48},{24,56},{32,0},{40,8},{48,16},{56,24},{64,96... | collective-permute-start | bytes 196616 | tf_op jit(solution)/shard_map/ppermute | solution.py:29
  70.4 5.8 %collective-permute-done.8 = bf16[4,2,16,256]{3,2,1,0:T(8,128)(2,1)S(1)} collective-permute-done((bf16[4,2,16,256]{3,2,1,0:T(8,128)(2,1)S(1)}, bf16[4,2,16,256]{3,2,1,0:T(8,128)(2,1)S(1)}, u32[]{:S(2)}, u32[]{:S(2)}) %collective-permute-start.8) | collective-permute-done | bytes 65568 | tf_op jit(solution)/shard_map/ppermute | solution.py:29
  76.3 1.9 %collective-permute-start.9 = (bf16[8,2,16,256]{3,2,1,0:T(8,128)(2,1)S(1)}, bf16[8,2,16,256]{3,2,1,0:T(8,128)(2,1)S(1)}, u32[]{:S(2)}, u32[]{:S(2)}) collective-permute-start(bf16[8,2,16,256]{3,2,1,0:T(8,128)(2,1)S(1)} %bitcast.217), channel_id=1, source_target_pairs={{0,16},{8,24},{16,0},{24,8},{32,48},{40,56},{48,32},{56,40},{64,80... | collective-permute-start | bytes 393224 | tf_op jit(solution)/shard_map/ppermute | solution.py:29
  78.2 0.1 select_bitcast_fusion.3
  78.4 0.1 pad_maximum_fusion.1
  78.5 7.9 %collective-permute-start.4 = (bf16[2,4,4,16,1024]{4,3,2,1,0:T(8,128)(2,1)S(1)}, bf16[2,4,4,16,1024]{4,3,2,1,0:T(8,128)(2,1)S(1)}, u32[]{:S(2)}, u32[]{:S(2)}) collective-permute-start(bf16[2,4,4,16,1024]{4,3,2,1,0:T(8,128)(2,1)S(1)} %pad_maximum_fusion.1), channel_id=1, source_target_pairs={{0,1},{1,0},{2,3},{3,2},{4,5},{5,4},{6,7},{7,6},{8,9},{9,8},{10,11... | collective-permute-start | bytes 3145736 | tf_op jit(solution)/shard_map/ppermute | solution.py:29
  86.5 2.0 %collective-permute-start.10 = (bf16[16,2,16,256]{3,2,1,0:T(8,128)(2,1)S(1)}, bf16[16,2,16,256]{3,2,1,0:T(8,128)(2,1)}, u32[]{:S(2)}, u32[]{:S(2)}) collective-permute-start(bf16[16,2,16,256]{3,2,1,0:T(8,128)(2,1)S(1)} %bitcast.216), channel_id=1, source_target_pairs={{0,8},{8,0},{16,24},{24,16},{32,40},{40,32},{48,56},{56,48},{64,72... | collective-permute-start | bytes 786440 | tf_op jit(solution)/shard_map/ppermute | solution.py:29
  88.5 5.2 %collective-permute-done.10 = bf16[16,2,16,256]{3,2,1,0:T(8,128)(2,1)} collective-permute-done((bf16[16,2,16,256]{3,2,1,0:T(8,128)(2,1)S(1)}, bf16[16,2,16,256]{3,2,1,0:T(8,128)(2,1)}, u32[]{:S(2)}, u32[]{:S(2)}) %collective-permute-start.10) | collective-permute-done | bytes 262176 | tf_op jit(solution)/shard_map/ppermute | solution.py:29
  93.7 1.0 select_bitcast_fusion.5
  94.8 0.1 select_bitcast_fusion.1
  95.0 0.2 pad_maximum_fusion
  95.2 0.3 copy.25
  95.6 0.7 fusion.60
  96.3 1.9 %collective-permute-start.11 = (bf16[4,4,16,256]{3,2,1,0:T(8,128)(2,1)S(1)}, bf16[4,4,16,256]{3,2,1,0:T(8,128)(2,1)S(1)}, u32[]{:S(2)}, u32[]{:S(2)}) collective-permute-start(bf16[4,4,16,256]{3,2,1,0:T(8,128)(2,1)S(1)} %get-tuple-element.555), channel_id=1, source_target_pairs={{0,256},{256,0},{512,768},{768,512},{1,257},{257,1},{513,769},{769... | collective-permute-start | bytes 393224 | tf_op jit(solution)/shard_map/ppermute | solution.py:29
  98.3 5.3 %collective-permute-start.12 = (bf16[4,4,16,256]{3,2,1,0:T(8,128)(2,1)S(1)}, bf16[4,4,16,256]{3,2,1,0:T(8,128)(2,1)S(1)}, u32[]{:S(2)}, u32[]{:S(2)}) collective-permute-start(bf16[4,4,16,256]{3,2,1,0:T(8,128)(2,1)S(1)} %get-tuple-element.557), channel_id=1, source_target_pairs={{0,512},{256,768},{512,0},{768,256},{1,513},{257,769},{513,1},{769... | collective-permute-start | bytes 393224 | tf_op jit(solution)/shard_map/ppermute | solution.py:29
  103.6 2.3 %collective-permute-start.13 = (bf16[4,4,16,256]{3,2,1,0:T(8,128)(2,1)S(1)}, bf16[4,4,16,256]{3,2,1,0:T(8,128)(2,1)S(1)}, u32[]{:S(2)}, u32[]{:S(2)}) collective-permute-start(bf16[4,4,16,256]{3,2,1,0:T(8,128)(2,1)S(1)} %get-tuple-element.556), channel_id=1, source_target_pairs={{0,768},{256,512},{512,256},{768,0},{1,769},{257,513},{513,257},{7... | collective-permute-start | bytes 393224 | tf_op jit(solution)/shard_map/ppermute | solution.py:29
  106.6 4.2 %collective-permute-done.13 = bf16[4,4,16,256]{3,2,1,0:T(8,128)(2,1)S(1)} collective-permute-done((bf16[4,4,16,256]{3,2,1,0:T(8,128)(2,1)S(1)}, bf16[4,4,16,256]{3,2,1,0:T(8,128)(2,1)S(1)}, u32[]{:S(2)}, u32[]{:S(2)}) %collective-permute-start.13) | collective-permute-done | bytes 131104 | tf_op jit(solution)/shard_map/ppermute | solution.py:29
  110.8 0.1 fusion.50
  110.9 0.1 multiply_reduce_fusion
  111.1 0.1 multiply_convert_fusion
  111.2 8.3 %conditional.4 = (bf16[64,4096]{1,0:T(8,128)(2,1)S(1)}) conditional(s32[]{:T(128)} %convert_element_type.147, bf16[64,4096]{1,0:T(8,128)(2,1)S(1)} %bitcast.210, (bf16[64,4096]{1,0:T(8,128)(2,1)S(1)}, s32[]{:T(128)}, s32[4,1]{0,1:T(1,128)S(1)}, s32[64]{0:T(128)S(1)}, f32[]{:T(128)}, /*index=5*/bf16[4096,512]{1,0:T(8,128)(2,1)}, ...), branch_computations={%region_1.2_spmd, %region_2.5_spmd} | conditional | flops 546570368 | bytes 11711927 | solution.py:127
  111.3 3.0 %fusion.52 = (f32[64,512]{1,0:T(8,128)S(1)}, f32[64,512]{1,0:T(8,128)S(1)}) fusion(bf16[64,4096]{1,0:T(8,128)(2,1)S(1)} %get-tuple-element.429, bf16[4096,512]{1,0:T(8,128)(2,1)} %get-tuple-element.434), kind=kOutput, calls=%fused_computation.136 | convolution fusion | flops 268468224 | bytes 4980736 | tf_op jit(solution)/shard_map/cond/branch_1_fun/dot_general | solution.py:109
  114.3 0.1 reduce_sum.88
  114.4 0.1 rsqrt.52
  114.5 0.1 mul.200
  114.8 0.2 fusion.53
  115.0 0.2 convolution_convert_fusion
  115.2 0.6 constant_dynamic-slice_fusion
  115.8 0.6 compare_select_fusion
  116.4 3.1 %fusion.1 = bf16[64,4096]{1,0:T(8,128)(2,1)S(1)} fusion(bf16[64,512]{1,0:T(8,128)(2,1)S(1)} %reshape.217, bf16[512,4096]{1,0:T(8,128)(2,1)} %get-tuple-element.438, bf16[64,4096]{1,0:T(8,128)(2,1)S(1)} %get-tuple-element.429, f32[64]{0:T(128)S(1)} %compare_select_fusion), kind=kOutput, calls=%fused_computation.3 | convolution fusion | flops 269484032 | bytes 5308672 | tf_op jit(solution)/shard_map/cond/branch_1_fun/dot_general | solution.py:119
  119.5 9.8 %collective-permute-start.14 = (bf16[64,4096]{1,0:T(8,128)(2,1)S(1)}, bf16[64,4096]{1,0:T(8,128)(2,1)S(1)}, u32[]{:S(2)}, u32[]{:S(2)}) collective-permute-start(bf16[64,4096]{1,0:T(8,128)(2,1)S(1)} %get-tuple-element.576), channel_id=1, source_target_pairs={{3,0},{0,1},{1,2},{2,3},{7,4},{4,5},{5,6},{6,7},{11,8},{8,9},{9,10... | collective-permute-start | bytes 1572872 | tf_op jit(solution)/shard_map/ppermute | solution.py:15
  129.3 6.1 %collective-permute-done.14 = bf16[64,4096]{1,0:T(8,128)(2,1)S(1)} collective-permute-done((bf16[64,4096]{1,0:T(8,128)(2,1)S(1)}, bf16[64,4096]{1,0:T(8,128)(2,1)S(1)}, u32[]{:S(2)}, u32[]{:S(2)}) %collective-permute-start.14) | collective-permute-done | bytes 524320 | tf_op jit(solution)/shard_map/ppermute | solution.py:15
  135.4 8.2 %conditional.5 = (bf16[64,4096]{1,0:T(8,128)(2,1)S(1)}) conditional(s32[]{:T(128)} %convert_element_type.146, bf16[64,4096]{1,0:T(8,128)(2,1)S(1)} %collective-permute-done.14, (bf16[64,4096]{1,0:T(8,128)(2,1)S(1)}, s32[]{:T(128)}, s32[4,1]{0,1:T(1,128)S(1)}, s32[64]{0:T(128)S(1)}, f32[]{:T(128)}, /*index=5*/bf16[4096,512]{1,0:T(8,128)(2,1)}, ...), branch_computations={%region_5.6_spmd, %region_6.9_spmd.clone} | conditional | flops 546570368 | bytes 11711939 | solution.py:127
  135.4 3.0 %fusion.54 = (f32[64,512]{1,0:T(8,128)S(1)}, f32[64,512]{1,0:T(8,128)S(1)}) fusion(bf16[64,4096]{1,0:T(8,128)(2,1)S(1)} %get-tuple-element.475, bf16[4096,512]{1,0:T(8,128)(2,1)} %get-tuple-element.479), kind=kOutput, calls=%fused_computation.138 | convolution fusion | flops 268468224 | bytes 4980736 | tf_op jit(solution)/shard_map/cond/branch_1_fun/dot_general | solution.py:109
  138.4 0.1 reduce_sum.98
  138.6 0.1 rsqrt.62
  138.7 0.1 mul.268
  138.9 0.2 fusion.55
  139.1 0.2 convolution_convert_fusion.1
  139.4 0.6 constant_dynamic-slice_fusion.1
  139.9 0.6 compare_select_fusion.1
  140.5 3.1 %fusion.13 = bf16[64,4096]{1,0:T(8,128)(2,1)S(1)} fusion(bf16[64,512]{1,0:T(8,128)(2,1)S(1)} %reshape.233, bf16[512,4096]{1,0:T(8,128)(2,1)} %get-tuple-element.483, bf16[64,4096]{1,0:T(8,128)(2,1)S(1)} %get-tuple-element.475, f32[64]{0:T(128)S(1)} %compare_select_fusion.1), kind=kOutput, calls=%fused_computation.24 | convolution fusion | flops 269484032 | bytes 5308672 | tf_op jit(solution)/shard_map/cond/branch_1_fun/dot_general | solution.py:119
  143.6 4.4 %collective-permute-start.15 = (bf16[64,4096]{1,0:T(8,128)(2,1)S(1)}, bf16[64,4096]{1,0:T(8,128)(2,1)S(1)}, u32[]{:S(2)}, u32[]{:S(2)}) collective-permute-start(bf16[64,4096]{1,0:T(8,128)(2,1)S(1)} %get-tuple-element.577), channel_id=1, source_target_pairs={{3,0},{0,1},{1,2},{2,3},{7,4},{4,5},{5,6},{6,7},{11,8},{8,9},{9,10... | collective-permute-start | bytes 1572872 | tf_op jit(solution)/shard_map/ppermute | solution.py:15
  148.0 6.1 %collective-permute-done.15 = bf16[64,4096]{1,0:T(8,128)(2,1)S(1)} collective-permute-done((bf16[64,4096]{1,0:T(8,128)(2,1)S(1)}, bf16[64,4096]{1,0:T(8,128)(2,1)S(1)}, u32[]{:S(2)}, u32[]{:S(2)}) %collective-permute-start.15) | collective-permute-done | bytes 524320 | tf_op jit(solution)/shard_map/ppermute | solution.py:15
  154.1 12.6 %collective-permute-start.16 = (bf16[64,4096]{1,0:T(8,128)(2,1)S(1)}, bf16[64,4096]{1,0:T(8,128)(2,1)S(1)}, u32[]{:S(2)}, u32[]{:S(2)}) collective-permute-start(bf16[64,4096]{1,0:T(8,128)(2,1)S(1)} %get-tuple-element.578), channel_id=1, source_target_pairs={{3,0},{0,1},{1,2},{2,3},{7,4},{4,5},{5,6},{6,7},{11,8},{8,9},{9,10... | collective-permute-start | bytes 1572872 | tf_op jit(solution)/shard_map/ppermute | solution.py:15
  166.8 6.1 %collective-permute-done.16 = bf16[64,4096]{1,0:T(8,128)(2,1)S(1)} collective-permute-done((bf16[64,4096]{1,0:T(8,128)(2,1)S(1)}, bf16[64,4096]{1,0:T(8,128)(2,1)S(1)}, u32[]{:S(2)}, u32[]{:S(2)}) %collective-permute-start.16) | collective-permute-done | bytes 524320 | tf_op jit(solution)/shard_map/ppermute | solution.py:15
  172.9 4.4 %collective-permute-start.17 = (bf16[64,4096]{1,0:T(8,128)(2,1)S(1)}, bf16[64,4096]{1,0:T(8,128)(2,1)S(1)}, u32[]{:S(2)}, u32[]{:S(2)}) collective-permute-start(bf16[64,4096]{1,0:T(8,128)(2,1)S(1)} %get-tuple-element.579), channel_id=1, source_target_pairs={{3,0},{0,1},{1,2},{2,3},{7,4},{4,5},{5,6},{6,7},{11,8},{8,9},{9,10... | collective-permute-start | bytes 1572872 | tf_op jit(solution)/shard_map/ppermute | solution.py:15
  177.3 6.1 %collective-permute-done.17 = bf16[64,4096]{1,0:T(8,128)(2,1)S(1)} collective-permute-done((bf16[64,4096]{1,0:T(8,128)(2,1)S(1)}, bf16[64,4096]{1,0:T(8,128)(2,1)S(1)}, u32[]{:S(2)}, u32[]{:S(2)}) %collective-permute-start.17) | collective-permute-done | bytes 524320 | tf_op jit(solution)/shard_map/ppermute | solution.py:15
  183.4 0.8 copy.64
  (64 shorter events, 0.9 us)
Async XLA Ops:
  0.0 18.8 %copy-start.2 = (bf16[1,16,128]{2,1,0:T(8,128)(2,1)S(1)}, bf16[1,16,128]{2,1,0:T(8,128)(2,1)}, u32[]{:S(2)}) copy-start(bf16[1,16,128]{2,1,0:T(8,128)(2,1)} %param.22) | copy-start | bytes 12292
  0.0 18.8 %copy-start.1 = (bf16[1,16,128]{2,1,0:T(8,128)(2,1)S(1)}, bf16[1,16,128]{2,1,0:T(8,128)(2,1)}, u32[]{:S(2)}) copy-start(bf16[1,16,128]{2,1,0:T(8,128)(2,1)} %param.23) | copy-start | bytes 12292
  0.8 18.0 %collective-permute-start.5 = (bf16[1,16,256]{2,1,0:T(8,128)(2,1)S(1)}, bf16[1,16,256]{2,1,0:T(8,128)(2,1)S(1)}, u32[]{:S(2)}, u32[]{:S(2)}) collective-permute-start(bf16[1,16,256]{2,1,0:T(8,128)(2,1)S(1)} %maximum_bitcast_fusion.1), channel_id=1, source_target_pairs={{0,4},{4,0},{1,5},{5,1},{2,6},{6,2},{3,7},{7,3},{8,12},{12,8},{9,1... | collective-permute-start | bytes 24584 | tf_op jit(solution)/shard_map/ppermute | solution.py:29
  9.0 53.0 %collective-permute-start.2 = (bf16[4,16,1024]{2,1,0:T(8,128)(2,1)S(1)}, bf16[4,16,1024]{2,1,0:T(8,128)(2,1)S(1)}, u32[]{:S(2)}, u32[]{:S(2)}) collective-permute-start(bf16[4,16,1024]{2,1,0:T(8,128)(2,1)S(1)} %bitcast.225), channel_id=1, source_target_pairs={{0,768},{256,512},{512,256},{768,0},{1,769},{257,513},{513,257},{7... | collective-permute-start | bytes 393224 | tf_op jit(solution)/shard_map/ppermute | solution.py:29
  13.5 48.6 %collective-permute-start = (bf16[4,16,1024]{2,1,0:T(8,128)(2,1)S(1)}, bf16[4,16,1024]{2,1,0:T(8,128)(2,1)S(1)}, u32[]{:S(2)}, u32[]{:S(2)}) collective-permute-start(bf16[4,16,1024]{2,1,0:T(8,128)(2,1)S(1)} %bitcast.226), channel_id=1, source_target_pairs={{0,256},{256,0},{512,768},{768,512},{1,257},{257,1},{513,769},{769... | collective-permute-start | bytes 393224 | tf_op jit(solution)/shard_map/ppermute | solution.py:29
  15.5 46.6 %collective-permute-start.1 = (bf16[4,16,1024]{2,1,0:T(8,128)(2,1)S(1)}, bf16[4,16,1024]{2,1,0:T(8,128)(2,1)S(1)}, u32[]{:S(2)}, u32[]{:S(2)}) collective-permute-start(bf16[4,16,1024]{2,1,0:T(8,128)(2,1)S(1)} %bitcast.227), channel_id=1, source_target_pairs={{0,512},{256,768},{512,0},{768,256},{1,513},{257,769},{513,1},{769... | collective-permute-start | bytes 393224 | tf_op jit(solution)/shard_map/ppermute | solution.py:29
  18.8 29.8 %collective-permute-start.6 = (bf16[1,2,16,256]{3,2,1,0:T(8,128)(2,1)S(1)}, bf16[1,2,16,256]{3,2,1,0:T(8,128)(2,1)S(1)}, u32[]{:S(2)}, u32[]{:S(2)}) collective-permute-start(bf16[1,2,16,256]{3,2,1,0:T(8,128)(2,1)S(1)} %pad_maximum_fusion.7), channel_id=1, source_target_pairs={{0,128},{8,136},{16,144},{24,152},{32,160},{40,168},{48,176},{56,1... | collective-permute-start | bytes 49160 | tf_op jit(solution)/shard_map/ppermute | solution.py:29
  48.7 13.4 %collective-permute-start.7 = (bf16[2,2,16,256]{3,2,1,0:T(8,128)(2,1)S(1)}, bf16[2,2,16,256]{3,2,1,0:T(8,128)(2,1)S(1)}, u32[]{:S(2)}, u32[]{:S(2)}) collective-permute-start(bf16[2,2,16,256]{3,2,1,0:T(8,128)(2,1)S(1)} %maximum_bitcast_fusion), channel_id=1, source_target_pairs={{0,64},{8,72},{16,80},{24,88},{32,96},{40,104},{48,112},{56,120},{... | collective-permute-start | bytes 98312 | tf_op jit(solution)/shard_map/ppermute | solution.py:29
  62.9 15.3 %collective-permute-start.3 = (bf16[4,4,16,1024]{3,2,1,0:T(8,128)(2,1)S(1)}, bf16[4,4,16,1024]{3,2,1,0:T(8,128)(2,1)S(1)}, u32[]{:S(2)}, u32[]{:S(2)}) collective-permute-start(bf16[4,4,16,1024]{3,2,1,0:T(8,128)(2,1)S(1)} %broadcast_select_fusion), channel_id=1, source_target_pairs={{0,2},{1,3},{2,0},{3,1},{4,6},{5,7},{6,4},{7,5},{8,10},{9,11},{10,... | collective-permute-start | bytes 1572872 | tf_op jit(solution)/shard_map/ppermute | solution.py:29
  65.2 11.0 %collective-permute-start.8 = (bf16[4,2,16,256]{3,2,1,0:T(8,128)(2,1)S(1)}, bf16[4,2,16,256]{3,2,1,0:T(8,128)(2,1)S(1)}, u32[]{:S(2)}, u32[]{:S(2)}) collective-permute-start(bf16[4,2,16,256]{3,2,1,0:T(8,128)(2,1)S(1)} %bitcast.224), channel_id=1, source_target_pairs={{0,32},{8,40},{16,48},{24,56},{32,0},{40,8},{48,16},{56,24},{64,96... | collective-permute-start | bytes 196616 | tf_op jit(solution)/shard_map/ppermute | solution.py:29
  76.3 10.1 %collective-permute-start.9 = (bf16[8,2,16,256]{3,2,1,0:T(8,128)(2,1)S(1)}, bf16[8,2,16,256]{3,2,1,0:T(8,128)(2,1)S(1)}, u32[]{:S(2)}, u32[]{:S(2)}) collective-permute-start(bf16[8,2,16,256]{3,2,1,0:T(8,128)(2,1)S(1)} %bitcast.217), channel_id=1, source_target_pairs={{0,16},{8,24},{16,0},{24,8},{32,48},{40,56},{48,32},{56,40},{64,80... | collective-permute-start | bytes 393224 | tf_op jit(solution)/shard_map/ppermute | solution.py:29
  78.5 16.4 %collective-permute-start.4 = (bf16[2,4,4,16,1024]{4,3,2,1,0:T(8,128)(2,1)S(1)}, bf16[2,4,4,16,1024]{4,3,2,1,0:T(8,128)(2,1)S(1)}, u32[]{:S(2)}, u32[]{:S(2)}) collective-permute-start(bf16[2,4,4,16,1024]{4,3,2,1,0:T(8,128)(2,1)S(1)} %pad_maximum_fusion.1), channel_id=1, source_target_pairs={{0,1},{1,0},{2,3},{3,2},{4,5},{5,4},{6,7},{7,6},{8,9},{9,8},{10,11... | collective-permute-start | bytes 3145736 | tf_op jit(solution)/shard_map/ppermute | solution.py:29
  86.5 7.2 %collective-permute-start.10 = (bf16[16,2,16,256]{3,2,1,0:T(8,128)(2,1)S(1)}, bf16[16,2,16,256]{3,2,1,0:T(8,128)(2,1)}, u32[]{:S(2)}, u32[]{:S(2)}) collective-permute-start(bf16[16,2,16,256]{3,2,1,0:T(8,128)(2,1)S(1)} %bitcast.216), channel_id=1, source_target_pairs={{0,8},{8,0},{16,24},{24,16},{32,40},{40,32},{48,56},{56,48},{64,72... | collective-permute-start | bytes 786440 | tf_op jit(solution)/shard_map/ppermute | solution.py:29
  95.5 15.6 %copy-start.4 = (f32[1,128]{1,0:T(1,128)S(1)}, f32[1,128]{1,0:T(1,128)}, u32[]{:S(2)}) copy-start(f32[1,128]{1,0:T(1,128)} %param.26) | copy-start | bytes 1540
  95.5 15.7 %copy-start = (bf16[1,64,4096]{2,1,0:T(8,128)(2,1)S(1)}, bf16[1,64,4096]{2,1,0:T(8,128)(2,1)}, u32[]{:S(2)}) copy-start(bf16[1,64,4096]{2,1,0:T(8,128)(2,1)} %param.18) | copy-start | bytes 1572868
  95.5 15.7 %copy-start.3 = (f32[1,128]{1,0:T(1,128)S(1)}, f32[1,128]{1,0:T(1,128)}, u32[]{:S(2)}) copy-start(f32[1,128]{1,0:T(1,128)} %param.25) | copy-start | bytes 1540
  95.5 15.7 %copy-start.5 = (s32[4,1]{0,1:T(1,128)S(1)}, s32[4,1]{0,1:T(1,128)}, u32[]{:S(2)}) copy-start(s32[4,1]{0,1:T(1,128)} %param.20) | copy-start | bytes 52
  96.3 10.3 %collective-permute-start.11 = (bf16[4,4,16,256]{3,2,1,0:T(8,128)(2,1)S(1)}, bf16[4,4,16,256]{3,2,1,0:T(8,128)(2,1)S(1)}, u32[]{:S(2)}, u32[]{:S(2)}) collective-permute-start(bf16[4,4,16,256]{3,2,1,0:T(8,128)(2,1)S(1)} %get-tuple-element.555), channel_id=1, source_target_pairs={{0,256},{256,0},{512,768},{768,512},{1,257},{257,1},{513,769},{769... | collective-permute-start | bytes 393224 | tf_op jit(solution)/shard_map/ppermute | solution.py:29
  98.3 8.4 %collective-permute-start.12 = (bf16[4,4,16,256]{3,2,1,0:T(8,128)(2,1)S(1)}, bf16[4,4,16,256]{3,2,1,0:T(8,128)(2,1)S(1)}, u32[]{:S(2)}, u32[]{:S(2)}) collective-permute-start(bf16[4,4,16,256]{3,2,1,0:T(8,128)(2,1)S(1)} %get-tuple-element.557), channel_id=1, source_target_pairs={{0,512},{256,768},{512,0},{768,256},{1,513},{257,769},{513,1},{769... | collective-permute-start | bytes 393224 | tf_op jit(solution)/shard_map/ppermute | solution.py:29
  103.6 7.2 %collective-permute-start.13 = (bf16[4,4,16,256]{3,2,1,0:T(8,128)(2,1)S(1)}, bf16[4,4,16,256]{3,2,1,0:T(8,128)(2,1)S(1)}, u32[]{:S(2)}, u32[]{:S(2)}) collective-permute-start(bf16[4,4,16,256]{3,2,1,0:T(8,128)(2,1)S(1)} %get-tuple-element.556), channel_id=1, source_target_pairs={{0,768},{256,512},{512,256},{768,0},{1,769},{257,513},{513,257},{7... | collective-permute-start | bytes 393224 | tf_op jit(solution)/shard_map/ppermute | solution.py:29
  119.5 15.9 %collective-permute-start.14 = (bf16[64,4096]{1,0:T(8,128)(2,1)S(1)}, bf16[64,4096]{1,0:T(8,128)(2,1)S(1)}, u32[]{:S(2)}, u32[]{:S(2)}) collective-permute-start(bf16[64,4096]{1,0:T(8,128)(2,1)S(1)} %get-tuple-element.576), channel_id=1, source_target_pairs={{3,0},{0,1},{1,2},{2,3},{7,4},{4,5},{5,6},{6,7},{11,8},{8,9},{9,10... | collective-permute-start | bytes 1572872 | tf_op jit(solution)/shard_map/ppermute | solution.py:15
  143.6 10.5 %collective-permute-start.15 = (bf16[64,4096]{1,0:T(8,128)(2,1)S(1)}, bf16[64,4096]{1,0:T(8,128)(2,1)S(1)}, u32[]{:S(2)}, u32[]{:S(2)}) collective-permute-start(bf16[64,4096]{1,0:T(8,128)(2,1)S(1)} %get-tuple-element.577), channel_id=1, source_target_pairs={{3,0},{0,1},{1,2},{2,3},{7,4},{4,5},{5,6},{6,7},{11,8},{8,9},{9,10... | collective-permute-start | bytes 1572872 | tf_op jit(solution)/shard_map/ppermute | solution.py:15
  154.1 18.7 %collective-permute-start.16 = (bf16[64,4096]{1,0:T(8,128)(2,1)S(1)}, bf16[64,4096]{1,0:T(8,128)(2,1)S(1)}, u32[]{:S(2)}, u32[]{:S(2)}) collective-permute-start(bf16[64,4096]{1,0:T(8,128)(2,1)S(1)} %get-tuple-element.578), channel_id=1, source_target_pairs={{3,0},{0,1},{1,2},{2,3},{7,4},{4,5},{5,6},{6,7},{11,8},{8,9},{9,10... | collective-permute-start | bytes 1572872 | tf_op jit(solution)/shard_map/ppermute | solution.py:15
  172.9 10.5 %collective-permute-start.17 = (bf16[64,4096]{1,0:T(8,128)(2,1)S(1)}, bf16[64,4096]{1,0:T(8,128)(2,1)S(1)}, u32[]{:S(2)}, u32[]{:S(2)}) collective-permute-start(bf16[64,4096]{1,0:T(8,128)(2,1)S(1)} %get-tuple-element.579), channel_id=1, source_target_pairs={{3,0},{0,1},{1,2},{2,3},{7,4},{4,5},{5,6},{6,7},{11,8},{8,9},{9,10... | collective-permute-start | bytes 1572872 | tf_op jit(solution)/shard_map/ppermute | solution.py:15

commit v2 on v1

--- a/solution.py
+++ b/solution.py
@@ -1,8 +1,11 @@
+import functools
 import math
 
 import jax
 import jax.numpy as jnp
 from jax import lax
+from jax.experimental import pallas as pl
+from jax.experimental.pallas import tpu as pltpu
 from jax.sharding import Mesh
 from jax.sharding import PartitionSpec as P
 
@@ -20,8 +23,110 @@
     return projected * lax.rsqrt(mean_square + epsilon) * scales
 
 
-def keep_state(current, holding):
-    return current
+def layer_kernel(
+    parts,
+    moment_ref,
+    first_seen_ref,
+    factor_ref,
+    current_ref,
+    key_ref,
+    value_ref,
+    gain_ref,
+    w_query_ref,
+    w_out_ref,
+    out_ref,
+    query_weight,
+    out_weight,
+    sems,
+):
+    rows, width = current_ref.shape
+    columns = w_query_ref.shape[1]
+    head_size = key_ref.shape[2]
+    heads = columns // head_size
+    step = width // parts
+    holding = moment_ref[0]
+    active = moment_ref[1] == 1
+
+    @pl.when(active)
+    def _():
+        copies = []
+        for part in range(parts):
+            piece = pl.ds(part * step, step)
+            copies.append(
+                pltpu.make_async_copy(
+                    w_query_ref.at[piece, :], query_weight.at[piece, :], sems.at[0, part]
+                )
+            )
+        for part in range(parts):
+            piece = pl.ds(part * step, step)
+            copies.append(
+                pltpu.make_async_copy(
+                    w_out_ref.at[:, piece], out_weight.at[:, piece], sems.at[1, part]
+                )
+            )
+        for copy in copies:
+            copy.start()
+        query_sums = jnp.zeros((rows, columns), jnp.float32)
+        for part in range(parts):
+            copies[part].wait()
+            piece = pl.ds(part * step, step)
+            query_sums += jnp.dot(
+                current_ref[:, piece], query_weight[piece, :], preferred_element_type=jnp.float32
+            )
+        stacked = jnp.concatenate(
+            [query_sums[:, h * head_size : (h + 1) * head_size] for h in range(heads)], axis=0
+        )
+        queries = normalized(stacked, gain_ref[...]).astype(jnp.bfloat16)
+        scores = lax.dot_general(
+            queries,
+            key_ref[holding],
+            (((1,), (1,)), ((), ())),
+            preferred_element_type=jnp.float32,
+        ) / math.sqrt(head_size)
+        exponent = jnp.exp(scores)
+        probs = (exponent / jnp.sum(exponent, axis=-1, keepdims=True)).astype(jnp.bfloat16)
+        attended = jnp.dot(probs, value_ref[holding], preferred_element_type=jnp.float32)
+        attended = attended.astype(jnp.bfloat16)
+        attended = jnp.concatenate(
+            [attended[h * rows : (h + 1) * rows] for h in range(heads)], axis=1
+        )
+        positions = lax.broadcasted_iota(jnp.int32, (rows, 1), 0)
+        scale = jnp.where(positions >= first_seen_ref[holding], factor_ref[0], 0.0)
+        for part in range(parts):
+            copies[parts + part].wait()
+            piece = pl.ds(part * step, step)
+            update = jnp.dot(attended, out_weight[:, piece], preferred_element_type=jnp.float32)
+            state = current_ref[:, piece].astype(jnp.float32) + scale * update
+            out_ref[:, piece] = state.astype(jnp.bfloat16)
+
+    @pl.when(jnp.logical_not(active))
+    def _():
+        out_ref[...] = current_ref[...]
+
+
+def layer(moment, first_seen, factor, current, key_rows, value_rows, gain, w_query, w_out):
+    parts = 4
+    rows, width = current.shape
+    columns = w_query.shape[1]
+    smem = pl.BlockSpec(memory_space=pltpu.SMEM)
+    vmem = pl.BlockSpec(memory_space=pltpu.VMEM)
+    return pl.pallas_call(
+        functools.partial(layer_kernel, parts),
+        out_shape=jax.ShapeDtypeStruct(current.shape, current.dtype),
+        in_specs=[smem] * 3 + [vmem] * 4 + [pl.BlockSpec(memory_space=pl.ANY)] * 2,
+        out_specs=vmem,
+        scratch_shapes=[
+            pltpu.VMEM(w_query.shape, w_query.dtype),
+            pltpu.VMEM(w_out.shape, w_out.dtype),
+            pltpu.SemaphoreType.DMA((2, parts)),
+        ],
+        compiler_params=pltpu.CompilerParams(vmem_limit_bytes=24 * 2**20),
+        cost_estimate=pl.CostEstimate(
+            flops=4 * rows * width * columns,
+            bytes_accessed=4 * width * columns,
+            transcendentals=rows * columns,
+        ),
+    )(moment, first_seen, factor, current, key_rows, value_rows, gain, w_query, w_out)
 
 
 def exchanged(block, axis, distance):
@@ -80,7 +185,6 @@
     sections = lax.axis_size("pipe")
     section_index = lax.axis_index("pipe")
     head_size = w_key.shape[2]
-    head_count = w_query.shape[2] // head_size
     weights = gathered_rows(jnp.concatenate([w_key[0], w_value[0]], axis=1))
     pictures = column_slices(image_states)
     parts, depth = lax.axis_size("x"), weights.shape[0]
@@ -96,35 +200,22 @@
     total = total.reshape(total.shape[0], -1, 2 * head_size)
     key_rows = normalized(total[..., :head_size], key_gain[0]).astype(jnp.bfloat16)
     value_rows = total[..., head_size:].astype(jnp.bfloat16)
-    query_weight = w_query[0]
-    out_weight = w_out[0]
-    factor = jnp.tanh(cross_gate[0])
-    tok_rows = text_states.shape[1]
-    positions = jnp.arange(tok_rows, dtype=jnp.int32)
-    root_size = math.sqrt(head_size)
-
-    def apply_layer(current, holding):
-        own_keys = lax.dynamic_index_in_dim(key_rows, holding, 0, keepdims=False)
-        own_values = lax.dynamic_index_in_dim(value_rows, holding, 0, keepdims=False)
-        query_sums = jnp.dot(current, query_weight, preferred_element_type=jnp.float32)
-        query_sums = query_sums.reshape(tok_rows * head_count, head_size)
-        queries = normalized(query_sums, query_gain[0]).astype(jnp.bfloat16)
-        scores = jnp.dot(queries, own_keys.T, preferred_element_type=jnp.float32) / root_size
-        exponent = jnp.exp(scores)
-        probs = (exponent / jnp.sum(exponent, axis=-1, keepdims=True)).astype(jnp.bfloat16)
-        attended = jnp.dot(probs, own_values, preferred_element_type=jnp.float32).astype(
-            jnp.bfloat16
-        )
-        attended = attended.reshape(tok_rows, head_count * head_size)
-        update = jnp.dot(attended, out_weight, preferred_element_type=jnp.float32)
-        first_seen = lax.dynamic_index_in_dim(image_start[:, 0], holding, 0, keepdims=False)
-        seen = (positions >= first_seen).astype(jnp.float32)[:, None]
-        return (current.astype(jnp.float32) + factor * seen * update).astype(jnp.bfloat16)
-
+    factor = jnp.tanh(cross_gate)
     current = text_states[0]
     for moment in range(sections):
         holding = jnp.mod(section_index - moment, sections)
-        current = lax.cond(moment <= section_index, apply_layer, keep_state, current, holding)
+        active = (moment <= section_index).astype(jnp.int32)
+        current = layer(
+            jnp.stack([holding, active]),
+            image_start[:, 0],
+            factor,
+            current,
+            key_rows,
+            value_rows,
+            query_gain,
+            w_query[0],
+            w_out[0],
+        )
         current = shifted(current, "pipe", 1)
     return current[None]
 

time: 185 us -> 191 us (1.032)
  the two profiles are of different devices: /device:TPU:1 before, /device:TPU:10 now
where the time goes in v2:
time: 191 us; the launch traced here: 190 us
  starting transfers between devices  84.4 us (44%)
  waiting for transfers between devices  66.2 us (35%)
  local copies, waits for them, and re-layouts  22.1 us (12%)
  Pallas kernels  12.8 us (7%)
  other arithmetic  2.57 us (1%)
    ppermute x14, starting transfers between devices, exchanged(): return lax.ppermute(block, axis, [(i, i ^ distance) for i in devices])  76.7 us
    ppermute x4, waiting for transfers between devices, shifted(): return lax.ppermute(block, axis, route)  34 us
    ppermute x14, waiting for transfers between devices, exchanged(): return lax.ppermute(block, axis, [(i, i ^ distance) for i in devices])  32.2 us
    unnamed x33, local copies, waits for them, and re-layouts  18.5 us
    pallas_call x4, Pallas kernels, layer(): pl.pallas_call(functools.partial(layer_kernel, parts), out_shape=jax.Shap...  12.8 us
    ppermute x4, starting transfers between devices, shifted(): return lax.ppermute(block, axis, route)  7.68 us
  transfers between devices with their start and end apart: 18, of which 12 were waited for; matrix products, arithmetic and copies ran while one was open for 1% of the time, Pallas kernels for 0%

profile of v2, /device:TPU:10, one launch (start us, length us, event | category | flops | bytes accessed | tf_op | source)
XLA Modules:
  0.0 190.1 jit_solution(3055008983729356384)
XLA Ops:
  0.0 1.5 reshape.58
  1.5 1.1 constant_dynamic-slice_fusion.3
  2.6 3.4 %collective-permute-start.2 = (bf16[4,16,1024]{2,1,0:T(8,128)(2,1)S(1)}, bf16[4,16,1024]{2,1,0:T(8,128)(2,1)S(1)}, u32[]{:S(2)}, u32[]{:S(2)}) collective-permute-start(bf16[4,16,1024]{2,1,0:T(8,128)(2,1)S(1)} %bitcast.136), channel_id=1, source_target_pairs={{0,768},{256,512},{512,256},{768,0},{1,769},{257,513},{513,257},{7... | collective-permute-start | bytes 393224 | tf_op jit(solution)/shard_map/ppermute | solution.py:134
  6.1 3.0 %collective-permute-start.1 = (bf16[4,16,1024]{2,1,0:T(8,128)(2,1)S(1)}, bf16[4,16,1024]{2,1,0:T(8,128)(2,1)S(1)}, u32[]{:S(2)}, u32[]{:S(2)}) collective-permute-start(bf16[4,16,1024]{2,1,0:T(8,128)(2,1)S(1)} %bitcast.137), channel_id=1, source_target_pairs={{0,512},{256,768},{512,0},{768,256},{1,513},{257,769},{513,1},{769... | collective-permute-start | bytes 393224 | tf_op jit(solution)/shard_map/ppermute | solution.py:134
  9.2 3.4 %collective-permute-start = (bf16[4,16,1024]{2,1,0:T(8,128)(2,1)S(1)}, bf16[4,16,1024]{2,1,0:T(8,128)(2,1)S(1)}, u32[]{:S(2)}, u32[]{:S(2)}) collective-permute-start(bf16[4,16,1024]{2,1,0:T(8,128)(2,1)S(1)} %bitcast.138), channel_id=1, source_target_pairs={{0,256},{256,0},{512,768},{768,512},{1,257},{257,1},{513,769},{769... | collective-permute-start | bytes 393224 | tf_op jit(solution)/shard_map/ppermute | solution.py:134
  12.6 4.2 %collective-permute-start.5 = (bf16[1,16,256]{2,1,0:T(8,128)(2,1)S(1)}, bf16[1,16,256]{2,1,0:T(8,128)(2,1)S(1)}, u32[]{:S(2)}, u32[]{:S(2)}) collective-permute-start(bf16[1,16,256]{2,1,0:T(8,128)(2,1)S(1)} %maximum_bitcast_fusion.1), channel_id=1, source_target_pairs={{0,4},{4,0},{1,5},{5,1},{2,6},{6,2},{3,7},{7,3},{8,12},{12,8},{9,1... | collective-permute-start | bytes 24584 | tf_op jit(solution)/shard_map/ppermute | solution.py:134
  16.8 2.8 %collective-permute-done.5 = bf16[1,16,256]{2,1,0:T(8,128)(2,1)S(1)} collective-permute-done((bf16[1,16,256]{2,1,0:T(8,128)(2,1)S(1)}, bf16[1,16,256]{2,1,0:T(8,128)(2,1)S(1)}, u32[]{:S(2)}, u32[]{:S(2)}) %collective-permute-start.5) | collective-permute-done | bytes 8224 | tf_op jit(solution)/shard_map/ppermute | solution.py:134
  19.7 29.0 %collective-permute-start.6 = (bf16[1,2,16,256]{3,2,1,0:T(8,128)(2,1)S(1)}, bf16[1,2,16,256]{3,2,1,0:T(8,128)(2,1)S(1)}, u32[]{:S(2)}, u32[]{:S(2)}) collective-permute-start(bf16[1,2,16,256]{3,2,1,0:T(8,128)(2,1)S(1)} %pad_maximum_fusion.7), channel_id=1, source_target_pairs={{0,128},{8,136},{16,144},{24,152},{32,160},{40,168},{48,176},{56,1... | collective-permute-start | bytes 49160 | tf_op jit(solution)/shard_map/ppermute | solution.py:134
  48.7 1.7 collective-permute-done.6
  50.4 9.0 %collective-permute-start.7 = (bf16[2,2,16,256]{3,2,1,0:T(8,128)(2,1)S(1)}, bf16[2,2,16,256]{3,2,1,0:T(8,128)(2,1)S(1)}, u32[]{:S(2)}, u32[]{:S(2)}) collective-permute-start(bf16[2,2,16,256]{3,2,1,0:T(8,128)(2,1)S(1)} %maximum_bitcast_fusion), channel_id=1, source_target_pairs={{0,64},{8,72},{16,80},{24,88},{32,96},{40,104},{48,112},{56,120},{... | collective-permute-start | bytes 98312 | tf_op jit(solution)/shard_map/ppermute | solution.py:134
  59.5 5.4 %collective-permute-done.7 = bf16[2,2,16,256]{3,2,1,0:T(8,128)(2,1)S(1)} collective-permute-done((bf16[2,2,16,256]{3,2,1,0:T(8,128)(2,1)S(1)}, bf16[2,2,16,256]{3,2,1,0:T(8,128)(2,1)S(1)}, u32[]{:S(2)}, u32[]{:S(2)}) %collective-permute-start.7) | collective-permute-done | bytes 32800 | tf_op jit(solution)/shard_map/ppermute | solution.py:134
  64.9 0.1 pad_maximum_fusion.2
  65.0 0.6 gather_fusion
  65.6 0.1 broadcast_select_fusion
  65.7 7.0 %collective-permute-start.3 = (bf16[4,4,16,1024]{3,2,1,0:T(8,128)(2,1)S(1)}, bf16[4,4,16,1024]{3,2,1,0:T(8,128)(2,1)S(1)}, u32[]{:S(2)}, u32[]{:S(2)}) collective-permute-start(bf16[4,4,16,1024]{3,2,1,0:T(8,128)(2,1)S(1)} %broadcast_select_fusion), channel_id=1, source_target_pairs={{0,2},{1,3},{2,0},{3,1},{4,6},{5,7},{6,4},{7,5},{8,10},{9,11},{10,... | collective-permute-start | bytes 1572872 | tf_op jit(solution)/shard_map/ppermute | solution.py:134
  72.8 1.9 %collective-permute-start.8 = (bf16[4,2,16,256]{3,2,1,0:T(8,128)(2,1)S(1)}, bf16[4,2,16,256]{3,2,1,0:T(8,128)(2,1)S(1)}, u32[]{:S(2)}, u32[]{:S(2)}) collective-permute-start(bf16[4,2,16,256]{3,2,1,0:T(8,128)(2,1)S(1)} %bitcast.135), channel_id=1, source_target_pairs={{0,32},{8,40},{16,48},{24,56},{32,0},{40,8},{48,16},{56,24},{64,96... | collective-permute-start | bytes 196616 | tf_op jit(solution)/shard_map/ppermute | solution.py:134
  74.7 8.2 %collective-permute-done.8 = bf16[4,2,16,256]{3,2,1,0:T(8,128)(2,1)S(1)} collective-permute-done((bf16[4,2,16,256]{3,2,1,0:T(8,128)(2,1)S(1)}, bf16[4,2,16,256]{3,2,1,0:T(8,128)(2,1)S(1)}, u32[]{:S(2)}, u32[]{:S(2)}) %collective-permute-start.8) | collective-permute-done | bytes 65568 | tf_op jit(solution)/shard_map/ppermute | solution.py:134
  83.0 1.9 %collective-permute-start.9 = (bf16[8,2,16,256]{3,2,1,0:T(8,128)(2,1)S(1)}, bf16[8,2,16,256]{3,2,1,0:T(8,128)(2,1)S(1)}, u32[]{:S(2)}, u32[]{:S(2)}) collective-permute-start(bf16[8,2,16,256]{3,2,1,0:T(8,128)(2,1)S(1)} %bitcast.132), channel_id=1, source_target_pairs={{0,16},{8,24},{16,0},{24,8},{32,48},{40,56},{48,32},{56,40},{64,80... | collective-permute-start | bytes 393224 | tf_op jit(solution)/shard_map/ppermute | solution.py:134
  85.0 0.1 select_bitcast_fusion.3
  85.1 0.1 pad_maximum_fusion.1
  85.2 1.9 %collective-permute-start.4 = (bf16[2,4,4,16,1024]{4,3,2,1,0:T(8,128)(2,1)S(1)}, bf16[2,4,4,16,1024]{4,3,2,1,0:T(8,128)(2,1)S(1)}, u32[]{:S(2)}, u32[]{:S(2)}) collective-permute-start(bf16[2,4,4,16,1024]{4,3,2,1,0:T(8,128)(2,1)S(1)} %pad_maximum_fusion.1), channel_id=1, source_target_pairs={{0,1},{1,0},{2,3},{3,2},{4,5},{5,4},{6,7},{7,6},{8,9},{9,8},{10,11... | collective-permute-start | bytes 3145736 | tf_op jit(solution)/shard_map/ppermute | solution.py:134
  87.2 3.6 %collective-permute-done.9 = bf16[8,2,16,256]{3,2,1,0:T(8,128)(2,1)S(1)} collective-permute-done((bf16[8,2,16,256]{3,2,1,0:T(8,128)(2,1)S(1)}, bf16[8,2,16,256]{3,2,1,0:T(8,128)(2,1)S(1)}, u32[]{:S(2)}, u32[]{:S(2)}) %collective-permute-start.9) | collective-permute-done | bytes 131104 | tf_op jit(solution)/shard_map/ppermute | solution.py:134
  90.9 1.9 %collective-permute-start.10 = (bf16[16,2,16,256]{3,2,1,0:T(8,128)(2,1)S(1)}, bf16[16,2,16,256]{3,2,1,0:T(8,128)(2,1)}, u32[]{:S(2)}, u32[]{:S(2)}) collective-permute-start(bf16[16,2,16,256]{3,2,1,0:T(8,128)(2,1)S(1)} %bitcast.131), channel_id=1, source_target_pairs={{0,8},{8,0},{16,24},{24,16},{32,40},{40,32},{48,56},{56,48},{64,72... | collective-permute-start | bytes 786440 | tf_op jit(solution)/shard_map/ppermute | solution.py:134
  92.8 6.4 %collective-permute-done.10 = bf16[16,2,16,256]{3,2,1,0:T(8,128)(2,1)} collective-permute-done((bf16[16,2,16,256]{3,2,1,0:T(8,128)(2,1)S(1)}, bf16[16,2,16,256]{3,2,1,0:T(8,128)(2,1)}, u32[]{:S(2)}, u32[]{:S(2)}) %collective-permute-start.10) | collective-permute-done | bytes 262176 | tf_op jit(solution)/shard_map/ppermute | solution.py:134
  99.3 1.0 select_bitcast_fusion.5
  100.3 0.1 pad_maximum_fusion.3
  100.4 0.1 select_bitcast_fusion.1
  100.5 0.2 pad_maximum_fusion
  100.7 0.3 copy.25
  101.0 0.7 fusion.4
  101.8 0.0 copy-start.9
  101.9 2.7 %collective-permute-start.13 = (bf16[4,4,16,256]{3,2,1,0:T(8,128)(2,1)S(1)}, bf16[4,4,16,256]{3,2,1,0:T(8,128)(2,1)S(1)}, u32[]{:S(2)}, u32[]{:S(2)}) collective-permute-start(bf16[4,4,16,256]{3,2,1,0:T(8,128)(2,1)S(1)} %get-tuple-element.10), channel_id=1, source_target_pairs={{0,768},{256,512},{512,256},{768,0},{1,769},{257,513},{513,257},{7... | collective-permute-start | bytes 393224 | tf_op jit(solution)/shard_map/ppermute | solution.py:134
  104.6 5.1 %collective-permute-start.12 = (bf16[4,4,16,256]{3,2,1,0:T(8,128)(2,1)S(1)}, bf16[4,4,16,256]{3,2,1,0:T(8,128)(2,1)S(1)}, u32[]{:S(2)}, u32[]{:S(2)}) collective-permute-start(bf16[4,4,16,256]{3,2,1,0:T(8,128)(2,1)S(1)} %get-tuple-element.11), channel_id=1, source_target_pairs={{0,512},{256,768},{512,0},{768,256},{1,513},{257,769},{513,1},{769... | collective-permute-start | bytes 393224 | tf_op jit(solution)/shard_map/ppermute | solution.py:134
  109.7 2.1 %collective-permute-start.11 = (bf16[4,4,16,256]{3,2,1,0:T(8,128)(2,1)S(1)}, bf16[4,4,16,256]{3,2,1,0:T(8,128)(2,1)S(1)}, u32[]{:S(2)}, u32[]{:S(2)}) collective-permute-start(bf16[4,4,16,256]{3,2,1,0:T(8,128)(2,1)S(1)} %get-tuple-element.9), channel_id=1, source_target_pairs={{0,256},{256,0},{512,768},{768,512},{1,257},{257,1},{513,769},{769... | collective-permute-start | bytes 393224 | tf_op jit(solution)/shard_map/ppermute | solution.py:134
  112.5 0.1 pad_add_fusion.3.moment_ref
  112.6 0.4 collective-permute-done.12
  113.0 3.6 %collective-permute-done.11 = bf16[4,4,16,256]{3,2,1,0:T(8,128)(2,1)S(1)} collective-permute-done((bf16[4,4,16,256]{3,2,1,0:T(8,128)(2,1)S(1)}, bf16[4,4,16,256]{3,2,1,0:T(8,128)(2,1)S(1)}, u32[]{:S(2)}, u32[]{:S(2)}) %collective-permute-start.11) | collective-permute-done | bytes 131104 | tf_op jit(solution)/shard_map/ppermute | solution.py:134
  116.5 0.1 fusion.2
  116.6 0.1 multiply_reduce_fusion
  116.8 0.1 multiply_convert_fusion.key_ref
  117.0 2.2 %copy-done = bf16[1,4096,512]{2,1,0:T(8,128)(2,1)S(1)} copy-done((bf16[1,4096,512]{2,1,0:T(8,128)(2,1)S(1)}, bf16[1,4096,512]{2,1,0:T(8,128)(2,1)}, u32[]{:S(2)}) %copy-start) | copy-done | bytes 4194328
  119.1 2.2 %copy-done.4 = bf16[1,512,4096]{2,1,0:T(8,128)(2,1)S(1)} copy-done((bf16[1,512,4096]{2,1,0:T(8,128)(2,1)S(1)}, bf16[1,512,4096]{2,1,0:T(8,128)(2,1)}, u32[]{:S(2)}) %copy-start.4) | copy-done | bytes 4194328
  121.3 4.0 %shard_map.100 = bf16[64,4096]{1,0:T(8,128)(2,1)S(1)} custom-call(s32[2]{0:T(128)S(1)} %pad_add_fusion.3.moment_ref, s32[4]{0:T(128)S(1)} %bitcast.122, f32[1]{0:T(128)S(6)} %tanh.3.factor_ref, bf16[64,4096]{1,0:T(8,128)(2,1)S(1)} %bitcast.121, bf16[4,64,128]{2,1,0:T(8,128)(2,1)S(1)} %multiply_convert_fusion.key_ref, ...), custom_call_target="tpu_custom_call" | custom-call | flops 536870912 | bytes 8388608 | tf_op jit(solution)/shard_map/pallas_call | solution.py:113
  125.4 1.9 %collective-permute-start.14 = (bf16[64,4096]{1,0:T(8,128)(2,1)S(1)}, bf16[64,4096]{1,0:T(8,128)(2,1)S(1)}, u32[]{:S(2)}, u32[]{:S(2)}) collective-permute-start(bf16[64,4096]{1,0:T(8,128)(2,1)S(1)} %shard_map.100), channel_id=1, source_target_pairs={{3,0},{0,1},{1,2},{2,3},{7,4},{4,5},{5,6},{6,7},{11,8},{8,9},{9,10... | collective-permute-start | bytes 1572872 | tf_op jit(solution)/shard_map/ppermute | solution.py:18
  127.3 0.1 pad_add_fusion.2.moment_ref
  127.4 8.5 %collective-permute-done.14.current_ref = bf16[64,4096]{1,0:T(8,128)(2,1)S(1)} collective-permute-done((bf16[64,4096]{1,0:T(8,128)(2,1)S(1)}, bf16[64,4096]{1,0:T(8,128)(2,1)S(1)}, u32[]{:S(2)}, u32[]{:S(2)}) %collective-permute-start.14) | collective-permute-done | bytes 524320 | tf_op jit(solution)/shard_map/ppermute | solution.py:18
  135.9 2.2 %copy-done.1 = bf16[1,4096,512]{2,1,0:T(8,128)(2,1)S(1)} copy-done((bf16[1,4096,512]{2,1,0:T(8,128)(2,1)S(1)}, bf16[1,4096,512]{2,1,0:T(8,128)(2,1)}, u32[]{:S(2)}) %copy-start.1) | copy-done | bytes 4194328
  138.1 2.2 %copy-done.5 = bf16[1,512,4096]{2,1,0:T(8,128)(2,1)S(1)} copy-done((bf16[1,512,4096]{2,1,0:T(8,128)(2,1)S(1)}, bf16[1,512,4096]{2,1,0:T(8,128)(2,1)}, u32[]{:S(2)}) %copy-start.5) | copy-done | bytes 4194328
  140.2 4.0 %shard_map.101 = bf16[64,4096]{1,0:T(8,128)(2,1)S(1)} custom-call(s32[2]{0:T(128)S(1)} %pad_add_fusion.2.moment_ref, s32[4]{0:T(128)S(1)} %bitcast.123, f32[1]{0:T(128)S(6)} %tanh.3.factor_ref, bf16[64,4096]{1,0:T(8,128)(2,1)S(1)} %collective-permute-done.14.current_ref, bf16[4,64,128]{2,1,0:T(8,128)(2,1)S(1)} %multiply_convert_fusion.key_ref, ...), custom_call_target="tpu_custom_call" | custom-call | flops 536870912 | bytes 8388608 | tf_op jit(solution)/shard_map/pallas_call | solution.py:113
  144.3 1.9 %collective-permute-start.15 = (bf16[64,4096]{1,0:T(8,128)(2,1)S(1)}, bf16[64,4096]{1,0:T(8,128)(2,1)S(1)}, u32[]{:S(2)}, u32[]{:S(2)}) collective-permute-start(bf16[64,4096]{1,0:T(8,128)(2,1)S(1)} %shard_map.101), channel_id=1, source_target_pairs={{3,0},{0,1},{1,2},{2,3},{7,4},{4,5},{5,6},{6,7},{11,8},{8,9},{9,10... | collective-permute-start | bytes 1572872 | tf_op jit(solution)/shard_map/ppermute | solution.py:18
  146.2 0.1 pad_add_fusion.1.moment_ref
  146.3 8.5 %collective-permute-done.15.current_ref = bf16[64,4096]{1,0:T(8,128)(2,1)S(1)} collective-permute-done((bf16[64,4096]{1,0:T(8,128)(2,1)S(1)}, bf16[64,4096]{1,0:T(8,128)(2,1)S(1)}, u32[]{:S(2)}, u32[]{:S(2)}) %collective-permute-start.15) | collective-permute-done | bytes 524320 | tf_op jit(solution)/shard_map/ppermute | solution.py:18
  154.8 2.2 %copy-done.2 = bf16[1,4096,512]{2,1,0:T(8,128)(2,1)S(1)} copy-done((bf16[1,4096,512]{2,1,0:T(8,128)(2,1)S(1)}, bf16[1,4096,512]{2,1,0:T(8,128)(2,1)}, u32[]{:S(2)}) %copy-start.2) | copy-done | bytes 4194328
  157.0 2.2 %copy-done.6 = bf16[1,512,4096]{2,1,0:T(8,128)(2,1)S(1)} copy-done((bf16[1,512,4096]{2,1,0:T(8,128)(2,1)S(1)}, bf16[1,512,4096]{2,1,0:T(8,128)(2,1)}, u32[]{:S(2)}) %copy-start.6) | copy-done | bytes 4194328
  159.2 4.0 %shard_map.102 = bf16[64,4096]{1,0:T(8,128)(2,1)S(1)} custom-call(s32[2]{0:T(128)S(1)} %pad_add_fusion.1.moment_ref, s32[4]{0:T(128)S(1)} %bitcast.124, f32[1]{0:T(128)S(6)} %tanh.3.factor_ref, bf16[64,4096]{1,0:T(8,128)(2,1)S(1)} %collective-permute-done.15.current_ref, bf16[4,64,128]{2,1,0:T(8,128)(2,1)S(1)} %multiply_convert_fusion.key_ref, ...), custom_call_target="tpu_custom_call" | custom-call | flops 536870912 | bytes 8388608 | tf_op jit(solution)/shard_map/pallas_call | solution.py:113
  163.2 1.9 %collective-permute-start.16 = (bf16[64,4096]{1,0:T(8,128)(2,1)S(1)}, bf16[64,4096]{1,0:T(8,128)(2,1)S(1)}, u32[]{:S(2)}, u32[]{:S(2)}) collective-permute-start(bf16[64,4096]{1,0:T(8,128)(2,1)S(1)} %shard_map.102), channel_id=1, source_target_pairs={{3,0},{0,1},{1,2},{2,3},{7,4},{4,5},{5,6},{6,7},{11,8},{8,9},{9,10... | collective-permute-start | bytes 1572872 | tf_op jit(solution)/shard_map/ppermute | solution.py:18
  165.2 0.1 pad_add_fusion.moment_ref
  165.3 8.5 %collective-permute-done.16.current_ref = bf16[64,4096]{1,0:T(8,128)(2,1)S(1)} collective-permute-done((bf16[64,4096]{1,0:T(8,128)(2,1)S(1)}, bf16[64,4096]{1,0:T(8,128)(2,1)S(1)}, u32[]{:S(2)}, u32[]{:S(2)}) %collective-permute-start.16) | collective-permute-done | bytes 524320 | tf_op jit(solution)/shard_map/ppermute | solution.py:18
  173.7 2.2 %copy-done.3 = bf16[1,4096,512]{2,1,0:T(8,128)(2,1)S(1)} copy-done((bf16[1,4096,512]{2,1,0:T(8,128)(2,1)S(1)}, bf16[1,4096,512]{2,1,0:T(8,128)(2,1)}, u32[]{:S(2)}) %copy-start.3) | copy-done | bytes 4194328
  175.9 2.2 %copy-done.7 = bf16[1,512,4096]{2,1,0:T(8,128)(2,1)S(1)} copy-done((bf16[1,512,4096]{2,1,0:T(8,128)(2,1)S(1)}, bf16[1,512,4096]{2,1,0:T(8,128)(2,1)}, u32[]{:S(2)}) %copy-start.7) | copy-done | bytes 4194328
  178.1 0.7 shard_map.103
  178.8 1.9 %collective-permute-start.17 = (bf16[64,4096]{1,0:T(8,128)(2,1)S(1)}, bf16[64,4096]{1,0:T(8,128)(2,1)S(1)}, u32[]{:S(2)}, u32[]{:S(2)}) collective-permute-start(bf16[64,4096]{1,0:T(8,128)(2,1)S(1)} %shard_map.103), channel_id=1, source_target_pairs={{3,0},{0,1},{1,2},{2,3},{7,4},{4,5},{5,6},{6,7},{11,8},{8,9},{9,10... | collective-permute-start | bytes 1572872 | tf_op jit(solution)/shard_map/ppermute | solution.py:18
  180.7 8.6 %collective-permute-done.17 = bf16[64,4096]{1,0:T(8,128)(2,1)S(1)} collective-permute-done((bf16[64,4096]{1,0:T(8,128)(2,1)S(1)}, bf16[64,4096]{1,0:T(8,128)(2,1)S(1)}, u32[]{:S(2)}, u32[]{:S(2)}) %collective-permute-start.17) | collective-permute-done | bytes 524320 | tf_op jit(solution)/shard_map/ppermute | solution.py:18
  189.3 0.8 copy.46
  (50 shorter events, 0.5 us)
Async XLA Ops:
  0.0 12.6 %copy-start.11 = (bf16[1,16,128]{2,1,0:T(8,128)(2,1)S(1)}, bf16[1,16,128]{2,1,0:T(8,128)(2,1)}, u32[]{:S(2)}) copy-start(bf16[1,16,128]{2,1,0:T(8,128)(2,1)} %param.15) | copy-start | bytes 12292
  0.0 12.6 %copy-start.12 = (bf16[1,16,128]{2,1,0:T(8,128)(2,1)S(1)}, bf16[1,16,128]{2,1,0:T(8,128)(2,1)}, u32[]{:S(2)}) copy-start(bf16[1,16,128]{2,1,0:T(8,128)(2,1)} %param.14) | copy-start | bytes 12292
  2.6 62.3 %collective-permute-start.2 = (bf16[4,16,1024]{2,1,0:T(8,128)(2,1)S(1)}, bf16[4,16,1024]{2,1,0:T(8,128)(2,1)S(1)}, u32[]{:S(2)}, u32[]{:S(2)}) collective-permute-start(bf16[4,16,1024]{2,1,0:T(8,128)(2,1)S(1)} %bitcast.136), channel_id=1, source_target_pairs={{0,768},{256,512},{512,256},{768,0},{1,769},{257,513},{513,257},{7... | collective-permute-start | bytes 393224 | tf_op jit(solution)/shard_map/ppermute | solution.py:134
  6.1 58.8 %collective-permute-start.1 = (bf16[4,16,1024]{2,1,0:T(8,128)(2,1)S(1)}, bf16[4,16,1024]{2,1,0:T(8,128)(2,1)S(1)}, u32[]{:S(2)}, u32[]{:S(2)}) collective-permute-start(bf16[4,16,1024]{2,1,0:T(8,128)(2,1)S(1)} %bitcast.137), channel_id=1, source_target_pairs={{0,512},{256,768},{512,0},{768,256},{1,513},{257,769},{513,1},{769... | collective-permute-start | bytes 393224 | tf_op jit(solution)/shard_map/ppermute | solution.py:134
  9.2 55.8 %collective-permute-start = (bf16[4,16,1024]{2,1,0:T(8,128)(2,1)S(1)}, bf16[4,16,1024]{2,1,0:T(8,128)(2,1)S(1)}, u32[]{:S(2)}, u32[]{:S(2)}) collective-permute-start(bf16[4,16,1024]{2,1,0:T(8,128)(2,1)S(1)} %bitcast.138), channel_id=1, source_target_pairs={{0,256},{256,0},{512,768},{768,512},{1,257},{257,1},{513,769},{769... | collective-permute-start | bytes 393224 | tf_op jit(solution)/shard_map/ppermute | solution.py:134
  12.6 7.0 %collective-permute-start.5 = (bf16[1,16,256]{2,1,0:T(8,128)(2,1)S(1)}, bf16[1,16,256]{2,1,0:T(8,128)(2,1)S(1)}, u32[]{:S(2)}, u32[]{:S(2)}) collective-permute-start(bf16[1,16,256]{2,1,0:T(8,128)(2,1)S(1)} %maximum_bitcast_fusion.1), channel_id=1, source_target_pairs={{0,4},{4,0},{1,5},{5,1},{2,6},{6,2},{3,7},{7,3},{8,12},{12,8},{9,1... | collective-permute-start | bytes 24584 | tf_op jit(solution)/shard_map/ppermute | solution.py:134
  19.7 30.7 %collective-permute-start.6 = (bf16[1,2,16,256]{3,2,1,0:T(8,128)(2,1)S(1)}, bf16[1,2,16,256]{3,2,1,0:T(8,128)(2,1)S(1)}, u32[]{:S(2)}, u32[]{:S(2)}) collective-permute-start(bf16[1,2,16,256]{3,2,1,0:T(8,128)(2,1)S(1)} %pad_maximum_fusion.7), channel_id=1, source_target_pairs={{0,128},{8,136},{16,144},{24,152},{32,160},{40,168},{48,176},{56,1... | collective-permute-start | bytes 49160 | tf_op jit(solution)/shard_map/ppermute | solution.py:134
  50.4 14.5 %collective-permute-start.7 = (bf16[2,2,16,256]{3,2,1,0:T(8,128)(2,1)S(1)}, bf16[2,2,16,256]{3,2,1,0:T(8,128)(2,1)S(1)}, u32[]{:S(2)}, u32[]{:S(2)}) collective-permute-start(bf16[2,2,16,256]{3,2,1,0:T(8,128)(2,1)S(1)} %maximum_bitcast_fusion), channel_id=1, source_target_pairs={{0,64},{8,72},{16,80},{24,88},{32,96},{40,104},{48,112},{56,120},{... | collective-permute-start | bytes 98312 | tf_op jit(solution)/shard_map/ppermute | solution.py:134
  65.7 19.2 %collective-permute-start.3 = (bf16[4,4,16,1024]{3,2,1,0:T(8,128)(2,1)S(1)}, bf16[4,4,16,1024]{3,2,1,0:T(8,128)(2,1)S(1)}, u32[]{:S(2)}, u32[]{:S(2)}) collective-permute-start(bf16[4,4,16,1024]{3,2,1,0:T(8,128)(2,1)S(1)} %broadcast_select_fusion), channel_id=1, source_target_pairs={{0,2},{1,3},{2,0},{3,1},{4,6},{5,7},{6,4},{7,5},{8,10},{9,11},{10,... | collective-permute-start | bytes 1572872 | tf_op jit(solution)/shard_map/ppermute | solution.py:134
  72.8 10.2 %collective-permute-start.8 = (bf16[4,2,16,256]{3,2,1,0:T(8,128)(2,1)S(1)}, bf16[4,2,16,256]{3,2,1,0:T(8,128)(2,1)S(1)}, u32[]{:S(2)}, u32[]{:S(2)}) collective-permute-start(bf16[4,2,16,256]{3,2,1,0:T(8,128)(2,1)S(1)} %bitcast.135), channel_id=1, source_target_pairs={{0,32},{8,40},{16,48},{24,56},{32,0},{40,8},{48,16},{56,24},{64,96... | collective-permute-start | bytes 196616 | tf_op jit(solution)/shard_map/ppermute | solution.py:134
  83.0 7.8 %collective-permute-start.9 = (bf16[8,2,16,256]{3,2,1,0:T(8,128)(2,1)S(1)}, bf16[8,2,16,256]{3,2,1,0:T(8,128)(2,1)S(1)}, u32[]{:S(2)}, u32[]{:S(2)}) collective-permute-start(bf16[8,2,16,256]{3,2,1,0:T(8,128)(2,1)S(1)} %bitcast.132), channel_id=1, source_target_pairs={{0,16},{8,24},{16,0},{24,8},{32,48},{40,56},{48,32},{56,40},{64,80... | collective-permute-start | bytes 393224 | tf_op jit(solution)/shard_map/ppermute | solution.py:134
  85.2 15.1 %collective-permute-start.4 = (bf16[2,4,4,16,1024]{4,3,2,1,0:T(8,128)(2,1)S(1)}, bf16[2,4,4,16,1024]{4,3,2,1,0:T(8,128)(2,1)S(1)}, u32[]{:S(2)}, u32[]{:S(2)}) collective-permute-start(bf16[2,4,4,16,1024]{4,3,2,1,0:T(8,128)(2,1)S(1)} %pad_maximum_fusion.1), channel_id=1, source_target_pairs={{0,1},{1,0},{2,3},{3,2},{4,5},{5,4},{6,7},{7,6},{8,9},{9,8},{10,11... | collective-permute-start | bytes 3145736 | tf_op jit(solution)/shard_map/ppermute | solution.py:134
  90.9 8.4 %collective-permute-start.10 = (bf16[16,2,16,256]{3,2,1,0:T(8,128)(2,1)S(1)}, bf16[16,2,16,256]{3,2,1,0:T(8,128)(2,1)}, u32[]{:S(2)}, u32[]{:S(2)}) collective-permute-start(bf16[16,2,16,256]{3,2,1,0:T(8,128)(2,1)S(1)} %bitcast.131), channel_id=1, source_target_pairs={{0,8},{8,0},{16,24},{24,16},{32,40},{40,32},{48,56},{56,48},{64,72... | collective-permute-start | bytes 786440 | tf_op jit(solution)/shard_map/ppermute | solution.py:134
  101.8 15.0 %copy-start.13 = (f32[1,128]{1,0:T(1,128)S(1)}, f32[1,128]{1,0:T(1,128)}, u32[]{:S(2)}) copy-start(f32[1,128]{1,0:T(1,128)} %param.18) | copy-start | bytes 1540
  101.8 15.1 %copy-start.8 = (bf16[1,64,4096]{2,1,0:T(8,128)(2,1)S(1)}, bf16[1,64,4096]{2,1,0:T(8,128)(2,1)}, u32[]{:S(2)}) copy-start(bf16[1,64,4096]{2,1,0:T(8,128)(2,1)} %param.10) | copy-start | bytes 1572868
  101.8 15.1 %copy-start.9 = (s32[4,1]{0,1:T(1,128)S(1)}, s32[4,1]{0,1:T(1,128)}, u32[]{:S(2)}) copy-start(s32[4,1]{0,1:T(1,128)} %param.12) | copy-start | bytes 52
  101.8 15.1 %copy-start.10 = (f32[1,128]{1,0:T(1,128)S(1)}, f32[1,128]{1,0:T(1,128)}, u32[]{:S(2)}) copy-start(f32[1,128]{1,0:T(1,128)} %gain_ref.7) | copy-start | bytes 1540
  101.9 10.8 %collective-permute-start.13 = (bf16[4,4,16,256]{3,2,1,0:T(8,128)(2,1)S(1)}, bf16[4,4,16,256]{3,2,1,0:T(8,128)(2,1)S(1)}, u32[]{:S(2)}, u32[]{:S(2)}) collective-permute-start(bf16[4,4,16,256]{3,2,1,0:T(8,128)(2,1)S(1)} %get-tuple-element.10), channel_id=1, source_target_pairs={{0,768},{256,512},{512,256},{768,0},{1,769},{257,513},{513,257},{7... | collective-permute-start | bytes 393224 | tf_op jit(solution)/shard_map/ppermute | solution.py:134
  104.6 8.4 %collective-permute-start.12 = (bf16[4,4,16,256]{3,2,1,0:T(8,128)(2,1)S(1)}, bf16[4,4,16,256]{3,2,1,0:T(8,128)(2,1)S(1)}, u32[]{:S(2)}, u32[]{:S(2)}) collective-permute-start(bf16[4,4,16,256]{3,2,1,0:T(8,128)(2,1)S(1)} %get-tuple-element.11), channel_id=1, source_target_pairs={{0,512},{256,768},{512,0},{768,256},{1,513},{257,769},{513,1},{769... | collective-permute-start | bytes 393224 | tf_op jit(solution)/shard_map/ppermute | solution.py:134
  109.7 6.9 %collective-permute-start.11 = (bf16[4,4,16,256]{3,2,1,0:T(8,128)(2,1)S(1)}, bf16[4,4,16,256]{3,2,1,0:T(8,128)(2,1)S(1)}, u32[]{:S(2)}, u32[]{:S(2)}) collective-permute-start(bf16[4,4,16,256]{3,2,1,0:T(8,128)(2,1)S(1)} %get-tuple-element.9), channel_id=1, source_target_pairs={{0,256},{256,0},{512,768},{768,512},{1,257},{257,1},{513,769},{769... | collective-permute-start | bytes 393224 | tf_op jit(solution)/shard_map/ppermute | solution.py:134
  116.9 2.2 %copy-start = (bf16[1,4096,512]{2,1,0:T(8,128)(2,1)S(1)}, bf16[1,4096,512]{2,1,0:T(8,128)(2,1)}, u32[]{:S(2)}) copy-start(bf16[1,4096,512]{2,1,0:T(8,128)(2,1)} %param.13) | copy-start | bytes 12582916
  119.1 2.2 %copy-start.4 = (bf16[1,512,4096]{2,1,0:T(8,128)(2,1)S(1)}, bf16[1,512,4096]{2,1,0:T(8,128)(2,1)}, u32[]{:S(2)}) copy-start(bf16[1,512,4096]{2,1,0:T(8,128)(2,1)} %param.16) | copy-start | bytes 12582916
  125.4 10.5 %collective-permute-start.14 = (bf16[64,4096]{1,0:T(8,128)(2,1)S(1)}, bf16[64,4096]{1,0:T(8,128)(2,1)S(1)}, u32[]{:S(2)}, u32[]{:S(2)}) collective-permute-start(bf16[64,4096]{1,0:T(8,128)(2,1)S(1)} %shard_map.100), channel_id=1, source_target_pairs={{3,0},{0,1},{1,2},{2,3},{7,4},{4,5},{5,6},{6,7},{11,8},{8,9},{9,10... | collective-permute-start | bytes 1572872 | tf_op jit(solution)/shard_map/ppermute | solution.py:18
  135.9 2.2 %copy-start.1 = (bf16[1,4096,512]{2,1,0:T(8,128)(2,1)S(1)}, bf16[1,4096,512]{2,1,0:T(8,128)(2,1)}, u32[]{:S(2)}) copy-start(bf16[1,4096,512]{2,1,0:T(8,128)(2,1)} %param.13) | copy-start | bytes 12582916
  138.1 2.2 %copy-start.5 = (bf16[1,512,4096]{2,1,0:T(8,128)(2,1)S(1)}, bf16[1,512,4096]{2,1,0:T(8,128)(2,1)}, u32[]{:S(2)}) copy-start(bf16[1,512,4096]{2,1,0:T(8,128)(2,1)} %param.16) | copy-start | bytes 12582916
  144.3 10.5 %collective-permute-start.15 = (bf16[64,4096]{1,0:T(8,128)(2,1)S(1)}, bf16[64,4096]{1,0:T(8,128)(2,1)S(1)}, u32[]{:S(2)}, u32[]{:S(2)}) collective-permute-start(bf16[64,4096]{1,0:T(8,128)(2,1)S(1)} %shard_map.101), channel_id=1, source_target_pairs={{3,0},{0,1},{1,2},{2,3},{7,4},{4,5},{5,6},{6,7},{11,8},{8,9},{9,10... | collective-permute-start | bytes 1572872 | tf_op jit(solution)/shard_map/ppermute | solution.py:18
  154.8 2.2 %copy-start.2 = (bf16[1,4096,512]{2,1,0:T(8,128)(2,1)S(1)}, bf16[1,4096,512]{2,1,0:T(8,128)(2,1)}, u32[]{:S(2)}) copy-start(bf16[1,4096,512]{2,1,0:T(8,128)(2,1)} %param.13) | copy-start | bytes 12582916
  157.0 2.2 %copy-start.6 = (bf16[1,512,4096]{2,1,0:T(8,128)(2,1)S(1)}, bf16[1,512,4096]{2,1,0:T(8,128)(2,1)}, u32[]{:S(2)}) copy-start(bf16[1,512,4096]{2,1,0:T(8,128)(2,1)} %param.16) | copy-start | bytes 12582916
  163.2 10.5 %collective-permute-start.16 = (bf16[64,4096]{1,0:T(8,128)(2,1)S(1)}, bf16[64,4096]{1,0:T(8,128)(2,1)S(1)}, u32[]{:S(2)}, u32[]{:S(2)}) collective-permute-start(bf16[64,4096]{1,0:T(8,128)(2,1)S(1)} %shard_map.102), channel_id=1, source_target_pairs={{3,0},{0,1},{1,2},{2,3},{7,4},{4,5},{5,6},{6,7},{11,8},{8,9},{9,10... | collective-permute-start | bytes 1572872 | tf_op jit(solution)/shard_map/ppermute | solution.py:18
  173.7 2.2 %copy-start.3 = (bf16[1,4096,512]{2,1,0:T(8,128)(2,1)S(1)}, bf16[1,4096,512]{2,1,0:T(8,128)(2,1)}, u32[]{:S(2)}) copy-start(bf16[1,4096,512]{2,1,0:T(8,128)(2,1)} %param.13) | copy-start | bytes 12582916
  175.9 2.2 %copy-start.7 = (bf16[1,512,4096]{2,1,0:T(8,128)(2,1)S(1)}, bf16[1,512,4096]{2,1,0:T(8,128)(2,1)}, u32[]{:S(2)}) copy-start(bf16[1,512,4096]{2,1,0:T(8,128)(2,1)} %param.16) | copy-start | bytes 12582916
  178.8 10.5 %collective-permute-start.17 = (bf16[64,4096]{1,0:T(8,128)(2,1)S(1)}, bf16[64,4096]{1,0:T(8,128)(2,1)S(1)}, u32[]{:S(2)}, u32[]{:S(2)}) collective-permute-start(bf16[64,4096]{1,0:T(8,128)(2,1)S(1)} %shard_map.103), channel_id=1, source_target_pairs={{3,0},{0,1},{1,2},{2,3},{7,4},{4,5},{5,6},{6,7},{11,8},{8,9},{9,10... | collective-permute-start | bytes 1572872 | tf_op jit(solution)/shard_map/ppermute | solution.py:18

commit v3 on v2

v3 whole, which is shorter than its diff:
```python
import functools
import math

import jax
import jax.numpy as jnp
from jax import lax
from jax.experimental import pallas as pl
from jax.experimental.pallas import tpu as pltpu
from jax.sharding import Mesh
from jax.sharding import PartitionSpec as P

epsilon = 1e-06
VMEM_LIMIT = 60 * 2**20


def unit(projected):
    mean_square = jnp.mean(projected * projected, axis=-1, keepdims=True)
    return projected * lax.rsqrt(mean_square + epsilon)


def layer_kernel(
    parts,
    arrivals,
    choosing,
    choice_ref,
    first_seen_ref,
    *refs,
):
    states = refs[:arrivals]
    (
        own_rows_ref,
        near_rows_ref,
        own_query_ref,
        near_query_ref,
        own_out_ref,
        near_out_ref,
        out_ref,
        query_weight,
        out_weight,
        sems,
    ) = refs[arrivals:]
    rows, width = out_ref.shape
    columns = query_weight.shape[1]
    head_size = own_rows_ref.shape[2] // 2
    heads = columns // head_size
    step = width // parts
    active = choice_ref[0] == 1
    near = choice_ref[1] == 1
    batch = choice_ref[2]

    def piece(part):
        return pl.ds(part * step, step)

    def query_copy(ref, part):
        return pltpu.make_async_copy(
            ref.at[piece(part), :], query_weight.at[piece(part), :], sems.at[0, part]
        )

    def out_copy(ref, part):
        return pltpu.make_async_copy(
            ref.at[:, piece(part)], out_weight.at[:, piece(part)], sems.at[1, part]
        )

    def state(part):
        held = states[0][:, piece(part)]
        for index in range(1, choosing):
            held = jnp.where(choice_ref[4] == index, states[index][:, piece(part)], held)
        return held

    @pl.when(jnp.logical_and(active, near))
    def _():
        for part in range(parts):
            query_copy(near_query_ref, part).start()
        for part in range(parts):
            out_copy(near_out_ref, part).start()

    @pl.when(jnp.logical_and(active, jnp.logical_not(near)))
    def _():
        for part in range(parts):
            query_copy(own_query_ref, part).start()
        for part in range(parts):
            out_copy(own_out_ref, part).start()

    @pl.when(active)
    def _():
        query_sums = jnp.zeros((rows, columns), jnp.float32)
        for part in range(parts):
            query_copy(own_query_ref, part).wait()
            query_sums += jnp.dot(
                state(part), query_weight[piece(part), :], preferred_element_type=jnp.float32
            )
        stacked = jnp.concatenate(
            [query_sums[:, h * head_size : (h + 1) * head_size] for h in range(heads)], axis=0
        )
        queries = unit(stacked).astype(jnp.bfloat16)
        image_rows = jnp.where(near, near_rows_ref[choice_ref[3]], own_rows_ref[batch])
        scores = lax.dot_general(
            queries,
            image_rows[:, :head_size],
            (((1,), (1,)), ((), ())),
            preferred_element_type=jnp.float32,
        ) / math.sqrt(head_size)
        exponent = jnp.exp(scores)
        probs = (exponent / jnp.sum(exponent, axis=-1, keepdims=True)).astype(jnp.bfloat16)
        attended = jnp.dot(probs, image_rows[:, head_size:], preferred_element_type=jnp.float32)
        attended = attended.astype(jnp.bfloat16)
        attended = jnp.concatenate(
            [attended[h * rows : (h + 1) * rows] for h in range(heads)], axis=1
        )
        positions = lax.broadcasted_iota(jnp.int32, (rows, 1), 0)
        seen = (positions >= first_seen_ref[batch]).astype(jnp.float32)
        for part in range(parts):
            out_copy(own_out_ref, part).wait()
            update = jnp.dot(attended, out_weight[:, piece(part)], preferred_element_type=jnp.float32)
            result = state(part).astype(jnp.float32) + seen * update
            out_ref[:, piece(part)] = result.astype(jnp.bfloat16)

    for index in range(arrivals):

        @pl.when(jnp.logical_and(jnp.logical_not(active), choice_ref[4] == index))
        def _(index=index):
            out_ref[...] = states[index][...]


def layer(choice, first_seen, states, own_rows, near_rows, weights, choosing=1):
    parts = 4
    rows, width = states[0].shape
    columns = weights[0].shape[1]
    smem = pl.BlockSpec(memory_space=pltpu.SMEM)
    vmem = pl.BlockSpec(memory_space=pltpu.VMEM)
    return pl.pallas_call(
        functools.partial(layer_kernel, parts, len(states), choosing),
        out_shape=jax.ShapeDtypeStruct((rows, width), states[0].dtype),
        in_specs=[smem] * 2
        + [vmem] * (len(states) + 2)
        + [pl.BlockSpec(memory_space=pl.ANY)] * 4,
        out_specs=vmem,
        scratch_shapes=[
            pltpu.VMEM((width, columns), jnp.bfloat16),
            pltpu.VMEM((columns, width), jnp.bfloat16),
            pltpu.SemaphoreType.DMA((2, parts)),
        ],
        compiler_params=pltpu.CompilerParams(vmem_limit_bytes=VMEM_LIMIT),
        cost_estimate=pl.CostEstimate(
            flops=4 * rows * width * columns,
            bytes_accessed=4 * width * columns,
            transcendentals=rows * columns,
        ),
    )(jnp.stack(choice).astype(jnp.int32), first_seen, *states, own_rows, near_rows, *weights)


def exchanged(block, axis, distance):
    devices = range(lax.axis_size(axis))
    return lax.ppermute(block, axis, [(i, i ^ distance) for i in devices])


def doubled(known, axis, distance, where):
    other = exchanged(known, axis, distance)
    upper = (lax.axis_index(axis) & distance) != 0
    first = jnp.where(upper, other, known)
    second = jnp.where(upper, known, other)
    return jnp.stack([first, second], axis=where)


def joined(known, axis, distance):
    known = doubled(known, axis, distance, 1)
    return known if axis == "yh" else known.reshape((-1,) + known.shape[2:])


def column_slices(image_states):
    batches, rows, width = image_states.shape
    parts = lax.axis_size("x")
    own = lax.axis_index("x")
    depth = width // parts

    def columns(plane):
        return lax.dynamic_slice_in_dim(image_states, plane * depth, depth, 2)

    blocks = [columns(own)]
    for distance in range(1, parts):
        blocks.append(exchanged(columns(own ^ distance), "x", distance))
    ordered = jnp.stack(blocks)
    ordered = jnp.take(ordered, own ^ jnp.arange(parts), axis=0)
    halves = doubled(ordered, "pipe", 2, 0)
    return doubled(halves, "pipe", 1, 1).reshape((-1,) + ordered.shape)


def local(
    text_states,
    image_states,
    image_start,
    w_query,
    w_key,
    w_value,
    w_out,
    query_gain,
    key_gain,
    cross_gate,
):
    sections = lax.axis_size("pipe")
    section_index = lax.axis_index("pipe")
    head_size = w_key.shape[2]
    known = jnp.concatenate([w_key[0], w_value[0]], axis=1)[None]
    known = joined(known, "yh", 1)
    distance = lax.axis_size("z") // 2
    known = joined(known, "z", distance)
    known, image_states = lax.optimization_barrier((known, image_states))
    pictures = column_slices(image_states)
    distance //= 2
    known = joined(known, "z", distance)
    known, w_query, w_out = lax.optimization_barrier((known, w_query, w_out))
    layer_weights = (
        w_query[0],
        exchanged(w_query[0], "pipe", 1),
        w_out[0],
        exchanged(w_out[0], "pipe", 1),
    )
    while distance > 1:
        distance //= 2
        known = joined(known, "z", distance)
    weights = known.reshape(-1, known.shape[-1])
    parts, depth = lax.axis_size("x"), weights.shape[0]
    sums = jnp.dot(pictures.reshape(-1, depth), weights, preferred_element_type=jnp.float32)
    sums = sums.reshape(pictures.shape[:-1] + (2 * head_size,))
    own = lax.axis_index("x")
    total = lax.dynamic_index_in_dim(sums, own, 1, keepdims=False)
    rounded = sums.astype(jnp.bfloat16)
    for distance in range(1, parts):
        block = lax.dynamic_index_in_dim(rounded, own ^ distance, 1, keepdims=False)
        total = total + exchanged(block, "x", distance).astype(jnp.float32)
    total = jnp.swapaxes(total, 0, 1)
    total = total.reshape(total.shape[0], -1, 2 * head_size)
    key_scale = key_gain * query_gain
    key_rows = (unit(total[..., :head_size]) * key_scale[0]).astype(jnp.bfloat16)
    value_rows = (total[..., head_size:] * jnp.tanh(cross_gate[0])).astype(jnp.bfloat16)
    own_rows = jnp.concatenate([key_rows, value_rows], axis=-1)
    parity = section_index & 1
    later_half = section_index >= sections // 2
    by_parity = own_rows.reshape((sections // 2, 2) + own_rows.shape[1:])
    near_rows = exchanged(
        lax.dynamic_index_in_dim(by_parity, 1 - parity, 1, keepdims=False), "pipe", 1
    )
    always, never = jnp.int32(1), jnp.int32(0)
    own_batch = section_index
    own_weights = (w_query[0], w_query[0], w_out[0], w_out[0])
    first = layer(
        (always, never, own_batch, never, never),
        image_start[:, 0],
        (text_states[0],),
        own_rows,
        own_rows,
        own_weights,
    )
    run = functools.partial(
        layer,
        first_seen=image_start[:, 0],
        own_rows=own_rows,
        near_rows=near_rows,
        weights=layer_weights,
    )
    from_odd = lax.ppermute(first, "pipe", [(1, 3)])
    second = run((1 - parity, always, own_batch, own_batch >> 1, never), states=(first,))
    from_even = lax.ppermute(second, "pipe", [(0, 2)])
    even = (section_index == 2).astype(jnp.int32)
    odd = (section_index == 3).astype(jnp.int32)
    late = later_half.astype(jnp.int32)
    ahead = run((odd, always, odd, never, never), states=(from_odd,))
    third = run((late, never, odd, never, odd), states=(from_even, ahead), choosing=2)
    home_odd = lax.ppermute(third, "pipe", [(3, 1)])
    kept = jnp.where(section_index == 1, 1, 2 * odd)
    fourth = run((even, always, never, never, kept), states=(third, home_odd, second), choosing=1)
    home_even = lax.ppermute(fourth, "pipe", [(2, 0)])
    kept_state = jnp.where(section_index == 2, second, fourth)
    return jnp.where(section_index == 0, home_even, kept_state)[None]


def solution(mesh):
    sections = mesh.shape["pipe"]
    planes, far = 4, 2
    groups = mesh.shape["dp"] // (planes * far)
    mesh = Mesh(mesh.devices.reshape(planes, groups, far, sections), ("x", "z", "yh", "pipe"))
    replicas = ("x", "z", "yh")
    placed = (
        P("pipe", replicas, None),
        P(None, replicas + ("pipe",), None),
        P(None, replicas),
        P("pipe", None, None),
        P("pipe", replicas, None),
        P("pipe", replicas, None),
        P("pipe", None, None),
        P("pipe", None),
        P("pipe", None),
        P("pipe"),
    )
    return jax.shard_map(
        local, mesh=mesh, in_specs=placed, out_specs=P("pipe", replicas, None), check_vma=False
    )
```

time: 191 us -> 177 us (0.927)
  the two profiles are of different devices: /device:TPU:10 before, /device:TPU:16 now
where the time goes in v3:
time: 177 us; the launch traced here: 176 us
  starting transfers between devices  93.9 us (53%)
  waiting for transfers between devices  47.9 us (27%)
  Pallas kernels  18.8 us (11%)
  other arithmetic  6.86 us (4%)
  local copies, waits for them, and re-layouts  6.39 us (4%)
    ppermute x17, starting transfers between devices, exchanged(): return lax.ppermute(block, axis, [(i, i ^ distance) for i in devices])  88.5 us
    ppermute x17, waiting for transfers between devices, exchanged(): return lax.ppermute(block, axis, [(i, i ^ distance) for i in devices])  26.6 us
    pallas_call x5, Pallas kernels, layer(): pl.pallas_call(functools.partial(layer_kernel, parts, len(states), choosi...  18.8 us
    ppermute x1, waiting for transfers between devices, local(): home_even = lax.ppermute(fourth, 'pipe', [(2, 0)])  17.8 us
  transfers between devices with their start and end apart: 21, of which 10 were waited for; matrix products, arithmetic and copies ran while one was open for 4% of the time, Pallas kernels for 8%

profile of v3, /device:TPU:16, one launch (start us, length us, event | category | flops | bytes accessed | tf_op | source)
XLA Modules:
  0.0 176.0 jit_solution(2197666801738608867)
XLA Ops:
  0.0 0.7 maximum_bitcast_fusion.1
  0.7 14.9 %collective-permute-start = (bf16[1,16,256]{2,1,0:T(8,128)(2,1)S(1)}, bf16[1,16,256]{2,1,0:T(8,128)(2,1)S(1)}, u32[]{:S(2)}, u32[]{:S(2)}) collective-permute-start(bf16[1,16,256]{2,1,0:T(8,128)(2,1)S(1)} %maximum_bitcast_fusion.1), channel_id=1, source_target_pairs={{0,4},{4,0},{1,5},{5,1},{2,6},{6,2},{3,7},{7,3},{8,12},{12,8},{9,1... | collective-permute-start | bytes 24584 | tf_op jit(solution)/shard_map/ppermute | solution.py:154
  15.6 1.6 collective-permute-done
  17.2 0.7 select_bitcast_fusion.16
  17.9 19.5 %collective-permute-start.1 = (bf16[1,2,16,256]{3,2,1,0:T(8,128)(2,1)S(1)}, bf16[1,2,16,256]{3,2,1,0:T(8,128)(2,1)S(1)}, u32[]{:S(2)}, u32[]{:S(2)}) collective-permute-start(bf16[1,2,16,256]{3,2,1,0:T(8,128)(2,1)S(1)} %pad_maximum_fusion.8), channel_id=1, source_target_pairs={{0,128},{8,136},{16,144},{24,152},{32,160},{40,168},{48,176},{56,1... | collective-permute-start | bytes 49160 | tf_op jit(solution)/shard_map/ppermute | solution.py:154
  37.5 4.4 %collective-permute-done.1 = bf16[1,2,16,256]{3,2,1,0:T(8,128)(2,1)S(1)} collective-permute-done((bf16[1,2,16,256]{3,2,1,0:T(8,128)(2,1)S(1)}, bf16[1,2,16,256]{3,2,1,0:T(8,128)(2,1)S(1)}, u32[]{:S(2)}, u32[]{:S(2)}) %collective-permute-start.1) | collective-permute-done | bytes 16416 | tf_op jit(solution)/shard_map/ppermute | solution.py:154
  41.9 6.3 %collective-permute-start.7 = (bf16[2,2,16,256]{3,2,1,0:T(8,128)(2,1)S(1)}, bf16[2,2,16,256]{3,2,1,0:T(8,128)(2,1)S(1)}, u32[]{:S(2)}, u32[]{:S(2)}) collective-permute-start(bf16[2,2,16,256]{3,2,1,0:T(8,128)(2,1)S(1)} %maximum_bitcast_fusion), channel_id=1, source_target_pairs={{0,64},{8,72},{16,80},{24,88},{32,96},{40,104},{48,112},{56,120},{... | collective-permute-start | bytes 98312 | tf_op jit(solution)/shard_map/ppermute | solution.py:154
  48.2 1.1 dynamic-slice_bitcast_fusion.3
  49.3 4.7 %collective-permute-start.4 = (bf16[4,16,1024]{2,1,0:T(8,128)(2,1)S(1)}, bf16[4,16,1024]{2,1,0:T(8,128)(2,1)S(1)}, u32[]{:S(2)}, u32[]{:S(2)}) collective-permute-start(bf16[4,16,1024]{2,1,0:T(8,128)(2,1)S(1)} %get-tuple-element.25), channel_id=1, source_target_pairs={{0,768},{256,512},{512,256},{768,0},{1,769},{257,513},{513,257},{7... | collective-permute-start | bytes 393224 | tf_op jit(solution)/shard_map/ppermute | solution.py:154
  54.0 2.7 %collective-permute-start.3 = (bf16[4,16,1024]{2,1,0:T(8,128)(2,1)S(1)}, bf16[4,16,1024]{2,1,0:T(8,128)(2,1)S(1)}, u32[]{:S(2)}, u32[]{:S(2)}) collective-permute-start(bf16[4,16,1024]{2,1,0:T(8,128)(2,1)S(1)} %get-tuple-element.26), channel_id=1, source_target_pairs={{0,512},{256,768},{512,0},{768,256},{1,513},{257,769},{513,1},{769... | collective-permute-start | bytes 393224 | tf_op jit(solution)/shard_map/ppermute | solution.py:154
  56.7 2.4 %collective-permute-start.2 = (bf16[4,16,1024]{2,1,0:T(8,128)(2,1)S(1)}, bf16[4,16,1024]{2,1,0:T(8,128)(2,1)S(1)}, u32[]{:S(2)}, u32[]{:S(2)}) collective-permute-start(bf16[4,16,1024]{2,1,0:T(8,128)(2,1)S(1)} %get-tuple-element.27), channel_id=1, source_target_pairs={{0,256},{256,0},{512,768},{768,512},{1,257},{257,1},{513,769},{769... | collective-permute-start | bytes 393224 | tf_op jit(solution)/shard_map/ppermute | solution.py:154
  59.2 3.2 %collective-permute-done.3 = bf16[4,16,1024]{2,1,0:T(8,128)(2,1)S(1)} collective-permute-done((bf16[4,16,1024]{2,1,0:T(8,128)(2,1)S(1)}, bf16[4,16,1024]{2,1,0:T(8,128)(2,1)S(1)}, u32[]{:S(2)}, u32[]{:S(2)}) %collective-permute-start.3) | collective-permute-done | bytes 131104 | tf_op jit(solution)/shard_map/ppermute | solution.py:154
  62.4 1.2 collective-permute-done.2
  63.6 0.1 pad_maximum_fusion.2
  63.6 0.6 gather_fusion
  64.2 0.1 broadcast_select_fusion
  64.4 3.2 %collective-permute-start.5 = (bf16[4,4,16,1024]{3,2,1,0:T(8,128)(2,1)S(1)}, bf16[4,4,16,1024]{3,2,1,0:T(8,128)(2,1)S(1)}, u32[]{:S(2)}, u32[]{:S(2)}) collective-permute-start(bf16[4,4,16,1024]{3,2,1,0:T(8,128)(2,1)S(1)} %broadcast_select_fusion), channel_id=1, source_target_pairs={{0,2},{1,3},{2,0},{3,1},{4,6},{5,7},{6,4},{7,5},{8,10},{9,11},{10,... | collective-permute-start | bytes 1572872 | tf_op jit(solution)/shard_map/ppermute | solution.py:154
  67.6 9.1 %collective-permute-start.8 = (bf16[4,2,16,256]{3,2,1,0:T(8,128)(2,1)S(1)}, bf16[4,2,16,256]{3,2,1,0:T(8,128)(2,1)S(1)}, u32[]{:S(2)}, u32[]{:S(2)}) collective-permute-start(bf16[4,2,16,256]{3,2,1,0:T(8,128)(2,1)S(1)} %bitcast.126), channel_id=1, source_target_pairs={{0,32},{8,40},{16,48},{24,56},{32,0},{40,8},{48,16},{56,24},{64,96... | collective-permute-start | bytes 196616 | tf_op jit(solution)/shard_map/ppermute | solution.py:154
  76.7 1.9 %collective-permute-start.16 = (bf16[512,4096]{1,0:T(8,128)(2,1)}, bf16[512,4096]{1,0:T(8,128)(2,1)}, u32[]{:S(2)}, u32[]{:S(2)}) collective-permute-start(bf16[512,4096]{1,0:T(8,128)(2,1)} %bitcast.111), channel_id=1, source_target_pairs={{0,1},{1,0},{2,3},{3,2},{4,5},{5,4},{6,7},{7,6},{8,9},{9,8},{10,11... | collective-permute-start | bytes 12582920 | tf_op jit(solution)/shard_map/ppermute | solution.py:154
  78.6 2.4 %collective-permute-start.15 = (bf16[4096,512]{1,0:T(8,128)(2,1)}, bf16[4096,512]{1,0:T(8,128)(2,1)}, u32[]{:S(2)}, u32[]{:S(2)}) collective-permute-start(bf16[4096,512]{1,0:T(8,128)(2,1)} %bitcast.104), channel_id=1, source_target_pairs={{0,1},{1,0},{2,3},{3,2},{4,5},{5,4},{6,7},{7,6},{8,9},{9,8},{10,11... | collective-permute-start | bytes 12582920 | tf_op jit(solution)/shard_map/ppermute | solution.py:154
  81.1 5.2 %collective-permute-start.9 = (bf16[8,2,16,256]{3,2,1,0:T(8,128)(2,1)S(1)}, bf16[8,2,16,256]{3,2,1,0:T(8,128)(2,1)S(1)}, u32[]{:S(2)}, u32[]{:S(2)}) collective-permute-start(bf16[8,2,16,256]{3,2,1,0:T(8,128)(2,1)S(1)} %bitcast.125), channel_id=1, source_target_pairs={{0,16},{8,24},{16,0},{24,8},{32,48},{40,56},{48,32},{56,40},{64,80... | collective-permute-start | bytes 393224 | tf_op jit(solution)/shard_map/ppermute | solution.py:154
  86.3 0.1 select_bitcast_fusion.4
  86.5 0.1 pad_maximum_fusion.1
  86.6 1.9 %collective-permute-start.6 = (bf16[2,4,4,16,1024]{4,3,2,1,0:T(8,128)(2,1)S(1)}, bf16[2,4,4,16,1024]{4,3,2,1,0:T(8,128)(2,1)S(1)}, u32[]{:S(2)}, u32[]{:S(2)}) collective-permute-start(bf16[2,4,4,16,1024]{4,3,2,1,0:T(8,128)(2,1)S(1)} %pad_maximum_fusion.1), channel_id=1, source_target_pairs={{0,1},{1,0},{2,3},{3,2},{4,5},{5,4},{6,7},{7,6},{8,9},{9,8},{10,11... | collective-permute-start | bytes 3145736 | tf_op jit(solution)/shard_map/ppermute | solution.py:154
  88.5 4.3 %collective-permute-done.9 = bf16[8,2,16,256]{3,2,1,0:T(8,128)(2,1)S(1)} collective-permute-done((bf16[8,2,16,256]{3,2,1,0:T(8,128)(2,1)S(1)}, bf16[8,2,16,256]{3,2,1,0:T(8,128)(2,1)S(1)}, u32[]{:S(2)}, u32[]{:S(2)}) %collective-permute-start.9) | collective-permute-done | bytes 131104 | tf_op jit(solution)/shard_map/ppermute | solution.py:154
  92.9 2.6 %collective-permute-start.10 = (bf16[16,2,16,256]{3,2,1,0:T(8,128)(2,1)S(1)}, bf16[16,2,16,256]{3,2,1,0:T(8,128)(2,1)}, u32[]{:S(2)}, u32[]{:S(2)}) collective-permute-start(bf16[16,2,16,256]{3,2,1,0:T(8,128)(2,1)S(1)} %bitcast.123), channel_id=1, source_target_pairs={{0,8},{8,0},{16,24},{24,16},{32,40},{40,32},{48,56},{56,48},{64,72... | collective-permute-start | bytes 786440 | tf_op jit(solution)/shard_map/ppermute | solution.py:154
  96.2 6.3 %collective-permute-done.10 = bf16[16,2,16,256]{3,2,1,0:T(8,128)(2,1)} collective-permute-done((bf16[16,2,16,256]{3,2,1,0:T(8,128)(2,1)S(1)}, bf16[16,2,16,256]{3,2,1,0:T(8,128)(2,1)}, u32[]{:S(2)}, u32[]{:S(2)}) %collective-permute-start.10) | collective-permute-done | bytes 262176 | tf_op jit(solution)/shard_map/ppermute | solution.py:154
  102.6 1.0 select_bitcast_fusion.6
  103.5 0.1 pad_maximum_fusion.3
  103.7 0.1 select_bitcast_fusion.1
  103.8 0.2 pad_maximum_fusion
  104.0 0.3 copy.28
  104.3 0.0 copy-start.6
  104.3 0.0 copy-start.7
  104.3 0.7 fusion.8
  105.1 2.4 %collective-permute-start.11 = (bf16[4,4,16,256]{3,2,1,0:T(8,128)(2,1)S(1)}, bf16[4,4,16,256]{3,2,1,0:T(8,128)(2,1)S(1)}, u32[]{:S(2)}, u32[]{:S(2)}) collective-permute-start(bf16[4,4,16,256]{3,2,1,0:T(8,128)(2,1)S(1)} %get-tuple-element.19), channel_id=1, source_target_pairs={{0,256},{256,0},{512,768},{768,512},{1,257},{257,1},{513,769},{769... | collective-permute-start | bytes 393224 | tf_op jit(solution)/shard_map/ppermute | solution.py:154
  107.6 4.7 %collective-permute-start.13 = (bf16[4,4,16,256]{3,2,1,0:T(8,128)(2,1)S(1)}, bf16[4,4,16,256]{3,2,1,0:T(8,128)(2,1)S(1)}, u32[]{:S(2)}, u32[]{:S(2)}) collective-permute-start(bf16[4,4,16,256]{3,2,1,0:T(8,128)(2,1)S(1)} %get-tuple-element.20), channel_id=1, source_target_pairs={{0,768},{256,512},{512,256},{768,0},{1,769},{257,513},{513,257},{7... | collective-permute-start | bytes 393224 | tf_op jit(solution)/shard_map/ppermute | solution.py:154
  112.2 2.7 %collective-permute-start.12 = (bf16[4,4,16,256]{3,2,1,0:T(8,128)(2,1)S(1)}, bf16[4,4,16,256]{3,2,1,0:T(8,128)(2,1)S(1)}, u32[]{:S(2)}, u32[]{:S(2)}) collective-permute-start(bf16[4,4,16,256]{3,2,1,0:T(8,128)(2,1)S(1)} %get-tuple-element.21), channel_id=1, source_target_pairs={{0,512},{256,768},{512,0},{768,256},{1,513},{257,769},{513,1},{769... | collective-permute-start | bytes 393224 | tf_op jit(solution)/shard_map/ppermute | solution.py:154
  115.0 0.8 collective-permute-done.13
  115.8 4.8 %collective-permute-done.12 = bf16[4,4,16,256]{3,2,1,0:T(8,128)(2,1)S(1)} collective-permute-done((bf16[4,4,16,256]{3,2,1,0:T(8,128)(2,1)S(1)}, bf16[4,4,16,256]{3,2,1,0:T(8,128)(2,1)S(1)}, u32[]{:S(2)}, u32[]{:S(2)}) %collective-permute-start.12) | collective-permute-done | bytes 131104 | tf_op jit(solution)/shard_map/ppermute | solution.py:154
  120.6 0.1 fusion.2
  120.7 0.1 multiply_reduce_fusion
  120.8 0.1 multiply_convert_fusion
  121.0 1.9 %collective-permute-start.14 = (bf16[2,64,256]{2,1,0:T(8,128)(2,1)S(1)}, bf16[2,64,256]{2,1,0:T(8,128)(2,1)S(1)}, u32[]{:S(2)}, u32[]{:S(2)}) collective-permute-start(bf16[2,64,256]{2,1,0:T(8,128)(2,1)S(1)} %dynamic-slice_bitcast_fusion.4), channel_id=1, source_target_pairs={{0,1},{1,0},{2,3},{3,2},{4,5},{5,4},{6,7},{7,6},{8,9},{9,8},{10,11... | collective-permute-start | bytes 196616 | tf_op jit(solution)/shard_map/ppermute | solution.py:154
  122.9 0.6 pad_add_fusion.2
  123.6 0.6 stack.148.choice_ref
  124.2 6.1 %shard_map.100.refs_0_ = bf16[64,4096]{1,0:T(8,128)(2,1)} custom-call(s32[5]{0:T(128)} %get-tuple-element.41.choice_ref, s32[4]{0:T(128)} %bitcast.135, bf16[64,4096]{1,0:T(8,128)(2,1)} %bitcast.124, bf16[4,64,256]{2,1,0:T(8,128)(2,1)} %copy-done, bf16[4,64,256]{2,1,0:T(8,128)(2,1)} %copy-done, bf16[4096,512]{1,0:T(8,128)(2,1)} %bitcast.105, ...), custom_call_target="tpu_custom_call" | custom-call | flops 536870912 | bytes 8388608 | tf_op jit(solution)/shard_map/pallas_call | solution.py:131
  130.3 0.7 collective-permute-start.18
  131.1 0.6 copy-done.2
  131.7 6.2 %shard_map.101.refs_2_ = bf16[64,4096]{1,0:T(8,128)(2,1)} custom-call(s32[5]{0:T(128)} %stack.148.choice_ref, s32[4]{0:T(128)} %bitcast.136, bf16[64,4096]{1,0:T(8,128)(2,1)} %shard_map.100.refs_0_, bf16[4,64,256]{2,1,0:T(8,128)(2,1)} %copy-done, bf16[2,64,256]{2,1,0:T(8,128)(2,1)} %copy-done.2, bf16[4096,512]{1,0:T(8,128)(2,1)} %bitcast.107, ...), custom_call_target="tpu_custom_call" | custom-call | flops 536870912 | bytes 8388608 | tf_op jit(solution)/shard_map/pallas_call | solution.py:131
  137.8 2.7 %collective-permute-start.17 = (bf16[64,4096]{1,0:T(8,128)(2,1)}, bf16[64,4096]{1,0:T(8,128)(2,1)S(1)}, u32[]{:S(2)}, u32[]{:S(2)}) collective-permute-start(bf16[64,4096]{1,0:T(8,128)(2,1)} %shard_map.101.refs_2_), channel_id=1, source_target_pairs={{0,2},{4,6},{8,10},{12,14},{16,18},{20,22},{24,26},{28,30},{32,34}... | collective-permute-start | bytes 1572872 | tf_op jit(solution)/shard_map/ppermute | solution.py:263
  140.5 0.6 stack.144.choice_ref
  141.2 0.8 copy-done.3
  142.0 2.0 %shard_map.102.refs_1_ = bf16[64,4096]{1,0:T(8,128)(2,1)} custom-call(s32[5]{0:T(128)} %get-tuple-element.40.choice_ref, s32[4]{0:T(128)} %bitcast.137, bf16[64,4096]{1,0:T(8,128)(2,1)} %copy-done.3, bf16[4,64,256]{2,1,0:T(8,128)(2,1)} %copy-done, bf16[2,64,256]{2,1,0:T(8,128)(2,1)} %copy-done.2, bf16[4096,512]{1,0:T(8,128)(2,1)} %bitcast.108, ...), custom_call_target="tpu_custom_call" | custom-call | flops 536870912 | bytes 8388608 | tf_op jit(solution)/shard_map/pallas_call | solution.py:131
  144.0 3.5 %collective-permute-done.17.refs_0_ = bf16[64,4096]{1,0:T(8,128)(2,1)S(1)} collective-permute-done((bf16[64,4096]{1,0:T(8,128)(2,1)}, bf16[64,4096]{1,0:T(8,128)(2,1)S(1)}, u32[]{:S(2)}, u32[]{:S(2)}) %collective-permute-start.17) | collective-permute-done | bytes 524320 | tf_op jit(solution)/shard_map/ppermute | solution.py:263
  147.5 0.8 copy-done.5
  148.3 2.2 %shard_map.103.refs_0_ = bf16[64,4096]{1,0:T(8,128)(2,1)} custom-call(s32[5]{0:T(128)} %stack.144.choice_ref, s32[4]{0:T(128)} %bitcast.138, bf16[64,4096]{1,0:T(8,128)(2,1)} %copy-done.5, bf16[64,4096]{1,0:T(8,128)(2,1)} %shard_map.102.refs_1_, bf16[4,64,256]{2,1,0:T(8,128)(2,1)} %copy-done, bf16[2,64,256]{2,1,0:T(8,128)(2,1)} %copy-done.2, ...), custom_call_target="tpu_custom_call" | custom-call | flops 536870912 | bytes 8388608 | tf_op jit(solution)/shard_map/pallas_call | solution.py:131
  150.5 0.7 collective-permute-start.19
  151.2 0.6 fusion.5.choice_ref
  151.8 0.8 copy-done.4
  152.6 2.3 %shard_map.104 = bf16[64,4096]{1,0:T(8,128)(2,1)} custom-call(s32[5]{0:T(128)} %fusion.5.choice_ref, s32[4]{0:T(128)} %bitcast.139, bf16[64,4096]{1,0:T(8,128)(2,1)} %shard_map.103.refs_0_, bf16[64,4096]{1,0:T(8,128)(2,1)} %copy-done.4, bf16[64,4096]{1,0:T(8,128)(2,1)} %shard_map.101.refs_2_, bf16[4,64,256]{2,1,0:T(8,128)(2,1)} %copy-done, ...), custom_call_target="tpu_custom_call" | custom-call | flops 536870912 | bytes 8388608 | tf_op jit(solution)/shard_map/pallas_call | solution.py:131
  154.9 1.3 collective-permute-start.20
  156.2 17.8 %collective-permute-done.20 = bf16[64,4096]{1,0:T(8,128)(2,1)S(1)} collective-permute-done((bf16[64,4096]{1,0:T(8,128)(2,1)}, bf16[64,4096]{1,0:T(8,128)(2,1)S(1)}, u32[]{:S(2)}, u32[]{:S(2)}) %collective-permute-start.20) | collective-permute-done | bytes 524320 | tf_op jit(solution)/shard_map/ppermute | solution.py:272
  174.1 1.9 %select_bitcast_fusion.2 = bf16[1,64,4096]{2,1,0:T(8,128)(2,1)} fusion(bf16[64,4096]{1,0:T(8,128)(2,1)S(1)} %collective-permute-done.20, bf16[64,4096]{1,0:T(8,128)(2,1)S(1)} %copy-done.1, bf16[64,4096]{1,0:T(8,128)(2,1)} %shard_map.104, pred[]{:T(512)S(6)} %eq.14, pred[]{:T(512)S(6)} %eq.13), kind=kLoop, calls=%fused_computation.7 | loop fusion | flops 524288 | bytes 2097154 | tf_op jit(solution)/shard_map/broadcast_in_dim | solution.py:274
  (43 shorter events, 0.4 us)
Async XLA Ops:
  0.7 16.5 %collective-permute-start = (bf16[1,16,256]{2,1,0:T(8,128)(2,1)S(1)}, bf16[1,16,256]{2,1,0:T(8,128)(2,1)S(1)}, u32[]{:S(2)}, u32[]{:S(2)}) collective-permute-start(bf16[1,16,256]{2,1,0:T(8,128)(2,1)S(1)} %maximum_bitcast_fusion.1), channel_id=1, source_target_pairs={{0,4},{4,0},{1,5},{5,1},{2,6},{6,2},{3,7},{7,3},{8,12},{12,8},{9,1... | collective-permute-start | bytes 24584 | tf_op jit(solution)/shard_map/ppermute | solution.py:154
  17.9 24.0 %collective-permute-start.1 = (bf16[1,2,16,256]{3,2,1,0:T(8,128)(2,1)S(1)}, bf16[1,2,16,256]{3,2,1,0:T(8,128)(2,1)S(1)}, u32[]{:S(2)}, u32[]{:S(2)}) collective-permute-start(bf16[1,2,16,256]{3,2,1,0:T(8,128)(2,1)S(1)} %pad_maximum_fusion.8), channel_id=1, source_target_pairs={{0,128},{8,136},{16,144},{24,152},{32,160},{40,168},{48,176},{56,1... | collective-permute-start | bytes 49160 | tf_op jit(solution)/shard_map/ppermute | solution.py:154
  41.9 17.3 %collective-permute-start.7 = (bf16[2,2,16,256]{3,2,1,0:T(8,128)(2,1)S(1)}, bf16[2,2,16,256]{3,2,1,0:T(8,128)(2,1)S(1)}, u32[]{:S(2)}, u32[]{:S(2)}) collective-permute-start(bf16[2,2,16,256]{3,2,1,0:T(8,128)(2,1)S(1)} %maximum_bitcast_fusion), channel_id=1, source_target_pairs={{0,64},{8,72},{16,80},{24,88},{32,96},{40,104},{48,112},{56,120},{... | collective-permute-start | bytes 98312 | tf_op jit(solution)/shard_map/ppermute | solution.py:154
  49.3 9.9 %collective-permute-start.4 = (bf16[4,16,1024]{2,1,0:T(8,128)(2,1)S(1)}, bf16[4,16,1024]{2,1,0:T(8,128)(2,1)S(1)}, u32[]{:S(2)}, u32[]{:S(2)}) collective-permute-start(bf16[4,16,1024]{2,1,0:T(8,128)(2,1)S(1)} %get-tuple-element.25), channel_id=1, source_target_pairs={{0,768},{256,512},{512,256},{768,0},{1,769},{257,513},{513,257},{7... | collective-permute-start | bytes 393224 | tf_op jit(solution)/shard_map/ppermute | solution.py:154
  54.0 8.4 %collective-permute-start.3 = (bf16[4,16,1024]{2,1,0:T(8,128)(2,1)S(1)}, bf16[4,16,1024]{2,1,0:T(8,128)(2,1)S(1)}, u32[]{:S(2)}, u32[]{:S(2)}) collective-permute-start(bf16[4,16,1024]{2,1,0:T(8,128)(2,1)S(1)} %get-tuple-element.26), channel_id=1, source_target_pairs={{0,512},{256,768},{512,0},{768,256},{1,513},{257,769},{513,1},{769... | collective-permute-start | bytes 393224 | tf_op jit(solution)/shard_map/ppermute | solution.py:154
  56.7 6.9 %collective-permute-start.2 = (bf16[4,16,1024]{2,1,0:T(8,128)(2,1)S(1)}, bf16[4,16,1024]{2,1,0:T(8,128)(2,1)S(1)}, u32[]{:S(2)}, u32[]{:S(2)}) collective-permute-start(bf16[4,16,1024]{2,1,0:T(8,128)(2,1)S(1)} %get-tuple-element.27), channel_id=1, source_target_pairs={{0,256},{256,0},{512,768},{768,512},{1,257},{257,1},{513,769},{769... | collective-permute-start | bytes 393224 | tf_op jit(solution)/shard_map/ppermute | solution.py:154
  64.4 21.9 %collective-permute-start.5 = (bf16[4,4,16,1024]{3,2,1,0:T(8,128)(2,1)S(1)}, bf16[4,4,16,1024]{3,2,1,0:T(8,128)(2,1)S(1)}, u32[]{:S(2)}, u32[]{:S(2)}) collective-permute-start(bf16[4,4,16,1024]{3,2,1,0:T(8,128)(2,1)S(1)} %broadcast_select_fusion), channel_id=1, source_target_pairs={{0,2},{1,3},{2,0},{3,1},{4,6},{5,7},{6,4},{7,5},{8,10},{9,11},{10,... | collective-permute-start | bytes 1572872 | tf_op jit(solution)/shard_map/ppermute | solution.py:154
  67.6 13.5 %collective-permute-start.8 = (bf16[4,2,16,256]{3,2,1,0:T(8,128)(2,1)S(1)}, bf16[4,2,16,256]{3,2,1,0:T(8,128)(2,1)S(1)}, u32[]{:S(2)}, u32[]{:S(2)}) collective-permute-start(bf16[4,2,16,256]{3,2,1,0:T(8,128)(2,1)S(1)} %bitcast.126), channel_id=1, source_target_pairs={{0,32},{8,40},{16,48},{24,56},{32,0},{40,8},{48,16},{56,24},{64,96... | collective-permute-start | bytes 196616 | tf_op jit(solution)/shard_map/ppermute | solution.py:154
  76.7 54.4 %collective-permute-start.16 = (bf16[512,4096]{1,0:T(8,128)(2,1)}, bf16[512,4096]{1,0:T(8,128)(2,1)}, u32[]{:S(2)}, u32[]{:S(2)}) collective-permute-start(bf16[512,4096]{1,0:T(8,128)(2,1)} %bitcast.111), channel_id=1, source_target_pairs={{0,1},{1,0},{2,3},{3,2},{4,5},{5,4},{6,7},{7,6},{8,9},{9,8},{10,11... | collective-permute-start | bytes 12582920 | tf_op jit(solution)/shard_map/ppermute | solution.py:154
  78.6 52.5 %collective-permute-start.15 = (bf16[4096,512]{1,0:T(8,128)(2,1)}, bf16[4096,512]{1,0:T(8,128)(2,1)}, u32[]{:S(2)}, u32[]{:S(2)}) collective-permute-start(bf16[4096,512]{1,0:T(8,128)(2,1)} %bitcast.104), channel_id=1, source_target_pairs={{0,1},{1,0},{2,3},{3,2},{4,5},{5,4},{6,7},{7,6},{8,9},{9,8},{10,11... | collective-permute-start | bytes 12582920 | tf_op jit(solution)/shard_map/ppermute | solution.py:154
  81.1 11.7 %collective-permute-start.9 = (bf16[8,2,16,256]{3,2,1,0:T(8,128)(2,1)S(1)}, bf16[8,2,16,256]{3,2,1,0:T(8,128)(2,1)S(1)}, u32[]{:S(2)}, u32[]{:S(2)}) collective-permute-start(bf16[8,2,16,256]{3,2,1,0:T(8,128)(2,1)S(1)} %bitcast.125), channel_id=1, source_target_pairs={{0,16},{8,24},{16,0},{24,8},{32,48},{40,56},{48,32},{56,40},{64,80... | collective-permute-start | bytes 393224 | tf_op jit(solution)/shard_map/ppermute | solution.py:154
  86.6 17.1 %collective-permute-start.6 = (bf16[2,4,4,16,1024]{4,3,2,1,0:T(8,128)(2,1)S(1)}, bf16[2,4,4,16,1024]{4,3,2,1,0:T(8,128)(2,1)S(1)}, u32[]{:S(2)}, u32[]{:S(2)}) collective-permute-start(bf16[2,4,4,16,1024]{4,3,2,1,0:T(8,128)(2,1)S(1)} %pad_maximum_fusion.1), channel_id=1, source_target_pairs={{0,1},{1,0},{2,3},{3,2},{4,5},{5,4},{6,7},{7,6},{8,9},{9,8},{10,11... | collective-permute-start | bytes 3145736 | tf_op jit(solution)/shard_map/ppermute | solution.py:154
  92.9 9.7 %collective-permute-start.10 = (bf16[16,2,16,256]{3,2,1,0:T(8,128)(2,1)S(1)}, bf16[16,2,16,256]{3,2,1,0:T(8,128)(2,1)}, u32[]{:S(2)}, u32[]{:S(2)}) collective-permute-start(bf16[16,2,16,256]{3,2,1,0:T(8,128)(2,1)S(1)} %bitcast.123), channel_id=1, source_target_pairs={{0,8},{8,0},{16,24},{24,16},{32,40},{40,32},{48,56},{56,48},{64,72... | collective-permute-start | bytes 786440 | tf_op jit(solution)/shard_map/ppermute | solution.py:154
  104.3 10.6 %copy-start.6 = (f32[1,128]{1,0:T(1,128)S(1)}, f32[1,128]{1,0:T(1,128)}, u32[]{:S(2)}) copy-start(f32[1,128]{1,0:T(1,128)} %param.18) | copy-start | bytes 1540
  104.3 10.6 %copy-start.7 = (f32[1,128]{1,0:T(1,128)S(1)}, f32[1,128]{1,0:T(1,128)}, u32[]{:S(2)}) copy-start(f32[1,128]{1,0:T(1,128)} %param.17) | copy-start | bytes 1540
  105.1 9.9 %collective-permute-start.11 = (bf16[4,4,16,256]{3,2,1,0:T(8,128)(2,1)S(1)}, bf16[4,4,16,256]{3,2,1,0:T(8,128)(2,1)S(1)}, u32[]{:S(2)}, u32[]{:S(2)}) collective-permute-start(bf16[4,4,16,256]{3,2,1,0:T(8,128)(2,1)S(1)} %get-tuple-element.19), channel_id=1, source_target_pairs={{0,256},{256,0},{512,768},{768,512},{1,257},{257,1},{513,769},{769... | collective-permute-start | bytes 393224 | tf_op jit(solution)/shard_map/ppermute | solution.py:154
  107.6 8.3 %collective-permute-start.13 = (bf16[4,4,16,256]{3,2,1,0:T(8,128)(2,1)S(1)}, bf16[4,4,16,256]{3,2,1,0:T(8,128)(2,1)S(1)}, u32[]{:S(2)}, u32[]{:S(2)}) collective-permute-start(bf16[4,4,16,256]{3,2,1,0:T(8,128)(2,1)S(1)} %get-tuple-element.20), channel_id=1, source_target_pairs={{0,768},{256,512},{512,256},{768,0},{1,769},{257,513},{513,257},{7... | collective-permute-start | bytes 393224 | tf_op jit(solution)/shard_map/ppermute | solution.py:154
  112.2 8.4 %collective-permute-start.12 = (bf16[4,4,16,256]{3,2,1,0:T(8,128)(2,1)S(1)}, bf16[4,4,16,256]{3,2,1,0:T(8,128)(2,1)S(1)}, u32[]{:S(2)}, u32[]{:S(2)}) collective-permute-start(bf16[4,4,16,256]{3,2,1,0:T(8,128)(2,1)S(1)} %get-tuple-element.21), channel_id=1, source_target_pairs={{0,512},{256,768},{512,0},{768,256},{1,513},{257,769},{513,1},{769... | collective-permute-start | bytes 393224 | tf_op jit(solution)/shard_map/ppermute | solution.py:154
  121.0 3.2 %copy-start = (bf16[4,64,256]{2,1,0:T(8,128)(2,1)}, bf16[4,64,256]{2,1,0:T(8,128)(2,1)S(1)}, u32[]{:S(2)}) copy-start(bf16[4,64,256]{2,1,0:T(8,128)(2,1)S(1)} %pad_maximum_fusion.6.refs_1_.refs_2_.refs_3_) | copy-start | bytes 393220
  121.0 10.0 %collective-permute-start.14 = (bf16[2,64,256]{2,1,0:T(8,128)(2,1)S(1)}, bf16[2,64,256]{2,1,0:T(8,128)(2,1)S(1)}, u32[]{:S(2)}, u32[]{:S(2)}) collective-permute-start(bf16[2,64,256]{2,1,0:T(8,128)(2,1)S(1)} %dynamic-slice_bitcast_fusion.4), channel_id=1, source_target_pairs={{0,1},{1,0},{2,3},{3,2},{4,5},{5,4},{6,7},{7,6},{8,9},{9,8},{10,11... | collective-permute-start | bytes 196616 | tf_op jit(solution)/shard_map/ppermute | solution.py:154
  130.3 10.8 %collective-permute-start.18 = (bf16[64,4096]{1,0:T(8,128)(2,1)}, bf16[64,4096]{1,0:T(8,128)(2,1)S(1)}, u32[]{:S(2)}, u32[]{:S(2)}) collective-permute-start(bf16[64,4096]{1,0:T(8,128)(2,1)} %shard_map.100.refs_0_), channel_id=1, source_target_pairs={{1,3},{5,7},{9,11},{13,15},{17,19},{21,23},{25,27},{29,31},{33,35}... | collective-permute-start | bytes 1572872 | tf_op jit(solution)/shard_map/ppermute | solution.py:261
  131.1 0.6 copy-start.2
  137.8 9.7 %collective-permute-start.17 = (bf16[64,4096]{1,0:T(8,128)(2,1)}, bf16[64,4096]{1,0:T(8,128)(2,1)S(1)}, u32[]{:S(2)}, u32[]{:S(2)}) collective-permute-start(bf16[64,4096]{1,0:T(8,128)(2,1)} %shard_map.101.refs_2_), channel_id=1, source_target_pairs={{0,2},{4,6},{8,10},{12,14},{16,18},{20,22},{24,26},{28,30},{32,34}... | collective-permute-start | bytes 1572872 | tf_op jit(solution)/shard_map/ppermute | solution.py:263
  141.2 0.8 copy-start.3
  147.5 0.8 copy-start.5
  150.5 1.3 collective-permute-start.19
  151.8 22.3 %copy-start.1 = (bf16[64,4096]{1,0:T(8,128)(2,1)S(1)}, bf16[64,4096]{1,0:T(8,128)(2,1)}, u32[]{:S(2)}) copy-start(bf16[64,4096]{1,0:T(8,128)(2,1)} %shard_map.101.refs_2_) | copy-start | bytes 1572868
  151.8 0.8 copy-start.4
  154.9 19.2 %collective-permute-start.20 = (bf16[64,4096]{1,0:T(8,128)(2,1)}, bf16[64,4096]{1,0:T(8,128)(2,1)S(1)}, u32[]{:S(2)}, u32[]{:S(2)}) collective-permute-start(bf16[64,4096]{1,0:T(8,128)(2,1)} %shard_map.104), channel_id=1, source_target_pairs={{2,0},{6,4},{10,8},{14,12},{18,16},{22,20},{26,24},{30,28},{34,32}... | collective-permute-start | bytes 1572872 | tf_op jit(solution)/shard_map/ppermute | solution.py:272

commit v4 on v3

v4 whole, which is shorter than its diff:
```python
import functools
import math

import jax
import jax.numpy as jnp
from jax import lax
from jax.experimental import pallas as pl
from jax.experimental.pallas import tpu as pltpu
from jax.sharding import Mesh
from jax.sharding import PartitionSpec as P

epsilon = 1e-06
VMEM_LIMIT = 48 * 2**20
SECTIONS = 4


def unit(projected):
    mean_square = jnp.mean(projected * projected, axis=-1, keepdims=True)
    return projected * lax.rsqrt(mean_square + epsilon)


def layer_kernel(slot, arrivals, choosing, section_ref, first_seen_ref, *refs):
    states = refs[:arrivals]
    rows_ref, weights_ref, out_ref, weights, sems = refs[arrivals:]
    rows, width = out_ref.shape
    columns = weights.shape[1]
    head_size = rows_ref.shape[2] // 2
    heads = columns // head_size
    pieces = sems.shape[0]
    depth = weights.shape[0] // pieces
    active, batch, chosen = slot(section_ref[0])

    def fetch(piece):
        rows_of = pl.ds(piece * depth, depth)
        return pltpu.make_async_copy(weights_ref.at[rows_of, :], weights.at[rows_of, :], sems.at[piece])

    def state(start, size):
        held = states[0][:, start : start + size]
        for index in range(1, choosing):
            held = jnp.where(chosen == index, states[index][:, start : start + size], held)
        return held

    @pl.when(active)
    def _():
        for piece in range(pieces):
            fetch(piece).start()
        query_sums = jnp.zeros((rows, columns), jnp.float32)
        for piece in range(width // depth):
            fetch(piece).wait()
            start = piece * depth
            query_sums += jnp.dot(
                state(start, depth), weights[start : start + depth], preferred_element_type=jnp.float32
            )
        stacked = jnp.concatenate(
            [query_sums[:, h * head_size : (h + 1) * head_size] for h in range(heads)], axis=0
        )
        queries = unit(stacked).astype(jnp.bfloat16)
        image_rows = rows_ref[batch if rows_ref.shape[0] == SECTIONS else batch >> 1]
        scores = lax.dot_general(
            queries,
            image_rows[:, :head_size],
            (((1,), (1,)), ((), ())),
            preferred_element_type=jnp.float32,
        ) / math.sqrt(head_size)
        exponent = jnp.exp(scores)
        probs = (exponent / jnp.sum(exponent, axis=-1, keepdims=True)).astype(jnp.bfloat16)
        attended = jnp.dot(probs, image_rows[:, head_size:], preferred_element_type=jnp.float32)
        attended = attended.astype(jnp.bfloat16)
        attended = jnp.concatenate(
            [attended[h * rows : (h + 1) * rows] for h in range(heads)], axis=1
        )
        positions = lax.broadcasted_iota(jnp.int32, (rows, 1), 0)
        seen = (positions >= first_seen_ref[batch]).astype(jnp.float32)
        for start in range(0, width, columns):
            if start % depth == 0:
                fetch((width + start) // depth).wait()
            block = weights[width + start : width + start + columns]
            update = jnp.dot(attended, block, preferred_element_type=jnp.float32)
            result = state(start, columns).astype(jnp.float32) + seen * update
            out_ref[:, start : start + columns] = result.astype(jnp.bfloat16)

    for index in range(arrivals):

        @pl.when(jnp.logical_and(jnp.logical_not(active), chosen == index))
        def _(index=index):
            out_ref[...] = states[index][...]


def stack_kernel(w_query_ref, w_out_ref, out_ref, sems):
    width, columns = w_query_ref.shape
    copies = [pltpu.make_async_copy(w_query_ref, out_ref.at[pl.ds(0, width), :], sems.at[0])]
    for block in range(width // columns):
        copies.append(
            pltpu.make_async_copy(
                w_out_ref.at[:, pl.ds(block * columns, columns)],
                out_ref.at[pl.ds(width + block * columns, columns), :],
                sems.at[1 + block],
            )
        )
    for copy in copies:
        copy.start()
    for copy in copies:
        copy.wait()


def stacked_weights(w_query, w_out):
    width, columns = w_query.shape
    return pl.pallas_call(
        stack_kernel,
        out_shape=jax.ShapeDtypeStruct((2 * width, columns), w_query.dtype),
        in_specs=[pl.BlockSpec(memory_space=pl.ANY)] * 2,
        out_specs=pl.BlockSpec(memory_space=pl.ANY),
        scratch_shapes=[pltpu.SemaphoreType.DMA((1 + width // columns,))],
        compiler_params=pltpu.CompilerParams(vmem_limit_bytes=VMEM_LIMIT),
        cost_estimate=pl.CostEstimate(
            flops=0, bytes_accessed=8 * width * columns, transcendentals=0
        ),
    )(w_query, w_out)


def slot_own(section):
    return section >= 0, section, 0


def slot_second(section):
    return (section & 1) == 0, section, 0


def slot_ahead(section):
    return section == 3, jnp.int32(1), 0


def slot_third(section):
    odd = jnp.where(section == 3, 1, 0)
    return section >= 2, odd, odd


def slot_fourth(section):
    kept = jnp.where(section == 1, 1, jnp.where(section == 3, 2, 0))
    return section == 2, jnp.int32(0), kept


def layer(slot, section, first_seen, states, rows_by_batch, weights, choosing=1):
    rows, width = states[0].shape
    columns = weights.shape[1]
    smem = pl.BlockSpec(memory_space=pltpu.SMEM)
    vmem = pl.BlockSpec(memory_space=pltpu.VMEM)
    return pl.pallas_call(
        functools.partial(layer_kernel, slot, len(states), choosing),
        out_shape=jax.ShapeDtypeStruct((rows, width), states[0].dtype),
        in_specs=[smem] * 2
        + [vmem] * (len(states) + 1)
        + [pl.BlockSpec(memory_space=pl.ANY)],
        out_specs=vmem,
        scratch_shapes=[
            pltpu.VMEM(weights.shape, weights.dtype),
            pltpu.SemaphoreType.DMA((2 * max(1, width // (2 * columns)),)),
        ],
        compiler_params=pltpu.CompilerParams(vmem_limit_bytes=VMEM_LIMIT),
        cost_estimate=pl.CostEstimate(
            flops=4 * rows * width * columns,
            bytes_accessed=4 * width * columns,
            transcendentals=rows * columns,
        ),
    )(section, first_seen, *states, rows_by_batch, weights)


def exchanged(block, axis, distance):
    devices = range(lax.axis_size(axis))
    return lax.ppermute(block, axis, [(i, i ^ distance) for i in devices])


def doubled(known, axis, distance, where):
    other = exchanged(known, axis, distance)
    upper = (lax.axis_index(axis) & distance) != 0
    first = jnp.where(upper, other, known)
    second = jnp.where(upper, known, other)
    return jnp.stack([first, second], axis=where)


def joined(known, axis, distance):
    known = doubled(known, axis, distance, 1)
    return known if axis == "yh" else known.reshape((-1,) + known.shape[2:])


def column_slices(image_states):
    batches, rows, width = image_states.shape
    parts = lax.axis_size("x")
    own = lax.axis_index("x")
    depth = width // parts

    def columns(plane):
        return lax.dynamic_slice_in_dim(image_states, plane * depth, depth, 2)

    blocks = [columns(own)]
    for distance in range(1, parts):
        blocks.append(exchanged(columns(own ^ distance), "x", distance))
    ordered = jnp.stack(blocks)
    ordered = jnp.take(ordered, own ^ jnp.arange(parts), axis=0)
    halves = doubled(ordered, "pipe", 2, 0)
    return doubled(halves, "pipe", 1, 1).reshape((-1,) + ordered.shape)


def local(
    text_states,
    image_states,
    image_start,
    w_query,
    w_key,
    w_value,
    w_out,
    query_gain,
    key_gain,
    cross_gate,
):
    sections = lax.axis_size("pipe")
    section_index = lax.axis_index("pipe")
    head_size = w_key.shape[2]
    known = jnp.concatenate([w_key[0], w_value[0]], axis=1)[None]
    known = joined(known, "yh", 1)
    distance = lax.axis_size("z") // 2
    known = joined(known, "z", distance)
    known, image_states = lax.optimization_barrier((known, image_states))
    pictures = column_slices(image_states)
    distance //= 2
    known = joined(known, "z", distance)
    own_weights = stacked_weights(w_query[0], w_out[0])
    known, own_weights = lax.optimization_barrier((known, own_weights))
    near_weights = exchanged(own_weights, "pipe", 1)
    while distance > 1:
        distance //= 2
        known = joined(known, "z", distance)
    weights = known.reshape(-1, known.shape[-1])
    parts, depth = lax.axis_size("x"), weights.shape[0]
    sums = jnp.dot(pictures.reshape(-1, depth), weights, preferred_element_type=jnp.float32)
    sums = sums.reshape(pictures.shape[:-1] + (2 * head_size,))
    own = lax.axis_index("x")
    total = lax.dynamic_index_in_dim(sums, own, 1, keepdims=False)
    rounded = sums.astype(jnp.bfloat16)
    for distance in range(1, parts):
        block = lax.dynamic_index_in_dim(rounded, own ^ distance, 1, keepdims=False)
        total = total + exchanged(block, "x", distance).astype(jnp.float32)
    total = jnp.swapaxes(total, 0, 1)
    total = total.reshape(total.shape[0], -1, 2 * head_size)
    key_scale = key_gain * query_gain
    key_rows = (unit(total[..., :head_size]) * key_scale[0]).astype(jnp.bfloat16)
    value_rows = (total[..., head_size:] * jnp.tanh(cross_gate[0])).astype(jnp.bfloat16)
    own_rows = jnp.concatenate([key_rows, value_rows], axis=-1)
    parity = section_index & 1
    by_parity = own_rows.reshape((sections // 2, 2) + own_rows.shape[1:])
    near_rows = exchanged(
        lax.dynamic_index_in_dim(by_parity, 1 - parity, 1, keepdims=False), "pipe", 1
    )
    section = section_index[None]
    first_seen = image_start[:, 0]
    run = functools.partial(layer, section=section, first_seen=first_seen)
    own = dict(rows_by_batch=own_rows, weights=own_weights)
    near = dict(rows_by_batch=near_rows, weights=near_weights)
    first = run(slot_own, states=(text_states[0],), **own)
    from_odd = lax.ppermute(first, "pipe", [(1, 3)])
    second = run(slot_second, states=(first,), **near)
    from_even = lax.ppermute(second, "pipe", [(0, 2)])
    ahead = run(slot_ahead, states=(from_odd,), **near)
    third = run(slot_third, states=(from_even, ahead), choosing=2, **own)
    home_odd = lax.ppermute(third, "pipe", [(3, 1)])
    fourth = run(slot_fourth, states=(third, home_odd, second), **near)
    home_even = lax.ppermute(fourth, "pipe", [(2, 0)])
    kept_state = jnp.where(section_index == 2, second, fourth)
    return jnp.where(section_index == 0, home_even, kept_state)[None]


def solution(mesh):
    sections = mesh.shape["pipe"]
    planes, far = 4, 2
    groups = mesh.shape["dp"] // (planes * far)
    mesh = Mesh(mesh.devices.reshape(planes, groups, far, sections), ("x", "z", "yh", "pipe"))
    replicas = ("x", "z", "yh")
    placed = (
        P("pipe", replicas, None),
        P(None, replicas + ("pipe",), None),
        P(None, replicas),
        P("pipe", None, None),
        P("pipe", replicas, None),
        P("pipe", replicas, None),
        P("pipe", None, None),
        P("pipe", None),
        P("pipe", None),
        P("pipe"),
    )
    return jax.shard_map(
        local, mesh=mesh, in_specs=placed, out_specs=P("pipe", replicas, None), check_vma=False
    )
```

time: 177 us -> 295 us (1.67)
  the two profiles are of different devices: /device:TPU:16 before, /device:TPU:80 now
where the time goes in v4:
time: 295 us
  Pallas kernels  140 us (47%)
  starting transfers between devices  94.4 us (32%)
  waiting for transfers between devices  50.5 us (17%)
  other arithmetic  4.56 us (2%)
  local copies, waits for them, and re-layouts  3.28 us (1%)
    pallas_call x1, Pallas kernels, stacked_weights(): pl.pallas_call(stack_kernel, out_shape=jax.ShapeDtypeStruct((2 * width, c...  128 us
    ppermute x16, starting transfers between devices, exchanged(): return lax.ppermute(block, axis, [(i, i ^ distance) for i in devices])  89.1 us
    ppermute x16, waiting for transfers between devices, exchanged(): return lax.ppermute(block, axis, [(i, i ^ distance) for i in devices])  26.8 us
    ppermute x1, waiting for transfers between devices, local(): home_even = lax.ppermute(fourth, 'pipe', [(2, 0)])  17.7 us
    pallas_call x5, Pallas kernels, layer(): pl.pallas_call(functools.partial(layer_kernel, slot, len(states), choosin...  11.4 us
    ppermute x1, waiting for transfers between devices, local(): from_even = lax.ppermute(second, 'pipe', [(0, 2)])  5.98 us
  transfers between devices with their start and end apart: 20, of which 10 were waited for; matrix products, arithmetic and copies ran while one was open for 1% of the time, Pallas kernels for 47%

profile of v4, /device:TPU:80, one launch (start us, length us, event | category | flops | bytes accessed | tf_op | source)
XLA Modules:
  0.0 294.5 jit_solution(836977793046230608)
XLA Ops:
  0.0 0.7 maximum_bitcast_fusion.1
  0.7 2.2 collective-permute-start
  3.0 4.8 %collective-permute-done = bf16[1,16,256]{2,1,0:T(8,128)(2,1)S(1)} collective-permute-done((bf16[1,16,256]{2,1,0:T(8,128)(2,1)S(1)}, bf16[1,16,256]{2,1,0:T(8,128)(2,1)S(1)}, u32[]{:S(2)}, u32[]{:S(2)}) %collective-permute-start) | collective-permute-done | bytes 8224 | tf_op jit(solution)/shard_map/ppermute | solution.py:170
  7.7 0.7 select_bitcast_fusion.16
  8.5 27.2 %collective-permute-start.1 = (bf16[1,2,16,256]{3,2,1,0:T(8,128)(2,1)S(1)}, bf16[1,2,16,256]{3,2,1,0:T(8,128)(2,1)S(1)}, u32[]{:S(2)}, u32[]{:S(2)}) collective-permute-start(bf16[1,2,16,256]{3,2,1,0:T(8,128)(2,1)S(1)} %pad_maximum_fusion.8), channel_id=1, source_target_pairs={{0,128},{8,136},{16,144},{24,152},{32,160},{40,168},{48,176},{56,1... | collective-permute-start | bytes 49160 | tf_op jit(solution)/shard_map/ppermute | solution.py:170
  35.6 1.7 collective-permute-done.1
  37.4 10.8 %collective-permute-start.7 = (bf16[2,2,16,256]{3,2,1,0:T(8,128)(2,1)S(1)}, bf16[2,2,16,256]{3,2,1,0:T(8,128)(2,1)S(1)}, u32[]{:S(2)}, u32[]{:S(2)}) collective-permute-start(bf16[2,2,16,256]{3,2,1,0:T(8,128)(2,1)S(1)} %maximum_bitcast_fusion), channel_id=1, source_target_pairs={{0,64},{8,72},{16,80},{24,88},{32,96},{40,104},{48,112},{56,120},{... | collective-permute-start | bytes 98312 | tf_op jit(solution)/shard_map/ppermute | solution.py:170
  48.2 0.0 copy-start
  48.2 2.2 copy-done
  50.4 128.2 %shard_map.100.refs_2_.refs_3_ = bf16[8192,512]{1,0:T(8,128)(2,1)} custom-call(bf16[4096,512]{1,0:T(8,128)(2,1)S(1)} %bitcast.98, bf16[512,4096]{1,0:T(8,128)(2,1)} %bitcast.107), custom_call_target="tpu_custom_call" | custom-call | bytes 16777216 | tf_op jit(solution)/shard_map/pallas_call | solution.py:108
  178.6 0.0 collective-permute-done.7
  178.7 1.9 collective-permute-start.15
  180.7 3.4 %collective-permute-start.2 = (bf16[4,16,1024]{2,1,0:T(8,128)(2,1)S(1)}, bf16[4,16,1024]{2,1,0:T(8,128)(2,1)S(1)}, u32[]{:S(2)}, u32[]{:S(2)}) collective-permute-start(bf16[4,16,1024]{2,1,0:T(8,128)(2,1)S(1)} %get-tuple-element.25), channel_id=1, source_target_pairs={{0,256},{256,0},{512,768},{768,512},{1,257},{257,1},{513,769},{769... | collective-permute-start | bytes 393224 | tf_op jit(solution)/shard_map/ppermute | solution.py:170
  184.1 4.6 %collective-permute-start.3 = (bf16[4,16,1024]{2,1,0:T(8,128)(2,1)S(1)}, bf16[4,16,1024]{2,1,0:T(8,128)(2,1)S(1)}, u32[]{:S(2)}, u32[]{:S(2)}) collective-permute-start(bf16[4,16,1024]{2,1,0:T(8,128)(2,1)S(1)} %get-tuple-element.24), channel_id=1, source_target_pairs={{0,512},{256,768},{512,0},{768,256},{1,513},{257,769},{513,1},{769... | collective-permute-start | bytes 393224 | tf_op jit(solution)/shard_map/ppermute | solution.py:170
  188.7 2.4 collective-permute-start.4
  191.2 2.3 collective-permute-done.3
  193.5 3.7 %collective-permute-done.4 = bf16[4,16,1024]{2,1,0:T(8,128)(2,1)S(1)} collective-permute-done((bf16[4,16,1024]{2,1,0:T(8,128)(2,1)S(1)}, bf16[4,16,1024]{2,1,0:T(8,128)(2,1)S(1)}, u32[]{:S(2)}, u32[]{:S(2)}) %collective-permute-start.4) | collective-permute-done | bytes 131104 | tf_op jit(solution)/shard_map/ppermute | solution.py:170
  197.2 0.1 pad_maximum_fusion.2
  197.3 0.6 gather_fusion
  197.9 0.1 broadcast_select_fusion
  198.0 3.2 %collective-permute-start.5 = (bf16[4,4,16,1024]{3,2,1,0:T(8,128)(2,1)S(1)}, bf16[4,4,16,1024]{3,2,1,0:T(8,128)(2,1)S(1)}, u32[]{:S(2)}, u32[]{:S(2)}) collective-permute-start(bf16[4,4,16,1024]{3,2,1,0:T(8,128)(2,1)S(1)} %broadcast_select_fusion), channel_id=1, source_target_pairs={{0,2},{1,3},{2,0},{3,1},{4,6},{5,7},{6,4},{7,5},{8,10},{9,11},{10,... | collective-permute-start | bytes 1572872 | tf_op jit(solution)/shard_map/ppermute | solution.py:170
  201.2 9.1 %collective-permute-start.8 = (bf16[4,2,16,256]{3,2,1,0:T(8,128)(2,1)S(1)}, bf16[4,2,16,256]{3,2,1,0:T(8,128)(2,1)S(1)}, u32[]{:S(2)}, u32[]{:S(2)}) collective-permute-start(bf16[4,2,16,256]{3,2,1,0:T(8,128)(2,1)S(1)} %bitcast.113), channel_id=1, source_target_pairs={{0,32},{8,40},{16,48},{24,56},{32,0},{40,8},{48,16},{56,24},{64,96... | collective-permute-start | bytes 196616 | tf_op jit(solution)/shard_map/ppermute | solution.py:170
  210.3 2.4 collective-permute-done.8
  212.8 4.3 %collective-permute-start.9 = (bf16[8,2,16,256]{3,2,1,0:T(8,128)(2,1)S(1)}, bf16[8,2,16,256]{3,2,1,0:T(8,128)(2,1)S(1)}, u32[]{:S(2)}, u32[]{:S(2)}) collective-permute-start(bf16[8,2,16,256]{3,2,1,0:T(8,128)(2,1)S(1)} %bitcast.112), channel_id=1, source_target_pairs={{0,16},{8,24},{16,0},{24,8},{32,48},{40,56},{48,32},{56,40},{64,80... | collective-permute-start | bytes 393224 | tf_op jit(solution)/shard_map/ppermute | solution.py:170
  217.1 0.1 select_bitcast_fusion.4
  217.3 0.1 pad_maximum_fusion.1
  217.4 1.9 collective-permute-start.6
  219.3 1.9 collective-permute-done.9
  221.3 5.5 %collective-permute-start.10 = (bf16[16,2,16,256]{3,2,1,0:T(8,128)(2,1)S(1)}, bf16[16,2,16,256]{3,2,1,0:T(8,128)(2,1)}, u32[]{:S(2)}, u32[]{:S(2)}) collective-permute-start(bf16[16,2,16,256]{3,2,1,0:T(8,128)(2,1)S(1)} %bitcast.111), channel_id=1, source_target_pairs={{0,8},{8,0},{16,24},{24,16},{32,40},{40,32},{48,56},{56,48},{64,72... | collective-permute-start | bytes 786440 | tf_op jit(solution)/shard_map/ppermute | solution.py:170
  227.5 5.9 %collective-permute-done.10 = bf16[16,2,16,256]{3,2,1,0:T(8,128)(2,1)} collective-permute-done((bf16[16,2,16,256]{3,2,1,0:T(8,128)(2,1)S(1)}, bf16[16,2,16,256]{3,2,1,0:T(8,128)(2,1)}, u32[]{:S(2)}, u32[]{:S(2)}) %collective-permute-start.10) | collective-permute-done | bytes 262176 | tf_op jit(solution)/shard_map/ppermute | solution.py:170
  233.4 1.0 select_bitcast_fusion.6
  234.4 0.1 pad_maximum_fusion.3
  234.5 0.1 select_bitcast_fusion.1
  234.7 0.2 pad_maximum_fusion
  234.9 0.3 copy.28
  235.2 0.0 copy-start.4
  235.2 0.0 copy-start.5
  235.2 0.7 fusion.5
  235.9 0.0 copy-start.1
  235.9 0.0 copy-start.2
  236.0 2.1 collective-permute-start.11
  238.0 4.5 %collective-permute-start.12 = (bf16[4,4,16,256]{3,2,1,0:T(8,128)(2,1)S(1)}, bf16[4,4,16,256]{3,2,1,0:T(8,128)(2,1)S(1)}, u32[]{:S(2)}, u32[]{:S(2)}) collective-permute-start(bf16[4,4,16,256]{3,2,1,0:T(8,128)(2,1)S(1)} %get-tuple-element.19), channel_id=1, source_target_pairs={{0,512},{256,768},{512,0},{768,256},{1,513},{257,769},{513,1},{769... | collective-permute-start | bytes 393224 | tf_op jit(solution)/shard_map/ppermute | solution.py:170
  242.6 4.0 %collective-permute-start.13 = (bf16[4,4,16,256]{3,2,1,0:T(8,128)(2,1)S(1)}, bf16[4,4,16,256]{3,2,1,0:T(8,128)(2,1)S(1)}, u32[]{:S(2)}, u32[]{:S(2)}) collective-permute-start(bf16[4,4,16,256]{3,2,1,0:T(8,128)(2,1)S(1)} %get-tuple-element.18), channel_id=1, source_target_pairs={{0,768},{256,512},{512,256},{768,0},{1,769},{257,513},{513,257},{7... | collective-permute-start | bytes 393224 | tf_op jit(solution)/shard_map/ppermute | solution.py:170
  246.6 0.0 collective-permute-done.11
  246.6 0.0 collective-permute-done.12
  246.6 4.1 %collective-permute-done.13 = bf16[4,4,16,256]{3,2,1,0:T(8,128)(2,1)S(1)} collective-permute-done((bf16[4,4,16,256]{3,2,1,0:T(8,128)(2,1)S(1)}, bf16[4,4,16,256]{3,2,1,0:T(8,128)(2,1)S(1)}, u32[]{:S(2)}, u32[]{:S(2)}) %collective-permute-start.13) | collective-permute-done | bytes 131104 | tf_op jit(solution)/shard_map/ppermute | solution.py:170
  250.7 0.1 fusion.2
  250.8 0.1 multiply_reduce_fusion
  250.9 0.1 multiply_convert_fusion
  251.1 1.9 collective-permute-start.14
  253.0 4.7 %shard_map.101.refs_0_ = bf16[64,4096]{1,0:T(8,128)(2,1)S(1)} custom-call(s32[1]{0:T(128)} %bitcast.section_ref, s32[4]{0:T(128)S(1)} %bitcast.101, bf16[64,4096]{1,0:T(8,128)(2,1)S(1)} %bitcast.100, bf16[4,64,256]{2,1,0:T(8,128)(2,1)S(1)} %pad_maximum_fusion.6.refs_1_.refs_2_, bf16[8192,512]{1,0:T(8,128)(2,1)} %shard_map.100.refs_2_.refs_3_), custom_call_target="tpu_custom_call" | custom-call | flops 536870912 | bytes 8388608 | tf_op jit(solution)/shard_map/pallas_call | solution.py:148
  257.7 0.7 collective-permute-start.17
  258.4 0.0 collective-permute-done.14.refs_1_.refs_3_
  258.5 4.7 %shard_map.102.refs_2_ = bf16[64,4096]{1,0:T(8,128)(2,1)S(1)} custom-call(s32[1]{0:T(128)} %bitcast.section_ref, s32[4]{0:T(128)S(1)} %bitcast.102, bf16[64,4096]{1,0:T(8,128)(2,1)S(1)} %shard_map.101.refs_0_, bf16[2,64,256]{2,1,0:T(8,128)(2,1)S(1)} %collective-permute-done.14.refs_1_.refs_3_, bf16[8192,512]{1,0:T(8,128)(2,1)} %collective-permute-done.15.refs_2_.refs_4_), custom_call_target="tpu_custom_call" | custom-call | flops 536870912 | bytes 8388608 | tf_op jit(solution)/shard_map/pallas_call | solution.py:148
  263.2 2.7 collective-permute-start.16
  265.9 0.0 collective-permute-done.17.refs_0_
  265.9 0.7 shard_map.103.refs_1_
  266.6 6.0 %collective-permute-done.16.refs_0_ = bf16[64,4096]{1,0:T(8,128)(2,1)S(1)} collective-permute-done((bf16[64,4096]{1,0:T(8,128)(2,1)S(1)}, bf16[64,4096]{1,0:T(8,128)(2,1)S(1)}, u32[]{:S(2)}, u32[]{:S(2)}) %collective-permute-start.16) | collective-permute-done | bytes 524320 | tf_op jit(solution)/shard_map/ppermute | solution.py:262
  272.5 0.7 shard_map.104.refs_0_
  273.2 0.7 collective-permute-start.18
  273.9 0.7 shard_map.105
  274.6 1.3 collective-permute-start.19
  275.9 17.7 %collective-permute-done.19 = bf16[64,4096]{1,0:T(8,128)(2,1)S(1)} collective-permute-done((bf16[64,4096]{1,0:T(8,128)(2,1)S(1)}, bf16[64,4096]{1,0:T(8,128)(2,1)S(1)}, u32[]{:S(2)}, u32[]{:S(2)}) %collective-permute-start.19) | collective-permute-done | bytes 524320 | tf_op jit(solution)/shard_map/ppermute | solution.py:267
  293.6 0.9 select_bitcast_fusion.2
  (33 shorter events, 0.4 us)
Async XLA Ops:
  0.7 7.0 %collective-permute-start = (bf16[1,16,256]{2,1,0:T(8,128)(2,1)S(1)}, bf16[1,16,256]{2,1,0:T(8,128)(2,1)S(1)}, u32[]{:S(2)}, u32[]{:S(2)}) collective-permute-start(bf16[1,16,256]{2,1,0:T(8,128)(2,1)S(1)} %maximum_bitcast_fusion.1), channel_id=1, source_target_pairs={{0,4},{4,0},{1,5},{5,1},{2,6},{6,2},{3,7},{7,3},{8,12},{12,8},{9,1... | collective-permute-start | bytes 24584 | tf_op jit(solution)/shard_map/ppermute | solution.py:170
  8.5 28.9 %collective-permute-start.1 = (bf16[1,2,16,256]{3,2,1,0:T(8,128)(2,1)S(1)}, bf16[1,2,16,256]{3,2,1,0:T(8,128)(2,1)S(1)}, u32[]{:S(2)}, u32[]{:S(2)}) collective-permute-start(bf16[1,2,16,256]{3,2,1,0:T(8,128)(2,1)S(1)} %pad_maximum_fusion.8), channel_id=1, source_target_pairs={{0,128},{8,136},{16,144},{24,152},{32,160},{40,168},{48,176},{56,1... | collective-permute-start | bytes 49160 | tf_op jit(solution)/shard_map/ppermute | solution.py:170
  37.4 141.3 %collective-permute-start.7 = (bf16[2,2,16,256]{3,2,1,0:T(8,128)(2,1)S(1)}, bf16[2,2,16,256]{3,2,1,0:T(8,128)(2,1)S(1)}, u32[]{:S(2)}, u32[]{:S(2)}) collective-permute-start(bf16[2,2,16,256]{3,2,1,0:T(8,128)(2,1)S(1)} %maximum_bitcast_fusion), channel_id=1, source_target_pairs={{0,64},{8,72},{16,80},{24,88},{32,96},{40,104},{48,112},{56,120},{... | collective-permute-start | bytes 98312 | tf_op jit(solution)/shard_map/ppermute | solution.py:170
  48.2 2.2 copy-start
  50.4 130.3 %copy-start.3 = (bf16[4,16,4096]{2,1,0:T(8,128)(2,1)S(1)}, bf16[4,16,4096]{2,1,0:T(8,128)(2,1)}, u32[]{:S(2)}) copy-start(bf16[4,16,4096]{2,1,0:T(8,128)(2,1)} %param.11) | copy-start | bytes 1572868
  178.7 79.8 %collective-permute-start.15 = (bf16[8192,512]{1,0:T(8,128)(2,1)}, bf16[8192,512]{1,0:T(8,128)(2,1)}, u32[]{:S(2)}, u32[]{:S(2)}) collective-permute-start(bf16[8192,512]{1,0:T(8,128)(2,1)} %shard_map.100.refs_2_.refs_3_), channel_id=1, source_target_pairs={{0,1},{1,0},{2,3},{3,2},{4,5},{5,4},{6,7},{7,6},{8,9},{9,8},{10,11... | collective-permute-start | bytes 25165832 | tf_op jit(solution)/shard_map/ppermute | solution.py:170
  180.7 10.5 %collective-permute-start.2 = (bf16[4,16,1024]{2,1,0:T(8,128)(2,1)S(1)}, bf16[4,16,1024]{2,1,0:T(8,128)(2,1)S(1)}, u32[]{:S(2)}, u32[]{:S(2)}) collective-permute-start(bf16[4,16,1024]{2,1,0:T(8,128)(2,1)S(1)} %get-tuple-element.25), channel_id=1, source_target_pairs={{0,256},{256,0},{512,768},{768,512},{1,257},{257,1},{513,769},{769... | collective-permute-start | bytes 393224 | tf_op jit(solution)/shard_map/ppermute | solution.py:170
  184.1 9.4 %collective-permute-start.3 = (bf16[4,16,1024]{2,1,0:T(8,128)(2,1)S(1)}, bf16[4,16,1024]{2,1,0:T(8,128)(2,1)S(1)}, u32[]{:S(2)}, u32[]{:S(2)}) collective-permute-start(bf16[4,16,1024]{2,1,0:T(8,128)(2,1)S(1)} %get-tuple-element.24), channel_id=1, source_target_pairs={{0,512},{256,768},{512,0},{768,256},{1,513},{257,769},{513,1},{769... | collective-permute-start | bytes 393224 | tf_op jit(solution)/shard_map/ppermute | solution.py:170
  188.7 8.4 %collective-permute-start.4 = (bf16[4,16,1024]{2,1,0:T(8,128)(2,1)S(1)}, bf16[4,16,1024]{2,1,0:T(8,128)(2,1)S(1)}, u32[]{:S(2)}, u32[]{:S(2)}) collective-permute-start(bf16[4,16,1024]{2,1,0:T(8,128)(2,1)S(1)} %get-tuple-element.23), channel_id=1, source_target_pairs={{0,768},{256,512},{512,256},{768,0},{1,769},{257,513},{513,257},{7... | collective-permute-start | bytes 393224 | tf_op jit(solution)/shard_map/ppermute | solution.py:170
  198.0 19.1 %collective-permute-start.5 = (bf16[4,4,16,1024]{3,2,1,0:T(8,128)(2,1)S(1)}, bf16[4,4,16,1024]{3,2,1,0:T(8,128)(2,1)S(1)}, u32[]{:S(2)}, u32[]{:S(2)}) collective-permute-start(bf16[4,4,16,1024]{3,2,1,0:T(8,128)(2,1)S(1)} %broadcast_select_fusion), channel_id=1, source_target_pairs={{0,2},{1,3},{2,0},{3,1},{4,6},{5,7},{6,4},{7,5},{8,10},{9,11},{10,... | collective-permute-start | bytes 1572872 | tf_op jit(solution)/shard_map/ppermute | solution.py:170
  201.2 11.6 %collective-permute-start.8 = (bf16[4,2,16,256]{3,2,1,0:T(8,128)(2,1)S(1)}, bf16[4,2,16,256]{3,2,1,0:T(8,128)(2,1)S(1)}, u32[]{:S(2)}, u32[]{:S(2)}) collective-permute-start(bf16[4,2,16,256]{3,2,1,0:T(8,128)(2,1)S(1)} %bitcast.113), channel_id=1, source_target_pairs={{0,32},{8,40},{16,48},{24,56},{32,0},{40,8},{48,16},{56,24},{64,96... | collective-permute-start | bytes 196616 | tf_op jit(solution)/shard_map/ppermute | solution.py:170
  212.8 8.4 %collective-permute-start.9 = (bf16[8,2,16,256]{3,2,1,0:T(8,128)(2,1)S(1)}, bf16[8,2,16,256]{3,2,1,0:T(8,128)(2,1)S(1)}, u32[]{:S(2)}, u32[]{:S(2)}) collective-permute-start(bf16[8,2,16,256]{3,2,1,0:T(8,128)(2,1)S(1)} %bitcast.112), channel_id=1, source_target_pairs={{0,16},{8,24},{16,0},{24,8},{32,48},{40,56},{48,32},{56,40},{64,80... | collective-permute-start | bytes 393224 | tf_op jit(solution)/shard_map/ppermute | solution.py:170
  217.4 17.1 %collective-permute-start.6 = (bf16[2,4,4,16,1024]{4,3,2,1,0:T(8,128)(2,1)S(1)}, bf16[2,4,4,16,1024]{4,3,2,1,0:T(8,128)(2,1)S(1)}, u32[]{:S(2)}, u32[]{:S(2)}) collective-permute-start(bf16[2,4,4,16,1024]{4,3,2,1,0:T(8,128)(2,1)S(1)} %pad_maximum_fusion.1), channel_id=1, source_target_pairs={{0,1},{1,0},{2,3},{3,2},{4,5},{5,4},{6,7},{7,6},{8,9},{9,8},{10,11... | collective-permute-start | bytes 3145736 | tf_op jit(solution)/shard_map/ppermute | solution.py:170
  221.3 12.1 %collective-permute-start.10 = (bf16[16,2,16,256]{3,2,1,0:T(8,128)(2,1)S(1)}, bf16[16,2,16,256]{3,2,1,0:T(8,128)(2,1)}, u32[]{:S(2)}, u32[]{:S(2)}) collective-permute-start(bf16[16,2,16,256]{3,2,1,0:T(8,128)(2,1)S(1)} %bitcast.111), channel_id=1, source_target_pairs={{0,8},{8,0},{16,24},{24,16},{32,40},{40,32},{48,56},{56,48},{64,72... | collective-permute-start | bytes 786440 | tf_op jit(solution)/shard_map/ppermute | solution.py:170
  235.2 11.4 %copy-start.4 = (f32[1,128]{1,0:T(1,128)S(1)}, f32[1,128]{1,0:T(1,128)}, u32[]{:S(2)}) copy-start(f32[1,128]{1,0:T(1,128)} %param.18) | copy-start | bytes 1540
  235.2 11.4 %copy-start.5 = (f32[1,128]{1,0:T(1,128)S(1)}, f32[1,128]{1,0:T(1,128)}, u32[]{:S(2)}) copy-start(f32[1,128]{1,0:T(1,128)} %param.17) | copy-start | bytes 1540
  235.9 17.1 %copy-start.1 = (bf16[1,64,4096]{2,1,0:T(8,128)(2,1)S(1)}, bf16[1,64,4096]{2,1,0:T(8,128)(2,1)}, u32[]{:S(2)}) copy-start(bf16[1,64,4096]{2,1,0:T(8,128)(2,1)} %param.10) | copy-start | bytes 1572868
  235.9 17.1 %copy-start.2 = (s32[4,1]{0,1:T(1,128)S(1)}, s32[4,1]{0,1:T(1,128)}, u32[]{:S(2)}) copy-start(s32[4,1]{0,1:T(1,128)} %param.12) | copy-start | bytes 52
  236.0 10.6 %collective-permute-start.11 = (bf16[4,4,16,256]{3,2,1,0:T(8,128)(2,1)S(1)}, bf16[4,4,16,256]{3,2,1,0:T(8,128)(2,1)S(1)}, u32[]{:S(2)}, u32[]{:S(2)}) collective-permute-start(bf16[4,4,16,256]{3,2,1,0:T(8,128)(2,1)S(1)} %get-tuple-element.17), channel_id=1, source_target_pairs={{0,256},{256,0},{512,768},{768,512},{1,257},{257,1},{513,769},{769... | collective-permute-start | bytes 393224 | tf_op jit(solution)/shard_map/ppermute | solution.py:170
  238.0 8.6 %collective-permute-start.12 = (bf16[4,4,16,256]{3,2,1,0:T(8,128)(2,1)S(1)}, bf16[4,4,16,256]{3,2,1,0:T(8,128)(2,1)S(1)}, u32[]{:S(2)}, u32[]{:S(2)}) collective-permute-start(bf16[4,4,16,256]{3,2,1,0:T(8,128)(2,1)S(1)} %get-tuple-element.19), channel_id=1, source_target_pairs={{0,512},{256,768},{512,0},{768,256},{1,513},{257,769},{513,1},{769... | collective-permute-start | bytes 393224 | tf_op jit(solution)/shard_map/ppermute | solution.py:170
  242.6 8.1 %collective-permute-start.13 = (bf16[4,4,16,256]{3,2,1,0:T(8,128)(2,1)S(1)}, bf16[4,4,16,256]{3,2,1,0:T(8,128)(2,1)S(1)}, u32[]{:S(2)}, u32[]{:S(2)}) collective-permute-start(bf16[4,4,16,256]{3,2,1,0:T(8,128)(2,1)S(1)} %get-tuple-element.18), channel_id=1, source_target_pairs={{0,768},{256,512},{512,256},{768,0},{1,769},{257,513},{513,257},{7... | collective-permute-start | bytes 393224 | tf_op jit(solution)/shard_map/ppermute | solution.py:170
  251.1 7.4 %collective-permute-start.14 = (bf16[2,64,256]{2,1,0:T(8,128)(2,1)S(1)}, bf16[2,64,256]{2,1,0:T(8,128)(2,1)S(1)}, u32[]{:S(2)}, u32[]{:S(2)}) collective-permute-start(bf16[2,64,256]{2,1,0:T(8,128)(2,1)S(1)} %dynamic-slice_bitcast_fusion.4), channel_id=1, source_target_pairs={{0,1},{1,0},{2,3},{3,2},{4,5},{5,4},{6,7},{7,6},{8,9},{9,8},{10,11... | collective-permute-start | bytes 196616 | tf_op jit(solution)/shard_map/ppermute | solution.py:170
  257.7 8.1 %collective-permute-start.17 = (bf16[64,4096]{1,0:T(8,128)(2,1)S(1)}, bf16[64,4096]{1,0:T(8,128)(2,1)S(1)}, u32[]{:S(2)}, u32[]{:S(2)}) collective-permute-start(bf16[64,4096]{1,0:T(8,128)(2,1)S(1)} %shard_map.101.refs_0_), channel_id=1, source_target_pairs={{1,3},{5,7},{9,11},{13,15},{17,19},{21,23},{25,27},{29,31},{33,35}... | collective-permute-start | bytes 1572872 | tf_op jit(solution)/shard_map/ppermute | solution.py:260
  263.2 9.3 %collective-permute-start.16 = (bf16[64,4096]{1,0:T(8,128)(2,1)S(1)}, bf16[64,4096]{1,0:T(8,128)(2,1)S(1)}, u32[]{:S(2)}, u32[]{:S(2)}) collective-permute-start(bf16[64,4096]{1,0:T(8,128)(2,1)S(1)} %shard_map.102.refs_2_), channel_id=1, source_target_pairs={{0,2},{4,6},{8,10},{12,14},{16,18},{20,22},{24,26},{28,30},{32,34}... | collective-permute-start | bytes 1572872 | tf_op jit(solution)/shard_map/ppermute | solution.py:262
  273.2 0.7 collective-permute-start.18
  274.6 19.1 %collective-permute-start.19 = (bf16[64,4096]{1,0:T(8,128)(2,1)S(1)}, bf16[64,4096]{1,0:T(8,128)(2,1)S(1)}, u32[]{:S(2)}, u32[]{:S(2)}) collective-permute-start(bf16[64,4096]{1,0:T(8,128)(2,1)S(1)} %shard_map.105), channel_id=1, source_target_pairs={{2,0},{6,4},{10,8},{14,12},{18,16},{22,20},{26,24},{30,28},{34,32}... | collective-permute-start | bytes 1572872 | tf_op jit(solution)/shard_map/ppermute | solution.py:267

commit v5 on v4

--- a/solution.py
+++ b/solution.py
@@ -86,20 +86,25 @@
             out_ref[...] = states[index][...]
 
 
-def stack_kernel(w_query_ref, w_out_ref, out_ref, sems):
+def stack_kernel(w_query_ref, w_out_ref, out_ref, held, in_sems, out_sems):
     width, columns = w_query_ref.shape
-    copies = [pltpu.make_async_copy(w_query_ref, out_ref.at[pl.ds(0, width), :], sems.at[0])]
-    for block in range(width // columns):
-        copies.append(
-            pltpu.make_async_copy(
-                w_out_ref.at[:, pl.ds(block * columns, columns)],
-                out_ref.at[pl.ds(width + block * columns, columns), :],
-                sems.at[1 + block],
-            )
-        )
-    for copy in copies:
+    pieces = in_sems.shape[0]
+    arriving, leaving = [], []
+    for piece in range(pieces):
+        rows = pl.ds(piece * columns, columns)
+        below = piece * columns - width
+        if below < 0:
+            source = w_query_ref.at[rows, :]
+        else:
+            source = w_out_ref.at[:, pl.ds(below, columns)]
+        arriving.append(pltpu.make_async_copy(source, held.at[rows, :], in_sems.at[piece]))
+        leaving.append(pltpu.make_async_copy(held.at[rows, :], out_ref.at[rows, :], out_sems.at[piece]))
+    for copy in arriving:
         copy.start()
-    for copy in copies:
+    for piece in range(pieces):
+        arriving[piece].wait()
+        leaving[piece].start()
+    for copy in leaving:
         copy.wait()
 
 
@@ -110,7 +115,11 @@
         out_shape=jax.ShapeDtypeStruct((2 * width, columns), w_query.dtype),
         in_specs=[pl.BlockSpec(memory_space=pl.ANY)] * 2,
         out_specs=pl.BlockSpec(memory_space=pl.ANY),
-        scratch_shapes=[pltpu.SemaphoreType.DMA((1 + width // columns,))],
+        scratch_shapes=[
+            pltpu.VMEM((2 * width, columns), w_query.dtype),
+            pltpu.SemaphoreType.DMA((2 * width // columns,)),
+            pltpu.SemaphoreType.DMA((2 * width // columns,)),
+        ],
         compiler_params=pltpu.CompilerParams(vmem_limit_bytes=VMEM_LIMIT),
         cost_estimate=pl.CostEstimate(
             flops=0, bytes_accessed=8 * width * columns, transcendentals=0
@@ -183,8 +192,26 @@
     return known if axis == "yh" else known.reshape((-1,) + known.shape[2:])
 
 
+def in_order(own, blocks):
+    low, high = (own & 1) != 0, (own & 2) != 0
+    near = [jnp.where(low, blocks[1], blocks[0]), jnp.where(low, blocks[0], blocks[1])]
+    far = [jnp.where(low, blocks[3], blocks[2]), jnp.where(low, blocks[2], blocks[3])]
+    first = [jnp.where(high, f, n) for n, f in zip(near, far)]
+    second = [jnp.where(high, n, f) for n, f in zip(near, far)]
+    return jnp.stack(first + second)
+
+
+def joined_four(known, distance):
+    blocks = {0: known}
+    for step in (2, 1, 3):
+        blocks[step] = exchanged(known, "z", step * distance)
+    own = (lax.axis_index("z") // distance) & 3
+    ordered = in_order(own, blocks)
+    return ordered.reshape((-1,) + known.shape[1:])
+
+
 def column_slices(image_states):
-    batches, rows, width = image_states.shape
+    width = image_states.shape[2]
     parts = lax.axis_size("x")
     own = lax.axis_index("x")
     depth = width // parts
@@ -195,10 +222,7 @@
     blocks = [columns(own)]
     for distance in range(1, parts):
         blocks.append(exchanged(columns(own ^ distance), "x", distance))
-    ordered = jnp.stack(blocks)
-    ordered = jnp.take(ordered, own ^ jnp.arange(parts), axis=0)
-    halves = doubled(ordered, "pipe", 2, 0)
-    return doubled(halves, "pipe", 1, 1).reshape((-1,) + ordered.shape)
+    return blocks
 
 
 def local(
@@ -218,14 +242,20 @@
     head_size = w_key.shape[2]
     known = jnp.concatenate([w_key[0], w_value[0]], axis=1)[None]
     known = joined(known, "yh", 1)
-    distance = lax.axis_size("z") // 2
-    known = joined(known, "z", distance)
-    known, image_states = lax.optimization_barrier((known, image_states))
-    pictures = column_slices(image_states)
+    known, image_states, w_query, w_out = lax.optimization_barrier(
+        (known, image_states, w_query, w_out)
+    )
+    distance = lax.axis_size("z") // 4
+    known = joined_four(known, distance)
+    slices = column_slices(image_states)
+    own_weights = stacked_weights(w_query[0], w_out[0])
+    known, slices, own_weights = lax.optimization_barrier((known, slices, own_weights))
+    ordered = in_order(lax.axis_index("x"), slices)
+    halves = doubled(ordered, "pipe", 2, 0)
     distance //= 2
     known = joined(known, "z", distance)
-    own_weights = stacked_weights(w_query[0], w_out[0])
-    known, own_weights = lax.optimization_barrier((known, own_weights))
+    known, halves, own_weights = lax.optimization_barrier((known, halves, own_weights))
+    pictures = doubled(halves, "pipe", 1, 1).reshape((-1,) + ordered.shape)
     near_weights = exchanged(own_weights, "pipe", 1)
     while distance > 1:
         distance //= 2

time: 295 us -> 170 us (0.58)
  the two profiles are of different devices: /device:TPU:80 before, /device:TPU:22 now
where the time goes in v5:
time: 170 us
  starting transfers between devices  83.1 us (49%)
  waiting for transfers between devices  59.9 us (35%)
  Pallas kernels  17.3 us (10%)
  local copies, waits for them, and re-layouts  3.78 us (2%)
  other arithmetic  3.47 us (2%)
    ppermute x17, starting transfers between devices, exchanged(): return lax.ppermute(block, axis, [(i, i ^ distance) for i in devices])  77.8 us
    ppermute x17, waiting for transfers between devices, exchanged(): return lax.ppermute(block, axis, [(i, i ^ distance) for i in devices])  36.1 us
    ppermute x1, waiting for transfers between devices, local(): home_even = lax.ppermute(fourth, 'pipe', [(2, 0)])  17.7 us
    pallas_call x5, Pallas kernels, layer(): pl.pallas_call(functools.partial(layer_kernel, slot, len(states), choosin...  11.4 us
    ppermute x1, waiting for transfers between devices, local(): from_even = lax.ppermute(second, 'pipe', [(0, 2)])  5.98 us
    pallas_call x1, Pallas kernels, stacked_weights(): pl.pallas_call(stack_kernel, out_shape=jax.ShapeDtypeStruct((2 * width, c...  5.86 us
  transfers between devices with their start and end apart: 21, of which 9 were waited for; matrix products, arithmetic and copies ran while one was open for 2% of the time, Pallas kernels for 9%

profile of v5, /device:TPU:22, one launch (start us, length us, event | category | flops | bytes accessed | tf_op | source)
XLA Modules:
  0.0 169.6 jit_solution(3201270628616522270)
XLA Ops:
  0.0 0.7 maximum_bitcast_fusion.1
  0.7 2.2 %collective-permute-start = (bf16[1,16,256]{2,1,0:T(8,128)(2,1)S(1)}, bf16[1,16,256]{2,1,0:T(8,128)(2,1)S(1)}, u32[]{:S(2)}, u32[]{:S(2)}) collective-permute-start(bf16[1,16,256]{2,1,0:T(8,128)(2,1)S(1)} %maximum_bitcast_fusion.1), channel_id=1, source_target_pairs={{0,4},{4,0},{1,5},{5,1},{2,6},{6,2},{3,7},{7,3},{8,12},{12,8},{9,1... | collective-permute-start | bytes 24584 | tf_op jit(solution)/shard_map/ppermute | solution.py:179
  3.0 4.7 %collective-permute-done = bf16[1,16,256]{2,1,0:T(8,128)(2,1)S(1)} collective-permute-done((bf16[1,16,256]{2,1,0:T(8,128)(2,1)S(1)}, bf16[1,16,256]{2,1,0:T(8,128)(2,1)S(1)}, u32[]{:S(2)}, u32[]{:S(2)}) %collective-permute-start) | collective-permute-done | bytes 8224 | tf_op jit(solution)/shard_map/ppermute | solution.py:179
  7.7 0.7 select_bitcast_fusion.20
  8.5 23.0 %collective-permute-start.1 = (bf16[1,2,16,256]{3,2,1,0:T(8,128)(2,1)S(1)}, bf16[1,2,16,256]{3,2,1,0:T(8,128)(2,1)S(1)}, u32[]{:S(2)}, u32[]{:S(2)}) collective-permute-start(bf16[1,2,16,256]{3,2,1,0:T(8,128)(2,1)S(1)} %pad_maximum_fusion.7), channel_id=1, source_target_pairs={{0,192},{8,200},{16,208},{24,216},{32,224},{40,232},{48,240},{56,2... | collective-permute-start | bytes 49160 | tf_op jit(solution)/shard_map/ppermute | solution.py:179
  31.5 7.9 %collective-permute-start.2 = (bf16[1,2,16,256]{3,2,1,0:T(8,128)(2,1)S(1)}, bf16[1,2,16,256]{3,2,1,0:T(8,128)(2,1)S(1)}, u32[]{:S(2)}, u32[]{:S(2)}) collective-permute-start(bf16[1,2,16,256]{3,2,1,0:T(8,128)(2,1)S(1)} %pad_maximum_fusion.7), channel_id=1, source_target_pairs={{0,128},{8,136},{16,144},{24,152},{32,160},{40,168},{48,176},{56,1... | collective-permute-start | bytes 49160 | tf_op jit(solution)/shard_map/ppermute | solution.py:179
  39.4 6.1 %collective-permute-start.3 = (bf16[1,2,16,256]{3,2,1,0:T(8,128)(2,1)S(1)}, bf16[1,2,16,256]{3,2,1,0:T(8,128)(2,1)S(1)}, u32[]{:S(2)}, u32[]{:S(2)}) collective-permute-start(bf16[1,2,16,256]{3,2,1,0:T(8,128)(2,1)S(1)} %pad_maximum_fusion.7), channel_id=1, source_target_pairs={{0,64},{8,72},{16,80},{24,88},{32,96},{40,104},{48,112},{56,120},{... | collective-permute-start | bytes 49160 | tf_op jit(solution)/shard_map/ppermute | solution.py:179
  45.5 1.1 constant_dynamic-slice_fusion
  46.6 2.7 %collective-permute-start.4 = (bf16[4,16,1024]{2,1,0:T(8,128)(2,1)S(1)}, bf16[4,16,1024]{2,1,0:T(8,128)(2,1)S(1)}, u32[]{:S(2)}, u32[]{:S(2)}) collective-permute-start(bf16[4,16,1024]{2,1,0:T(8,128)(2,1)S(1)} %get-tuple-element.46), channel_id=1, source_target_pairs={{0,256},{256,0},{512,768},{768,512},{1,257},{257,1},{513,769},{769... | collective-permute-start | bytes 393224 | tf_op jit(solution)/shard_map/ppermute | solution.py:179
  49.4 3.0 %collective-permute-start.5 = (bf16[4,16,1024]{2,1,0:T(8,128)(2,1)S(1)}, bf16[4,16,1024]{2,1,0:T(8,128)(2,1)S(1)}, u32[]{:S(2)}, u32[]{:S(2)}) collective-permute-start(bf16[4,16,1024]{2,1,0:T(8,128)(2,1)S(1)} %get-tuple-element.45), channel_id=1, source_target_pairs={{0,512},{256,768},{512,0},{768,256},{1,513},{257,769},{513,1},{769... | collective-permute-start | bytes 393224 | tf_op jit(solution)/shard_map/ppermute | solution.py:179
  52.4 0.0 copy-start
  52.4 2.2 %copy-done = bf16[1,4096,512]{2,1,0:T(8,128)(2,1)S(1)} copy-done((bf16[1,4096,512]{2,1,0:T(8,128)(2,1)S(1)}, bf16[1,4096,512]{2,1,0:T(8,128)(2,1)}, u32[]{:S(2)}) %copy-start) | copy-done | bytes 4194328
  54.6 5.9 %shard_map.100.refs_2_.refs_3_ = bf16[8192,512]{1,0:T(8,128)(2,1)} custom-call(bf16[4096,512]{1,0:T(8,128)(2,1)S(1)} %bitcast.102, bf16[512,4096]{1,0:T(8,128)(2,1)} %bitcast.111), custom_call_target="tpu_custom_call" | custom-call | bytes 16777216 | tf_op jit(solution)/shard_map/pallas_call | solution.py:113
  60.5 4.7 %collective-permute-start.6 = (bf16[4,16,1024]{2,1,0:T(8,128)(2,1)S(1)}, bf16[4,16,1024]{2,1,0:T(8,128)(2,1)S(1)}, u32[]{:S(2)}, u32[]{:S(2)}) collective-permute-start(bf16[4,16,1024]{2,1,0:T(8,128)(2,1)S(1)} %get-tuple-element.44), channel_id=1, source_target_pairs={{0,768},{256,512},{512,256},{768,0},{1,769},{257,513},{513,257},{7... | collective-permute-start | bytes 393224 | tf_op jit(solution)/shard_map/ppermute | solution.py:179
  65.1 0.0 collective-permute-done.2
  65.2 0.0 collective-permute-done.4
  65.2 0.0 collective-permute-done.5
  65.2 3.3 %collective-permute-done.6 = bf16[4,16,1024]{2,1,0:T(8,128)(2,1)S(1)} collective-permute-done((bf16[4,16,1024]{2,1,0:T(8,128)(2,1)S(1)}, bf16[4,16,1024]{2,1,0:T(8,128)(2,1)S(1)}, u32[]{:S(2)}, u32[]{:S(2)}) %collective-permute-start.6) | collective-permute-done | bytes 131104 | tf_op jit(solution)/shard_map/ppermute | solution.py:179
  68.6 0.1 pad_maximum_fusion.2
  68.7 3.2 %collective-permute-start.8 = (bf16[4,4,16,1024]{3,2,1,0:T(8,128)(2,1)S(1)}, bf16[4,4,16,1024]{3,2,1,0:T(8,128)(2,1)S(1)}, u32[]{:S(2)}, u32[]{:S(2)}) collective-permute-start(bf16[4,4,16,1024]{3,2,1,0:T(8,128)(2,1)S(1)} %pad_maximum_fusion.2), channel_id=1, source_target_pairs={{0,2},{1,3},{2,0},{3,1},{4,6},{5,7},{6,4},{7,5},{8,10},{9,11},{10,... | collective-permute-start | bytes 1572872 | tf_op jit(solution)/shard_map/ppermute | solution.py:179
  71.9 4.3 %collective-permute-start.7 = (bf16[4,2,16,256]{3,2,1,0:T(8,128)(2,1)S(1)}, bf16[4,2,16,256]{3,2,1,0:T(8,128)(2,1)S(1)}, u32[]{:S(2)}, u32[]{:S(2)}) collective-permute-start(bf16[4,2,16,256]{3,2,1,0:T(8,128)(2,1)S(1)} %maximum_bitcast_fusion), channel_id=1, source_target_pairs={{0,32},{8,40},{16,48},{24,56},{32,0},{40,8},{48,16},{56,24},{64,96... | collective-permute-start | bytes 196616 | tf_op jit(solution)/shard_map/ppermute | solution.py:179
  76.2 7.9 %collective-permute-done.7 = bf16[4,2,16,256]{3,2,1,0:T(8,128)(2,1)S(1)} collective-permute-done((bf16[4,2,16,256]{3,2,1,0:T(8,128)(2,1)S(1)}, bf16[4,2,16,256]{3,2,1,0:T(8,128)(2,1)S(1)}, u32[]{:S(2)}, u32[]{:S(2)}) %collective-permute-start.7) | collective-permute-done | bytes 65568 | tf_op jit(solution)/shard_map/ppermute | solution.py:179
  84.1 0.0 collective-permute-done.8
  84.1 0.1 select_bitcast_fusion.4
  84.2 0.1 pad_maximum_fusion.1
  84.3 1.9 %collective-permute-start.16 = (bf16[8192,512]{1,0:T(8,128)(2,1)}, bf16[8192,512]{1,0:T(8,128)(2,1)}, u32[]{:S(2)}, u32[]{:S(2)}) collective-permute-start(bf16[8192,512]{1,0:T(8,128)(2,1)} %shard_map.100.refs_2_.refs_3_), channel_id=1, source_target_pairs={{0,1},{1,0},{2,3},{3,2},{4,5},{5,4},{6,7},{7,6},{8,9},{9,8},{10,11... | collective-permute-start | bytes 25165832 | tf_op jit(solution)/shard_map/ppermute | solution.py:179
  86.2 2.2 %collective-permute-start.10 = (bf16[8,2,16,256]{3,2,1,0:T(8,128)(2,1)S(1)}, bf16[8,2,16,256]{3,2,1,0:T(8,128)(2,1)S(1)}, u32[]{:S(2)}, u32[]{:S(2)}) collective-permute-start(bf16[8,2,16,256]{3,2,1,0:T(8,128)(2,1)S(1)} %bitcast.116), channel_id=1, source_target_pairs={{0,16},{8,24},{16,0},{24,8},{32,48},{40,56},{48,32},{56,40},{64,80... | collective-permute-start | bytes 393224 | tf_op jit(solution)/shard_map/ppermute | solution.py:179
  88.4 2.2 %collective-permute-start.9 = (bf16[2,4,4,16,1024]{4,3,2,1,0:T(8,128)(2,1)S(1)}, bf16[2,4,4,16,1024]{4,3,2,1,0:T(8,128)(2,1)S(1)}, u32[]{:S(2)}, u32[]{:S(2)}) collective-permute-start(bf16[2,4,4,16,1024]{4,3,2,1,0:T(8,128)(2,1)S(1)} %pad_maximum_fusion.1), channel_id=1, source_target_pairs={{0,1},{1,0},{2,3},{3,2},{4,5},{5,4},{6,7},{7,6},{8,9},{9,8},{10,11... | collective-permute-start | bytes 3145736 | tf_op jit(solution)/shard_map/ppermute | solution.py:179
  90.6 7.0 %collective-permute-done.10 = bf16[8,2,16,256]{3,2,1,0:T(8,128)(2,1)S(1)} collective-permute-done((bf16[8,2,16,256]{3,2,1,0:T(8,128)(2,1)S(1)}, bf16[8,2,16,256]{3,2,1,0:T(8,128)(2,1)S(1)}, u32[]{:S(2)}, u32[]{:S(2)}) %collective-permute-start.10) | collective-permute-done | bytes 131104 | tf_op jit(solution)/shard_map/ppermute | solution.py:179
  97.7 1.9 %collective-permute-start.11 = (bf16[16,2,16,256]{3,2,1,0:T(8,128)(2,1)S(1)}, bf16[16,2,16,256]{3,2,1,0:T(8,128)(2,1)S(1)}, u32[]{:S(2)}, u32[]{:S(2)}) collective-permute-start(bf16[16,2,16,256]{3,2,1,0:T(8,128)(2,1)S(1)} %bitcast.115), channel_id=1, source_target_pairs={{0,8},{8,0},{16,24},{24,16},{32,40},{40,32},{48,56},{56,48},{64,72... | collective-permute-start | bytes 786440 | tf_op jit(solution)/shard_map/ppermute | solution.py:179
  100.3 7.5 %collective-permute-done.11 = bf16[16,2,16,256]{3,2,1,0:T(8,128)(2,1)S(1)} collective-permute-done((bf16[16,2,16,256]{3,2,1,0:T(8,128)(2,1)S(1)}, bf16[16,2,16,256]{3,2,1,0:T(8,128)(2,1)S(1)}, u32[]{:S(2)}, u32[]{:S(2)}) %collective-permute-start.11) | collective-permute-done | bytes 262176 | tf_op jit(solution)/shard_map/ppermute | solution.py:179
  107.9 0.1 select_bitcast_fusion.6
  107.9 0.1 pad_maximum_fusion.3
  108.0 0.0 collective-permute-done.9
  108.0 0.1 select_bitcast_fusion.1
  108.2 0.2 pad_maximum_fusion
  108.4 0.3 copy.27
  108.7 0.0 copy-start.3
  108.7 0.0 copy-start.4
  108.7 0.7 fusion.4
  109.4 0.0 copy-start.1
  109.5 0.0 copy-start.2
  109.5 2.1 %collective-permute-start.12 = (bf16[4,4,16,256]{3,2,1,0:T(8,128)(2,1)S(1)}, bf16[4,4,16,256]{3,2,1,0:T(8,128)(2,1)S(1)}, u32[]{:S(2)}, u32[]{:S(2)}) collective-permute-start(bf16[4,4,16,256]{3,2,1,0:T(8,128)(2,1)S(1)} %get-tuple-element.35), channel_id=1, source_target_pairs={{0,256},{256,0},{512,768},{768,512},{1,257},{257,1},{513,769},{769... | collective-permute-start | bytes 393224 | tf_op jit(solution)/shard_map/ppermute | solution.py:179
  111.6 6.1 %collective-permute-start.13 = (bf16[4,4,16,256]{3,2,1,0:T(8,128)(2,1)S(1)}, bf16[4,4,16,256]{3,2,1,0:T(8,128)(2,1)S(1)}, u32[]{:S(2)}, u32[]{:S(2)}) collective-permute-start(bf16[4,4,16,256]{3,2,1,0:T(8,128)(2,1)S(1)} %get-tuple-element.37), channel_id=1, source_target_pairs={{0,512},{256,768},{512,0},{768,256},{1,513},{257,769},{513,1},{769... | collective-permute-start | bytes 393224 | tf_op jit(solution)/shard_map/ppermute | solution.py:179
  117.7 2.4 %collective-permute-start.14 = (bf16[4,4,16,256]{3,2,1,0:T(8,128)(2,1)S(1)}, bf16[4,4,16,256]{3,2,1,0:T(8,128)(2,1)S(1)}, u32[]{:S(2)}, u32[]{:S(2)}) collective-permute-start(bf16[4,4,16,256]{3,2,1,0:T(8,128)(2,1)S(1)} %get-tuple-element.36), channel_id=1, source_target_pairs={{0,768},{256,512},{512,256},{768,0},{1,769},{257,513},{513,257},{7... | collective-permute-start | bytes 393224 | tf_op jit(solution)/shard_map/ppermute | solution.py:179
  120.1 0.0 collective-permute-done.12
  120.1 1.4 collective-permute-done.13
  121.5 4.3 %collective-permute-done.14 = bf16[4,4,16,256]{3,2,1,0:T(8,128)(2,1)S(1)} collective-permute-done((bf16[4,4,16,256]{3,2,1,0:T(8,128)(2,1)S(1)}, bf16[4,4,16,256]{3,2,1,0:T(8,128)(2,1)S(1)}, u32[]{:S(2)}, u32[]{:S(2)}) %collective-permute-start.14) | collective-permute-done | bytes 131104 | tf_op jit(solution)/shard_map/ppermute | solution.py:179
  125.8 0.1 fusion.2
  125.9 0.1 multiply_reduce_fusion
  126.0 0.1 multiply_convert_fusion
  126.2 1.9 %collective-permute-start.15 = (bf16[2,64,256]{2,1,0:T(8,128)(2,1)S(1)}, bf16[2,64,256]{2,1,0:T(8,128)(2,1)S(1)}, u32[]{:S(2)}, u32[]{:S(2)}) collective-permute-start(bf16[2,64,256]{2,1,0:T(8,128)(2,1)S(1)} %dynamic-slice_bitcast_fusion.3), channel_id=1, source_target_pairs={{0,1},{1,0},{2,3},{3,2},{4,5},{5,4},{6,7},{7,6},{8,9},{9,8},{10,11... | collective-permute-start | bytes 196616 | tf_op jit(solution)/shard_map/ppermute | solution.py:179
  128.1 4.7 %shard_map.101.refs_0_ = bf16[64,4096]{1,0:T(8,128)(2,1)S(1)} custom-call(s32[1]{0:T(128)} %bitcast.section_ref, s32[4]{0:T(128)S(1)} %bitcast.105, bf16[64,4096]{1,0:T(8,128)(2,1)S(1)} %bitcast.104, bf16[4,64,256]{2,1,0:T(8,128)(2,1)S(1)} %pad_maximum_fusion.6.refs_1_.refs_2_, bf16[8192,512]{1,0:T(8,128)(2,1)} %shard_map.100.refs_2_.refs_3_), custom_call_target="tpu_custom_call" | custom-call | flops 536870912 | bytes 8388608 | tf_op jit(solution)/shard_map/pallas_call | solution.py:157
  132.8 0.7 collective-permute-start.18
  133.6 4.7 %shard_map.102.refs_2_ = bf16[64,4096]{1,0:T(8,128)(2,1)S(1)} custom-call(s32[1]{0:T(128)} %bitcast.section_ref, s32[4]{0:T(128)S(1)} %bitcast.106, bf16[64,4096]{1,0:T(8,128)(2,1)S(1)} %shard_map.101.refs_0_, bf16[2,64,256]{2,1,0:T(8,128)(2,1)S(1)} %collective-permute-done.15.refs_1_.refs_3_, bf16[8192,512]{1,0:T(8,128)(2,1)} %collective-permute-done.16.refs_2_.refs_4_), custom_call_target="tpu_custom_call" | custom-call | flops 536870912 | bytes 8388608 | tf_op jit(solution)/shard_map/pallas_call | solution.py:157
  138.3 2.7 %collective-permute-start.17 = (bf16[64,4096]{1,0:T(8,128)(2,1)S(1)}, bf16[64,4096]{1,0:T(8,128)(2,1)S(1)}, u32[]{:S(2)}, u32[]{:S(2)}) collective-permute-start(bf16[64,4096]{1,0:T(8,128)(2,1)S(1)} %shard_map.102.refs_2_), channel_id=1, source_target_pairs={{0,2},{4,6},{8,10},{12,14},{16,18},{20,22},{24,26},{28,30},{32,34}... | collective-permute-start | bytes 1572872 | tf_op jit(solution)/shard_map/ppermute | solution.py:292
  141.0 0.7 shard_map.103.refs_1_
  141.7 6.0 %collective-permute-done.17.refs_0_ = bf16[64,4096]{1,0:T(8,128)(2,1)S(1)} collective-permute-done((bf16[64,4096]{1,0:T(8,128)(2,1)S(1)}, bf16[64,4096]{1,0:T(8,128)(2,1)S(1)}, u32[]{:S(2)}, u32[]{:S(2)}) %collective-permute-start.17) | collective-permute-done | bytes 524320 | tf_op jit(solution)/shard_map/ppermute | solution.py:292
  147.6 0.7 shard_map.104.refs_0_
  148.3 0.7 collective-permute-start.19
  149.0 0.7 shard_map.105
  149.7 1.3 collective-permute-start.20
  151.0 17.7 %collective-permute-done.20 = bf16[64,4096]{1,0:T(8,128)(2,1)S(1)} collective-permute-done((bf16[64,4096]{1,0:T(8,128)(2,1)S(1)}, bf16[64,4096]{1,0:T(8,128)(2,1)S(1)}, u32[]{:S(2)}, u32[]{:S(2)}) %collective-permute-start.20) | collective-permute-done | bytes 524320 | tf_op jit(solution)/shard_map/ppermute | solution.py:297
  168.7 0.9 select_bitcast_fusion.2
  (26 shorter events, 0.3 us)
Async XLA Ops:
  0.7 7.0 %collective-permute-start = (bf16[1,16,256]{2,1,0:T(8,128)(2,1)S(1)}, bf16[1,16,256]{2,1,0:T(8,128)(2,1)S(1)}, u32[]{:S(2)}, u32[]{:S(2)}) collective-permute-start(bf16[1,16,256]{2,1,0:T(8,128)(2,1)S(1)} %maximum_bitcast_fusion.1), channel_id=1, source_target_pairs={{0,4},{4,0},{1,5},{5,1},{2,6},{6,2},{3,7},{7,3},{8,12},{12,8},{9,1... | collective-permute-start | bytes 24584 | tf_op jit(solution)/shard_map/ppermute | solution.py:179
  8.5 52.0 %collective-permute-start.1 = (bf16[1,2,16,256]{3,2,1,0:T(8,128)(2,1)S(1)}, bf16[1,2,16,256]{3,2,1,0:T(8,128)(2,1)S(1)}, u32[]{:S(2)}, u32[]{:S(2)}) collective-permute-start(bf16[1,2,16,256]{3,2,1,0:T(8,128)(2,1)S(1)} %pad_maximum_fusion.7), channel_id=1, source_target_pairs={{0,192},{8,200},{16,208},{24,216},{32,224},{40,232},{48,240},{56,2... | collective-permute-start | bytes 49160 | tf_op jit(solution)/shard_map/ppermute | solution.py:179
  31.5 33.7 %collective-permute-start.2 = (bf16[1,2,16,256]{3,2,1,0:T(8,128)(2,1)S(1)}, bf16[1,2,16,256]{3,2,1,0:T(8,128)(2,1)S(1)}, u32[]{:S(2)}, u32[]{:S(2)}) collective-permute-start(bf16[1,2,16,256]{3,2,1,0:T(8,128)(2,1)S(1)} %pad_maximum_fusion.7), channel_id=1, source_target_pairs={{0,128},{8,136},{16,144},{24,152},{32,160},{40,168},{48,176},{56,1... | collective-permute-start | bytes 49160 | tf_op jit(solution)/shard_map/ppermute | solution.py:179
  39.4 25.8 %collective-permute-start.3 = (bf16[1,2,16,256]{3,2,1,0:T(8,128)(2,1)S(1)}, bf16[1,2,16,256]{3,2,1,0:T(8,128)(2,1)S(1)}, u32[]{:S(2)}, u32[]{:S(2)}) collective-permute-start(bf16[1,2,16,256]{3,2,1,0:T(8,128)(2,1)S(1)} %pad_maximum_fusion.7), channel_id=1, source_target_pairs={{0,64},{8,72},{16,80},{24,88},{32,96},{40,104},{48,112},{56,120},{... | collective-permute-start | bytes 49160 | tf_op jit(solution)/shard_map/ppermute | solution.py:179
  46.6 18.6 %collective-permute-start.4 = (bf16[4,16,1024]{2,1,0:T(8,128)(2,1)S(1)}, bf16[4,16,1024]{2,1,0:T(8,128)(2,1)S(1)}, u32[]{:S(2)}, u32[]{:S(2)}) collective-permute-start(bf16[4,16,1024]{2,1,0:T(8,128)(2,1)S(1)} %get-tuple-element.46), channel_id=1, source_target_pairs={{0,256},{256,0},{512,768},{768,512},{1,257},{257,1},{513,769},{769... | collective-permute-start | bytes 393224 | tf_op jit(solution)/shard_map/ppermute | solution.py:179
  49.4 15.8 %collective-permute-start.5 = (bf16[4,16,1024]{2,1,0:T(8,128)(2,1)S(1)}, bf16[4,16,1024]{2,1,0:T(8,128)(2,1)S(1)}, u32[]{:S(2)}, u32[]{:S(2)}) collective-permute-start(bf16[4,16,1024]{2,1,0:T(8,128)(2,1)S(1)} %get-tuple-element.45), channel_id=1, source_target_pairs={{0,512},{256,768},{512,0},{768,256},{1,513},{257,769},{513,1},{769... | collective-permute-start | bytes 393224 | tf_op jit(solution)/shard_map/ppermute | solution.py:179
  52.4 2.2 %copy-start = (bf16[1,4096,512]{2,1,0:T(8,128)(2,1)S(1)}, bf16[1,4096,512]{2,1,0:T(8,128)(2,1)}, u32[]{:S(2)}) copy-start(bf16[1,4096,512]{2,1,0:T(8,128)(2,1)} %param.13) | copy-start | bytes 12582916
  60.5 8.1 %collective-permute-start.6 = (bf16[4,16,1024]{2,1,0:T(8,128)(2,1)S(1)}, bf16[4,16,1024]{2,1,0:T(8,128)(2,1)S(1)}, u32[]{:S(2)}, u32[]{:S(2)}) collective-permute-start(bf16[4,16,1024]{2,1,0:T(8,128)(2,1)S(1)} %get-tuple-element.44), channel_id=1, source_target_pairs={{0,768},{256,512},{512,256},{768,0},{1,769},{257,513},{513,257},{7... | collective-permute-start | bytes 393224 | tf_op jit(solution)/shard_map/ppermute | solution.py:179
  68.7 15.4 %collective-permute-start.8 = (bf16[4,4,16,1024]{3,2,1,0:T(8,128)(2,1)S(1)}, bf16[4,4,16,1024]{3,2,1,0:T(8,128)(2,1)S(1)}, u32[]{:S(2)}, u32[]{:S(2)}) collective-permute-start(bf16[4,4,16,1024]{3,2,1,0:T(8,128)(2,1)S(1)} %pad_maximum_fusion.2), channel_id=1, source_target_pairs={{0,2},{1,3},{2,0},{3,1},{4,6},{5,7},{6,4},{7,5},{8,10},{9,11},{10,... | collective-permute-start | bytes 1572872 | tf_op jit(solution)/shard_map/ppermute | solution.py:179
  71.9 12.2 %collective-permute-start.7 = (bf16[4,2,16,256]{3,2,1,0:T(8,128)(2,1)S(1)}, bf16[4,2,16,256]{3,2,1,0:T(8,128)(2,1)S(1)}, u32[]{:S(2)}, u32[]{:S(2)}) collective-permute-start(bf16[4,2,16,256]{3,2,1,0:T(8,128)(2,1)S(1)} %maximum_bitcast_fusion), channel_id=1, source_target_pairs={{0,32},{8,40},{16,48},{24,56},{32,0},{40,8},{48,16},{56,24},{64,96... | collective-permute-start | bytes 196616 | tf_op jit(solution)/shard_map/ppermute | solution.py:179
  84.3 49.2 %collective-permute-start.16 = (bf16[8192,512]{1,0:T(8,128)(2,1)}, bf16[8192,512]{1,0:T(8,128)(2,1)}, u32[]{:S(2)}, u32[]{:S(2)}) collective-permute-start(bf16[8192,512]{1,0:T(8,128)(2,1)} %shard_map.100.refs_2_.refs_3_), channel_id=1, source_target_pairs={{0,1},{1,0},{2,3},{3,2},{4,5},{5,4},{6,7},{7,6},{8,9},{9,8},{10,11... | collective-permute-start | bytes 25165832 | tf_op jit(solution)/shard_map/ppermute | solution.py:179
  86.2 11.4 %collective-permute-start.10 = (bf16[8,2,16,256]{3,2,1,0:T(8,128)(2,1)S(1)}, bf16[8,2,16,256]{3,2,1,0:T(8,128)(2,1)S(1)}, u32[]{:S(2)}, u32[]{:S(2)}) collective-permute-start(bf16[8,2,16,256]{3,2,1,0:T(8,128)(2,1)S(1)} %bitcast.116), channel_id=1, source_target_pairs={{0,16},{8,24},{16,0},{24,8},{32,48},{40,56},{48,32},{56,40},{64,80... | collective-permute-start | bytes 393224 | tf_op jit(solution)/shard_map/ppermute | solution.py:179
  88.4 19.6 %collective-permute-start.9 = (bf16[2,4,4,16,1024]{4,3,2,1,0:T(8,128)(2,1)S(1)}, bf16[2,4,4,16,1024]{4,3,2,1,0:T(8,128)(2,1)S(1)}, u32[]{:S(2)}, u32[]{:S(2)}) collective-permute-start(bf16[2,4,4,16,1024]{4,3,2,1,0:T(8,128)(2,1)S(1)} %pad_maximum_fusion.1), channel_id=1, source_target_pairs={{0,1},{1,0},{2,3},{3,2},{4,5},{5,4},{6,7},{7,6},{8,9},{9,8},{10,11... | collective-permute-start | bytes 3145736 | tf_op jit(solution)/shard_map/ppermute | solution.py:179
  97.7 10.2 %collective-permute-start.11 = (bf16[16,2,16,256]{3,2,1,0:T(8,128)(2,1)S(1)}, bf16[16,2,16,256]{3,2,1,0:T(8,128)(2,1)S(1)}, u32[]{:S(2)}, u32[]{:S(2)}) collective-permute-start(bf16[16,2,16,256]{3,2,1,0:T(8,128)(2,1)S(1)} %bitcast.115), channel_id=1, source_target_pairs={{0,8},{8,0},{16,24},{24,16},{32,40},{40,32},{48,56},{56,48},{64,72... | collective-permute-start | bytes 786440 | tf_op jit(solution)/shard_map/ppermute | solution.py:179
  108.7 11.4 %copy-start.3 = (f32[1,128]{1,0:T(1,128)S(1)}, f32[1,128]{1,0:T(1,128)}, u32[]{:S(2)}) copy-start(f32[1,128]{1,0:T(1,128)} %param.18) | copy-start | bytes 1540
  108.7 11.4 %copy-start.4 = (f32[1,128]{1,0:T(1,128)S(1)}, f32[1,128]{1,0:T(1,128)}, u32[]{:S(2)}) copy-start(f32[1,128]{1,0:T(1,128)} %param.17) | copy-start | bytes 1540
  109.4 18.6 %copy-start.1 = (bf16[1,64,4096]{2,1,0:T(8,128)(2,1)S(1)}, bf16[1,64,4096]{2,1,0:T(8,128)(2,1)}, u32[]{:S(2)}) copy-start(bf16[1,64,4096]{2,1,0:T(8,128)(2,1)} %param.10) | copy-start | bytes 1572868
  109.5 18.6 %copy-start.2 = (s32[4,1]{0,1:T(1,128)S(1)}, s32[4,1]{0,1:T(1,128)}, u32[]{:S(2)}) copy-start(s32[4,1]{0,1:T(1,128)} %param.12) | copy-start | bytes 52
  109.5 10.6 %collective-permute-start.12 = (bf16[4,4,16,256]{3,2,1,0:T(8,128)(2,1)S(1)}, bf16[4,4,16,256]{3,2,1,0:T(8,128)(2,1)S(1)}, u32[]{:S(2)}, u32[]{:S(2)}) collective-permute-start(bf16[4,4,16,256]{3,2,1,0:T(8,128)(2,1)S(1)} %get-tuple-element.35), channel_id=1, source_target_pairs={{0,256},{256,0},{512,768},{768,512},{1,257},{257,1},{513,769},{769... | collective-permute-start | bytes 393224 | tf_op jit(solution)/shard_map/ppermute | solution.py:179
  111.6 9.9 %collective-permute-start.13 = (bf16[4,4,16,256]{3,2,1,0:T(8,128)(2,1)S(1)}, bf16[4,4,16,256]{3,2,1,0:T(8,128)(2,1)S(1)}, u32[]{:S(2)}, u32[]{:S(2)}) collective-permute-start(bf16[4,4,16,256]{3,2,1,0:T(8,128)(2,1)S(1)} %get-tuple-element.37), channel_id=1, source_target_pairs={{0,512},{256,768},{512,0},{768,256},{1,513},{257,769},{513,1},{769... | collective-permute-start | bytes 393224 | tf_op jit(solution)/shard_map/ppermute | solution.py:179
  117.7 8.1 %collective-permute-start.14 = (bf16[4,4,16,256]{3,2,1,0:T(8,128)(2,1)S(1)}, bf16[4,4,16,256]{3,2,1,0:T(8,128)(2,1)S(1)}, u32[]{:S(2)}, u32[]{:S(2)}) collective-permute-start(bf16[4,4,16,256]{3,2,1,0:T(8,128)(2,1)S(1)} %get-tuple-element.36), channel_id=1, source_target_pairs={{0,768},{256,512},{512,256},{768,0},{1,769},{257,513},{513,257},{7... | collective-permute-start | bytes 393224 | tf_op jit(solution)/shard_map/ppermute | solution.py:179
  126.2 7.4 %collective-permute-start.15 = (bf16[2,64,256]{2,1,0:T(8,128)(2,1)S(1)}, bf16[2,64,256]{2,1,0:T(8,128)(2,1)S(1)}, u32[]{:S(2)}, u32[]{:S(2)}) collective-permute-start(bf16[2,64,256]{2,1,0:T(8,128)(2,1)S(1)} %dynamic-slice_bitcast_fusion.3), channel_id=1, source_target_pairs={{0,1},{1,0},{2,3},{3,2},{4,5},{5,4},{6,7},{7,6},{8,9},{9,8},{10,11... | collective-permute-start | bytes 196616 | tf_op jit(solution)/shard_map/ppermute | solution.py:179
  132.8 8.1 %collective-permute-start.18 = (bf16[64,4096]{1,0:T(8,128)(2,1)S(1)}, bf16[64,4096]{1,0:T(8,128)(2,1)S(1)}, u32[]{:S(2)}, u32[]{:S(2)}) collective-permute-start(bf16[64,4096]{1,0:T(8,128)(2,1)S(1)} %shard_map.101.refs_0_), channel_id=1, source_target_pairs={{1,3},{5,7},{9,11},{13,15},{17,19},{21,23},{25,27},{29,31},{33,35}... | collective-permute-start | bytes 1572872 | tf_op jit(solution)/shard_map/ppermute | solution.py:290
  138.3 9.3 %collective-permute-start.17 = (bf16[64,4096]{1,0:T(8,128)(2,1)S(1)}, bf16[64,4096]{1,0:T(8,128)(2,1)S(1)}, u32[]{:S(2)}, u32[]{:S(2)}) collective-permute-start(bf16[64,4096]{1,0:T(8,128)(2,1)S(1)} %shard_map.102.refs_2_), channel_id=1, source_target_pairs={{0,2},{4,6},{8,10},{12,14},{16,18},{20,22},{24,26},{28,30},{32,34}... | collective-permute-start | bytes 1572872 | tf_op jit(solution)/shard_map/ppermute | solution.py:292
  148.3 0.7 collective-permute-start.19
  149.7 19.1 %collective-permute-start.20 = (bf16[64,4096]{1,0:T(8,128)(2,1)S(1)}, bf16[64,4096]{1,0:T(8,128)(2,1)S(1)}, u32[]{:S(2)}, u32[]{:S(2)}) collective-permute-start(bf16[64,4096]{1,0:T(8,128)(2,1)S(1)} %shard_map.105), channel_id=1, source_target_pairs={{2,0},{6,4},{10,8},{14,12},{18,16},{22,20},{26,24},{30,28},{34,32}... | collective-permute-start | bytes 1572872 | tf_op jit(solution)/shard_map/ppermute | solution.py:297

commit v6 on v5

--- a/solution.py
+++ b/solution.py
@@ -120,7 +120,7 @@
             pltpu.SemaphoreType.DMA((2 * width // columns,)),
             pltpu.SemaphoreType.DMA((2 * width // columns,)),
         ],
-        compiler_params=pltpu.CompilerParams(vmem_limit_bytes=VMEM_LIMIT),
+        compiler_params=pltpu.CompilerParams(vmem_limit_bytes=60 * 2**20),
         cost_estimate=pl.CostEstimate(
             flops=0, bytes_accessed=8 * width * columns, transcendentals=0
         ),
@@ -242,24 +242,27 @@
     head_size = w_key.shape[2]
     known = jnp.concatenate([w_key[0], w_value[0]], axis=1)[None]
     known = joined(known, "yh", 1)
-    known, image_states, w_query, w_out = lax.optimization_barrier(
-        (known, image_states, w_query, w_out)
-    )
+    known, image_states = lax.optimization_barrier((known, image_states))
     distance = lax.axis_size("z") // 4
     known = joined_four(known, distance)
     slices = column_slices(image_states)
-    own_weights = stacked_weights(w_query[0], w_out[0])
-    known, slices, own_weights = lax.optimization_barrier((known, slices, own_weights))
+    known, slices = lax.optimization_barrier((known, slices))
     ordered = in_order(lax.axis_index("x"), slices)
     halves = doubled(ordered, "pipe", 2, 0)
     distance //= 2
     known = joined(known, "z", distance)
-    known, halves, own_weights = lax.optimization_barrier((known, halves, own_weights))
-    pictures = doubled(halves, "pipe", 1, 1).reshape((-1,) + ordered.shape)
-    near_weights = exchanged(own_weights, "pipe", 1)
+    known, halves, w_query, w_out = lax.optimization_barrier((known, halves, w_query, w_out))
+    pictures = doubled(halves, "pipe", 1, 1)
+    own_weights = stacked_weights(w_query[0], w_out[0])
+    distance //= 2
+    known = joined(known, "z", distance)
+    known, pictures = lax.optimization_barrier((known, pictures))
+    pictures = pictures.reshape((-1,) + ordered.shape)
     while distance > 1:
         distance //= 2
         known = joined(known, "z", distance)
+    known, own_weights = lax.optimization_barrier((known, own_weights))
+    near_weights = exchanged(own_weights, "pipe", 1)
     weights = known.reshape(-1, known.shape[-1])
     parts, depth = lax.axis_size("x"), weights.shape[0]
     sums = jnp.dot(pictures.reshape(-1, depth), weights, preferred_element_type=jnp.float32)

time: 170 us -> 165 us (0.971)
  the two profiles are of different devices: /device:TPU:22 before, /device:TPU:16 now
where the time goes in v6:
time: 165 us; the launch traced here: 164 us
  starting transfers between devices  84.8 us (51%)
  waiting for transfers between devices  54.3 us (33%)
  Pallas kernels  18.1 us (11%)
  other arithmetic  3.47 us (2%)
    ppermute x17, starting transfers between devices, exchanged(): return lax.ppermute(block, axis, [(i, i ^ distance) for i in devices])  79.4 us
    ppermute x17, waiting for transfers between devices, exchanged(): return lax.ppermute(block, axis, [(i, i ^ distance) for i in devices])  30.6 us
    ppermute x1, waiting for transfers between devices, local(): home_even = lax.ppermute(fourth, 'pipe', [(2, 0)])  17.7 us
    pallas_call x5, Pallas kernels, layer(): pl.pallas_call(functools.partial(layer_kernel, slot, len(states), choosin...  11.4 us
    pallas_call x1, Pallas kernels, stacked_weights(): pl.pallas_call(stack_kernel, out_shape=jax.ShapeDtypeStruct((2 * width, c...  6.7 us
    ppermute x1, waiting for transfers between devices, local(): from_even = lax.ppermute(second, 'pipe', [(0, 2)])  5.98 us
  transfers between devices with their start and end apart: 21, of which 11 were waited for; matrix products, arithmetic and copies ran while one was open for 1% of the time, Pallas kernels for 10%

profile of v6, /device:TPU:16, one launch (start us, length us, event | category | flops | bytes accessed | tf_op | source)
XLA Modules:
  0.0 164.0 jit_solution(4792665855781931194)
XLA Ops:
  0.0 0.7 maximum_bitcast_fusion.1
  0.7 14.9 %collective-permute-start = (bf16[1,16,256]{2,1,0:T(8,128)(2,1)S(1)}, bf16[1,16,256]{2,1,0:T(8,128)(2,1)S(1)}, u32[]{:S(2)}, u32[]{:S(2)}) collective-permute-start(bf16[1,16,256]{2,1,0:T(8,128)(2,1)S(1)} %maximum_bitcast_fusion.1), channel_id=1, source_target_pairs={{0,4},{4,0},{1,5},{5,1},{2,6},{6,2},{3,7},{7,3},{8,12},{12,8},{9,1... | collective-permute-start | bytes 24584 | tf_op jit(solution)/shard_map/ppermute | solution.py:179
  15.6 1.6 collective-permute-done
  17.2 0.7 select_bitcast_fusion.20
  17.9 6.2 %collective-permute-start.3 = (bf16[1,2,16,256]{3,2,1,0:T(8,128)(2,1)S(1)}, bf16[1,2,16,256]{3,2,1,0:T(8,128)(2,1)S(1)}, u32[]{:S(2)}, u32[]{:S(2)}) collective-permute-start(bf16[1,2,16,256]{3,2,1,0:T(8,128)(2,1)S(1)} %pad_maximum_fusion.7), channel_id=1, source_target_pairs={{0,64},{8,72},{16,80},{24,88},{32,96},{40,104},{48,112},{56,120},{... | collective-permute-start | bytes 49160 | tf_op jit(solution)/shard_map/ppermute | solution.py:179
  24.2 19.4 %collective-permute-start.2 = (bf16[1,2,16,256]{3,2,1,0:T(8,128)(2,1)S(1)}, bf16[1,2,16,256]{3,2,1,0:T(8,128)(2,1)S(1)}, u32[]{:S(2)}, u32[]{:S(2)}) collective-permute-start(bf16[1,2,16,256]{3,2,1,0:T(8,128)(2,1)S(1)} %pad_maximum_fusion.7), channel_id=1, source_target_pairs={{0,128},{8,136},{16,144},{24,152},{32,160},{40,168},{48,176},{56,1... | collective-permute-start | bytes 49160 | tf_op jit(solution)/shard_map/ppermute | solution.py:179
  43.6 1.9 %collective-permute-start.1 = (bf16[1,2,16,256]{3,2,1,0:T(8,128)(2,1)S(1)}, bf16[1,2,16,256]{3,2,1,0:T(8,128)(2,1)S(1)}, u32[]{:S(2)}, u32[]{:S(2)}) collective-permute-start(bf16[1,2,16,256]{3,2,1,0:T(8,128)(2,1)S(1)} %pad_maximum_fusion.7), channel_id=1, source_target_pairs={{0,192},{8,200},{16,208},{24,216},{32,224},{40,232},{48,240},{56,2... | collective-permute-start | bytes 49160 | tf_op jit(solution)/shard_map/ppermute | solution.py:179
  45.5 1.1 constant_dynamic-slice_fusion
  46.6 4.7 %collective-permute-start.6 = (bf16[4,16,1024]{2,1,0:T(8,128)(2,1)S(1)}, bf16[4,16,1024]{2,1,0:T(8,128)(2,1)S(1)}, u32[]{:S(2)}, u32[]{:S(2)}) collective-permute-start(bf16[4,16,1024]{2,1,0:T(8,128)(2,1)S(1)} %get-tuple-element.48), channel_id=1, source_target_pairs={{0,768},{256,512},{512,256},{768,0},{1,769},{257,513},{513,257},{7... | collective-permute-start | bytes 393224 | tf_op jit(solution)/shard_map/ppermute | solution.py:179
  51.3 2.7 %collective-permute-start.5 = (bf16[4,16,1024]{2,1,0:T(8,128)(2,1)S(1)}, bf16[4,16,1024]{2,1,0:T(8,128)(2,1)S(1)}, u32[]{:S(2)}, u32[]{:S(2)}) collective-permute-start(bf16[4,16,1024]{2,1,0:T(8,128)(2,1)S(1)} %get-tuple-element.49), channel_id=1, source_target_pairs={{0,512},{256,768},{512,0},{768,256},{1,513},{257,769},{513,1},{769... | collective-permute-start | bytes 393224 | tf_op jit(solution)/shard_map/ppermute | solution.py:179
  54.0 0.0 collective-permute-done.3
  54.0 2.4 %collective-permute-start.4 = (bf16[4,16,1024]{2,1,0:T(8,128)(2,1)S(1)}, bf16[4,16,1024]{2,1,0:T(8,128)(2,1)S(1)}, u32[]{:S(2)}, u32[]{:S(2)}) collective-permute-start(bf16[4,16,1024]{2,1,0:T(8,128)(2,1)S(1)} %get-tuple-element.50), channel_id=1, source_target_pairs={{0,256},{256,0},{512,768},{768,512},{1,257},{257,1},{513,769},{769... | collective-permute-start | bytes 393224 | tf_op jit(solution)/shard_map/ppermute | solution.py:179
  56.5 0.0 collective-permute-done.2
  56.5 1.6 collective-permute-done.1
  58.1 0.0 collective-permute-done.6
  58.1 2.3 %collective-permute-done.5 = bf16[4,16,1024]{2,1,0:T(8,128)(2,1)S(1)} collective-permute-done((bf16[4,16,1024]{2,1,0:T(8,128)(2,1)S(1)}, bf16[4,16,1024]{2,1,0:T(8,128)(2,1)S(1)}, u32[]{:S(2)}, u32[]{:S(2)}) %collective-permute-start.5) | collective-permute-done | bytes 131104 | tf_op jit(solution)/shard_map/ppermute | solution.py:179
  60.4 0.5 collective-permute-done.4
  60.9 0.1 select_bitcast_fusion.12
  61.0 0.1 pad_maximum_fusion.2
  61.0 3.2 %collective-permute-start.8 = (bf16[4,4,16,1024]{3,2,1,0:T(8,128)(2,1)S(1)}, bf16[4,4,16,1024]{3,2,1,0:T(8,128)(2,1)S(1)}, u32[]{:S(2)}, u32[]{:S(2)}) collective-permute-start(bf16[4,4,16,1024]{3,2,1,0:T(8,128)(2,1)S(1)} %pad_maximum_fusion.2), channel_id=1, source_target_pairs={{0,2},{1,3},{2,0},{3,1},{4,6},{5,7},{6,4},{7,5},{8,10},{9,11},{10,... | collective-permute-start | bytes 1572872 | tf_op jit(solution)/shard_map/ppermute | solution.py:179
  64.2 4.3 %collective-permute-start.7 = (bf16[4,2,16,256]{3,2,1,0:T(8,128)(2,1)S(1)}, bf16[4,2,16,256]{3,2,1,0:T(8,128)(2,1)S(1)}, u32[]{:S(2)}, u32[]{:S(2)}) collective-permute-start(bf16[4,2,16,256]{3,2,1,0:T(8,128)(2,1)S(1)} %maximum_bitcast_fusion), channel_id=1, source_target_pairs={{0,32},{8,40},{16,48},{24,56},{32,0},{40,8},{48,16},{56,24},{64,96... | collective-permute-start | bytes 196616 | tf_op jit(solution)/shard_map/ppermute | solution.py:179
  68.6 7.9 %collective-permute-done.7 = bf16[4,2,16,256]{3,2,1,0:T(8,128)(2,1)S(1)} collective-permute-done((bf16[4,2,16,256]{3,2,1,0:T(8,128)(2,1)S(1)}, bf16[4,2,16,256]{3,2,1,0:T(8,128)(2,1)S(1)}, u32[]{:S(2)}, u32[]{:S(2)}) %collective-permute-start.7) | collective-permute-done | bytes 65568 | tf_op jit(solution)/shard_map/ppermute | solution.py:179
  76.5 0.0 collective-permute-done.8
  76.5 0.1 select_bitcast_fusion.4
  76.6 0.1 pad_maximum_fusion.1
  76.7 1.9 %collective-permute-start.10 = (bf16[2,4,4,16,1024]{4,3,2,1,0:T(8,128)(2,1)S(1)}, bf16[2,4,4,16,1024]{4,3,2,1,0:T(8,128)(2,1)S(1)}, u32[]{:S(2)}, u32[]{:S(2)}) collective-permute-start(bf16[2,4,4,16,1024]{4,3,2,1,0:T(8,128)(2,1)S(1)} %pad_maximum_fusion.1), channel_id=1, source_target_pairs={{0,1},{1,0},{2,3},{3,2},{4,5},{5,4},{6,7},{7,6},{8,9},{9,8},{10,11... | collective-permute-start | bytes 3145736 | tf_op jit(solution)/shard_map/ppermute | solution.py:179
  78.6 2.1 %collective-permute-start.9 = (bf16[8,2,16,256]{3,2,1,0:T(8,128)(2,1)S(1)}, bf16[8,2,16,256]{3,2,1,0:T(8,128)(2,1)S(1)}, u32[]{:S(2)}, u32[]{:S(2)}) collective-permute-start(bf16[8,2,16,256]{3,2,1,0:T(8,128)(2,1)S(1)} %bitcast.118), channel_id=1, source_target_pairs={{0,16},{8,24},{16,0},{24,8},{32,48},{40,56},{48,32},{56,40},{64,80... | collective-permute-start | bytes 393224 | tf_op jit(solution)/shard_map/ppermute | solution.py:179
  80.7 9.2 %collective-permute-done.9 = bf16[8,2,16,256]{3,2,1,0:T(8,128)(2,1)S(1)} collective-permute-done((bf16[8,2,16,256]{3,2,1,0:T(8,128)(2,1)S(1)}, bf16[8,2,16,256]{3,2,1,0:T(8,128)(2,1)S(1)}, u32[]{:S(2)}, u32[]{:S(2)}) %collective-permute-start.9) | collective-permute-done | bytes 131104 | tf_op jit(solution)/shard_map/ppermute | solution.py:179
  90.0 0.1 select_bitcast_fusion.1
  90.1 0.2 pad_maximum_fusion
  90.3 1.9 %collective-permute-start.11 = (bf16[16,2,16,256]{3,2,1,0:T(8,128)(2,1)S(1)}, bf16[16,2,16,256]{3,2,1,0:T(8,128)(2,1)S(1)}, u32[]{:S(2)}, u32[]{:S(2)}) collective-permute-start(bf16[16,2,16,256]{3,2,1,0:T(8,128)(2,1)S(1)} %bitcast.116), channel_id=1, source_target_pairs={{0,8},{8,0},{16,24},{24,16},{32,40},{40,32},{48,56},{56,48},{64,72... | collective-permute-start | bytes 786440 | tf_op jit(solution)/shard_map/ppermute | solution.py:179
  92.2 6.7 %shard_map.100.refs_2_.refs_3_ = bf16[8192,512]{1,0:T(8,128)(2,1)} custom-call(bf16[4096,512]{1,0:T(8,128)(2,1)} %bitcast.111, bf16[512,4096]{1,0:T(8,128)(2,1)} %bitcast.112), custom_call_target="tpu_custom_call" | custom-call | bytes 16777216 | tf_op jit(solution)/shard_map/pallas_call | solution.py:113
  99.0 1.5 collective-permute-done.11
  100.5 0.1 pad_maximum_fusion.3
  100.6 1.9 %collective-permute-start.16 = (bf16[8192,512]{1,0:T(8,128)(2,1)}, bf16[8192,512]{1,0:T(8,128)(2,1)}, u32[]{:S(2)}, u32[]{:S(2)}) collective-permute-start(bf16[8192,512]{1,0:T(8,128)(2,1)} %shard_map.100.refs_2_.refs_3_), channel_id=1, source_target_pairs={{0,1},{1,0},{2,3},{3,2},{4,5},{5,4},{6,7},{7,6},{8,9},{9,8},{10,11... | collective-permute-start | bytes 25165832 | tf_op jit(solution)/shard_map/ppermute | solution.py:179
  103.3 0.0 copy-start.2
  103.3 0.0 copy-start.3
  103.3 0.7 fusion.4
  104.0 0.0 copy-start
  104.0 0.0 copy-start.1
  104.1 2.7 %collective-permute-start.12 = (bf16[4,4,16,256]{3,2,1,0:T(8,128)(2,1)S(1)}, bf16[4,4,16,256]{3,2,1,0:T(8,128)(2,1)S(1)}, u32[]{:S(2)}, u32[]{:S(2)}) collective-permute-start(bf16[4,4,16,256]{3,2,1,0:T(8,128)(2,1)S(1)} %get-tuple-element.39), channel_id=1, source_target_pairs={{0,256},{256,0},{512,768},{768,512},{1,257},{257,1},{513,769},{769... | collective-permute-start | bytes 393224 | tf_op jit(solution)/shard_map/ppermute | solution.py:179
  106.8 4.7 %collective-permute-start.14 = (bf16[4,4,16,256]{3,2,1,0:T(8,128)(2,1)S(1)}, bf16[4,4,16,256]{3,2,1,0:T(8,128)(2,1)S(1)}, u32[]{:S(2)}, u32[]{:S(2)}) collective-permute-start(bf16[4,4,16,256]{3,2,1,0:T(8,128)(2,1)S(1)} %get-tuple-element.40), channel_id=1, source_target_pairs={{0,768},{256,512},{512,256},{768,0},{1,769},{257,513},{513,257},{7... | collective-permute-start | bytes 393224 | tf_op jit(solution)/shard_map/ppermute | solution.py:179
  111.5 2.6 %collective-permute-start.13 = (bf16[4,4,16,256]{3,2,1,0:T(8,128)(2,1)S(1)}, bf16[4,4,16,256]{3,2,1,0:T(8,128)(2,1)S(1)}, u32[]{:S(2)}, u32[]{:S(2)}) collective-permute-start(bf16[4,4,16,256]{3,2,1,0:T(8,128)(2,1)S(1)} %get-tuple-element.41), channel_id=1, source_target_pairs={{0,512},{256,768},{512,0},{768,256},{1,513},{257,769},{513,1},{769... | collective-permute-start | bytes 393224 | tf_op jit(solution)/shard_map/ppermute | solution.py:179
  114.1 3.3 %collective-permute-done.14 = bf16[4,4,16,256]{3,2,1,0:T(8,128)(2,1)S(1)} collective-permute-done((bf16[4,4,16,256]{3,2,1,0:T(8,128)(2,1)S(1)}, bf16[4,4,16,256]{3,2,1,0:T(8,128)(2,1)S(1)}, u32[]{:S(2)}, u32[]{:S(2)}) %collective-permute-start.14) | collective-permute-done | bytes 131104 | tf_op jit(solution)/shard_map/ppermute | solution.py:179
  117.4 2.8 %collective-permute-done.13 = bf16[4,4,16,256]{3,2,1,0:T(8,128)(2,1)S(1)} collective-permute-done((bf16[4,4,16,256]{3,2,1,0:T(8,128)(2,1)S(1)}, bf16[4,4,16,256]{3,2,1,0:T(8,128)(2,1)S(1)}, u32[]{:S(2)}, u32[]{:S(2)}) %collective-permute-start.13) | collective-permute-done | bytes 131104 | tf_op jit(solution)/shard_map/ppermute | solution.py:179
  120.2 0.1 fusion.2
  120.3 0.1 multiply_reduce_fusion
  120.4 0.1 multiply_convert_fusion
  120.6 1.9 %collective-permute-start.15 = (bf16[2,64,256]{2,1,0:T(8,128)(2,1)S(1)}, bf16[2,64,256]{2,1,0:T(8,128)(2,1)S(1)}, u32[]{:S(2)}, u32[]{:S(2)}) collective-permute-start(bf16[2,64,256]{2,1,0:T(8,128)(2,1)S(1)} %dynamic-slice_bitcast_fusion.3), channel_id=1, source_target_pairs={{0,1},{1,0},{2,3},{3,2},{4,5},{5,4},{6,7},{7,6},{8,9},{9,8},{10,11... | collective-permute-start | bytes 196616 | tf_op jit(solution)/shard_map/ppermute | solution.py:179
  122.5 4.7 %shard_map.101.refs_0_ = bf16[64,4096]{1,0:T(8,128)(2,1)S(1)} custom-call(s32[1]{0:T(128)} %bitcast.section_ref, s32[4]{0:T(128)S(1)} %bitcast.105, bf16[64,4096]{1,0:T(8,128)(2,1)S(1)} %bitcast.104, bf16[4,64,256]{2,1,0:T(8,128)(2,1)S(1)} %pad_maximum_fusion.6.refs_1_.refs_2_, bf16[8192,512]{1,0:T(8,128)(2,1)} %shard_map.100.refs_2_.refs_3_), custom_call_target="tpu_custom_call" | custom-call | flops 536870912 | bytes 8388608 | tf_op jit(solution)/shard_map/pallas_call | solution.py:157
  127.3 0.7 collective-permute-start.18
  128.0 0.0 collective-permute-done.15.refs_1_.refs_3_
  128.0 0.0 collective-permute-done.16.refs_2_.refs_4_
  128.0 4.7 %shard_map.102.refs_2_ = bf16[64,4096]{1,0:T(8,128)(2,1)S(1)} custom-call(s32[1]{0:T(128)} %bitcast.section_ref, s32[4]{0:T(128)S(1)} %bitcast.106, bf16[64,4096]{1,0:T(8,128)(2,1)S(1)} %shard_map.101.refs_0_, bf16[2,64,256]{2,1,0:T(8,128)(2,1)S(1)} %collective-permute-done.15.refs_1_.refs_3_, bf16[8192,512]{1,0:T(8,128)(2,1)} %collective-permute-done.16.refs_2_.refs_4_), custom_call_target="tpu_custom_call" | custom-call | flops 536870912 | bytes 8388608 | tf_op jit(solution)/shard_map/pallas_call | solution.py:157
  132.7 2.7 %collective-permute-start.17 = (bf16[64,4096]{1,0:T(8,128)(2,1)S(1)}, bf16[64,4096]{1,0:T(8,128)(2,1)S(1)}, u32[]{:S(2)}, u32[]{:S(2)}) collective-permute-start(bf16[64,4096]{1,0:T(8,128)(2,1)S(1)} %shard_map.102.refs_2_), channel_id=1, source_target_pairs={{0,2},{4,6},{8,10},{12,14},{16,18},{20,22},{24,26},{28,30},{32,34}... | collective-permute-start | bytes 1572872 | tf_op jit(solution)/shard_map/ppermute | solution.py:295
  135.4 0.0 collective-permute-done.18.refs_0_
  135.4 0.7 shard_map.103.refs_1_
  136.1 6.0 %collective-permute-done.17.refs_0_ = bf16[64,4096]{1,0:T(8,128)(2,1)S(1)} collective-permute-done((bf16[64,4096]{1,0:T(8,128)(2,1)S(1)}, bf16[64,4096]{1,0:T(8,128)(2,1)S(1)}, u32[]{:S(2)}, u32[]{:S(2)}) %collective-permute-start.17) | collective-permute-done | bytes 524320 | tf_op jit(solution)/shard_map/ppermute | solution.py:295
  142.1 0.7 shard_map.104.refs_0_
  142.7 0.7 collective-permute-start.19
  143.4 0.7 shard_map.105
  144.1 1.3 collective-permute-start.20
  145.4 17.7 %collective-permute-done.20 = bf16[64,4096]{1,0:T(8,128)(2,1)S(1)} collective-permute-done((bf16[64,4096]{1,0:T(8,128)(2,1)S(1)}, bf16[64,4096]{1,0:T(8,128)(2,1)S(1)}, u32[]{:S(2)}, u32[]{:S(2)}) %collective-permute-start.20) | collective-permute-done | bytes 524320 | tf_op jit(solution)/shard_map/ppermute | solution.py:300
  163.2 0.9 select_bitcast_fusion.2
  (23 shorter events, 0.3 us)
Async XLA Ops:
  0.7 16.5 %collective-permute-start = (bf16[1,16,256]{2,1,0:T(8,128)(2,1)S(1)}, bf16[1,16,256]{2,1,0:T(8,128)(2,1)S(1)}, u32[]{:S(2)}, u32[]{:S(2)}) collective-permute-start(bf16[1,16,256]{2,1,0:T(8,128)(2,1)S(1)} %maximum_bitcast_fusion.1), channel_id=1, source_target_pairs={{0,4},{4,0},{1,5},{5,1},{2,6},{6,2},{3,7},{7,3},{8,12},{12,8},{9,1... | collective-permute-start | bytes 24584 | tf_op jit(solution)/shard_map/ppermute | solution.py:179
  17.9 36.1 %collective-permute-start.3 = (bf16[1,2,16,256]{3,2,1,0:T(8,128)(2,1)S(1)}, bf16[1,2,16,256]{3,2,1,0:T(8,128)(2,1)S(1)}, u32[]{:S(2)}, u32[]{:S(2)}) collective-permute-start(bf16[1,2,16,256]{3,2,1,0:T(8,128)(2,1)S(1)} %pad_maximum_fusion.7), channel_id=1, source_target_pairs={{0,64},{8,72},{16,80},{24,88},{32,96},{40,104},{48,112},{56,120},{... | collective-permute-start | bytes 49160 | tf_op jit(solution)/shard_map/ppermute | solution.py:179
  24.2 32.3 %collective-permute-start.2 = (bf16[1,2,16,256]{3,2,1,0:T(8,128)(2,1)S(1)}, bf16[1,2,16,256]{3,2,1,0:T(8,128)(2,1)S(1)}, u32[]{:S(2)}, u32[]{:S(2)}) collective-permute-start(bf16[1,2,16,256]{3,2,1,0:T(8,128)(2,1)S(1)} %pad_maximum_fusion.7), channel_id=1, source_target_pairs={{0,128},{8,136},{16,144},{24,152},{32,160},{40,168},{48,176},{56,1... | collective-permute-start | bytes 49160 | tf_op jit(solution)/shard_map/ppermute | solution.py:179
  43.6 14.5 %collective-permute-start.1 = (bf16[1,2,16,256]{3,2,1,0:T(8,128)(2,1)S(1)}, bf16[1,2,16,256]{3,2,1,0:T(8,128)(2,1)S(1)}, u32[]{:S(2)}, u32[]{:S(2)}) collective-permute-start(bf16[1,2,16,256]{3,2,1,0:T(8,128)(2,1)S(1)} %pad_maximum_fusion.7), channel_id=1, source_target_pairs={{0,192},{8,200},{16,208},{24,216},{32,224},{40,232},{48,240},{56,2... | collective-permute-start | bytes 49160 | tf_op jit(solution)/shard_map/ppermute | solution.py:179
  46.6 11.5 %collective-permute-start.6 = (bf16[4,16,1024]{2,1,0:T(8,128)(2,1)S(1)}, bf16[4,16,1024]{2,1,0:T(8,128)(2,1)S(1)}, u32[]{:S(2)}, u32[]{:S(2)}) collective-permute-start(bf16[4,16,1024]{2,1,0:T(8,128)(2,1)S(1)} %get-tuple-element.48), channel_id=1, source_target_pairs={{0,768},{256,512},{512,256},{768,0},{1,769},{257,513},{513,257},{7... | collective-permute-start | bytes 393224 | tf_op jit(solution)/shard_map/ppermute | solution.py:179
  51.3 9.1 %collective-permute-start.5 = (bf16[4,16,1024]{2,1,0:T(8,128)(2,1)S(1)}, bf16[4,16,1024]{2,1,0:T(8,128)(2,1)S(1)}, u32[]{:S(2)}, u32[]{:S(2)}) collective-permute-start(bf16[4,16,1024]{2,1,0:T(8,128)(2,1)S(1)} %get-tuple-element.49), channel_id=1, source_target_pairs={{0,512},{256,768},{512,0},{768,256},{1,513},{257,769},{513,1},{769... | collective-permute-start | bytes 393224 | tf_op jit(solution)/shard_map/ppermute | solution.py:179
  54.0 6.9 %collective-permute-start.4 = (bf16[4,16,1024]{2,1,0:T(8,128)(2,1)S(1)}, bf16[4,16,1024]{2,1,0:T(8,128)(2,1)S(1)}, u32[]{:S(2)}, u32[]{:S(2)}) collective-permute-start(bf16[4,16,1024]{2,1,0:T(8,128)(2,1)S(1)} %get-tuple-element.50), channel_id=1, source_target_pairs={{0,256},{256,0},{512,768},{768,512},{1,257},{257,1},{513,769},{769... | collective-permute-start | bytes 393224 | tf_op jit(solution)/shard_map/ppermute | solution.py:179
  61.0 15.4 %collective-permute-start.8 = (bf16[4,4,16,1024]{3,2,1,0:T(8,128)(2,1)S(1)}, bf16[4,4,16,1024]{3,2,1,0:T(8,128)(2,1)S(1)}, u32[]{:S(2)}, u32[]{:S(2)}) collective-permute-start(bf16[4,4,16,1024]{3,2,1,0:T(8,128)(2,1)S(1)} %pad_maximum_fusion.2), channel_id=1, source_target_pairs={{0,2},{1,3},{2,0},{3,1},{4,6},{5,7},{6,4},{7,5},{8,10},{9,11},{10,... | collective-permute-start | bytes 1572872 | tf_op jit(solution)/shard_map/ppermute | solution.py:179
  64.2 12.2 %collective-permute-start.7 = (bf16[4,2,16,256]{3,2,1,0:T(8,128)(2,1)S(1)}, bf16[4,2,16,256]{3,2,1,0:T(8,128)(2,1)S(1)}, u32[]{:S(2)}, u32[]{:S(2)}) collective-permute-start(bf16[4,2,16,256]{3,2,1,0:T(8,128)(2,1)S(1)} %maximum_bitcast_fusion), channel_id=1, source_target_pairs={{0,32},{8,40},{16,48},{24,56},{32,0},{40,8},{48,16},{56,24},{64,96... | collective-permute-start | bytes 196616 | tf_op jit(solution)/shard_map/ppermute | solution.py:179
  76.7 13.3 %collective-permute-start.10 = (bf16[2,4,4,16,1024]{4,3,2,1,0:T(8,128)(2,1)S(1)}, bf16[2,4,4,16,1024]{4,3,2,1,0:T(8,128)(2,1)S(1)}, u32[]{:S(2)}, u32[]{:S(2)}) collective-permute-start(bf16[2,4,4,16,1024]{4,3,2,1,0:T(8,128)(2,1)S(1)} %pad_maximum_fusion.1), channel_id=1, source_target_pairs={{0,1},{1,0},{2,3},{3,2},{4,5},{5,4},{6,7},{7,6},{8,9},{9,8},{10,11... | collective-permute-start | bytes 3145736 | tf_op jit(solution)/shard_map/ppermute | solution.py:179
  78.6 11.3 %collective-permute-start.9 = (bf16[8,2,16,256]{3,2,1,0:T(8,128)(2,1)S(1)}, bf16[8,2,16,256]{3,2,1,0:T(8,128)(2,1)S(1)}, u32[]{:S(2)}, u32[]{:S(2)}) collective-permute-start(bf16[8,2,16,256]{3,2,1,0:T(8,128)(2,1)S(1)} %bitcast.118), channel_id=1, source_target_pairs={{0,16},{8,24},{16,0},{24,8},{32,48},{40,56},{48,32},{56,40},{64,80... | collective-permute-start | bytes 393224 | tf_op jit(solution)/shard_map/ppermute | solution.py:179
  90.3 10.2 %collective-permute-start.11 = (bf16[16,2,16,256]{3,2,1,0:T(8,128)(2,1)S(1)}, bf16[16,2,16,256]{3,2,1,0:T(8,128)(2,1)S(1)}, u32[]{:S(2)}, u32[]{:S(2)}) collective-permute-start(bf16[16,2,16,256]{3,2,1,0:T(8,128)(2,1)S(1)} %bitcast.116), channel_id=1, source_target_pairs={{0,8},{8,0},{16,24},{24,16},{32,40},{40,32},{48,56},{56,48},{64,72... | collective-permute-start | bytes 786440 | tf_op jit(solution)/shard_map/ppermute | solution.py:179
  100.6 27.3 %collective-permute-start.16 = (bf16[8192,512]{1,0:T(8,128)(2,1)}, bf16[8192,512]{1,0:T(8,128)(2,1)}, u32[]{:S(2)}, u32[]{:S(2)}) collective-permute-start(bf16[8192,512]{1,0:T(8,128)(2,1)} %shard_map.100.refs_2_.refs_3_), channel_id=1, source_target_pairs={{0,1},{1,0},{2,3},{3,2},{4,5},{5,4},{6,7},{7,6},{8,9},{9,8},{10,11... | collective-permute-start | bytes 25165832 | tf_op jit(solution)/shard_map/ppermute | solution.py:179
  103.3 10.8 %copy-start.2 = (f32[1,128]{1,0:T(1,128)S(1)}, f32[1,128]{1,0:T(1,128)}, u32[]{:S(2)}) copy-start(f32[1,128]{1,0:T(1,128)} %param.18) | copy-start | bytes 1540
  103.3 10.8 %copy-start.3 = (f32[1,128]{1,0:T(1,128)S(1)}, f32[1,128]{1,0:T(1,128)}, u32[]{:S(2)}) copy-start(f32[1,128]{1,0:T(1,128)} %param.17) | copy-start | bytes 1540
  104.0 18.5 %copy-start = (bf16[1,64,4096]{2,1,0:T(8,128)(2,1)S(1)}, bf16[1,64,4096]{2,1,0:T(8,128)(2,1)}, u32[]{:S(2)}) copy-start(bf16[1,64,4096]{2,1,0:T(8,128)(2,1)} %param.10) | copy-start | bytes 1572868
  104.0 18.5 %copy-start.1 = (s32[4,1]{0,1:T(1,128)S(1)}, s32[4,1]{0,1:T(1,128)}, u32[]{:S(2)}) copy-start(s32[4,1]{0,1:T(1,128)} %param.12) | copy-start | bytes 52
  104.1 10.0 %collective-permute-start.12 = (bf16[4,4,16,256]{3,2,1,0:T(8,128)(2,1)S(1)}, bf16[4,4,16,256]{3,2,1,0:T(8,128)(2,1)S(1)}, u32[]{:S(2)}, u32[]{:S(2)}) collective-permute-start(bf16[4,4,16,256]{3,2,1,0:T(8,128)(2,1)S(1)} %get-tuple-element.39), channel_id=1, source_target_pairs={{0,256},{256,0},{512,768},{768,512},{1,257},{257,1},{513,769},{769... | collective-permute-start | bytes 393224 | tf_op jit(solution)/shard_map/ppermute | solution.py:179
  106.8 10.6 %collective-permute-start.14 = (bf16[4,4,16,256]{3,2,1,0:T(8,128)(2,1)S(1)}, bf16[4,4,16,256]{3,2,1,0:T(8,128)(2,1)S(1)}, u32[]{:S(2)}, u32[]{:S(2)}) collective-permute-start(bf16[4,4,16,256]{3,2,1,0:T(8,128)(2,1)S(1)} %get-tuple-element.40), channel_id=1, source_target_pairs={{0,768},{256,512},{512,256},{768,0},{1,769},{257,513},{513,257},{7... | collective-permute-start | bytes 393224 | tf_op jit(solution)/shard_map/ppermute | solution.py:179
  111.5 8.7 %collective-permute-start.13 = (bf16[4,4,16,256]{3,2,1,0:T(8,128)(2,1)S(1)}, bf16[4,4,16,256]{3,2,1,0:T(8,128)(2,1)S(1)}, u32[]{:S(2)}, u32[]{:S(2)}) collective-permute-start(bf16[4,4,16,256]{3,2,1,0:T(8,128)(2,1)S(1)} %get-tuple-element.41), channel_id=1, source_target_pairs={{0,512},{256,768},{512,0},{768,256},{1,513},{257,769},{513,1},{769... | collective-permute-start | bytes 393224 | tf_op jit(solution)/shard_map/ppermute | solution.py:179
  120.6 7.4 %collective-permute-start.15 = (bf16[2,64,256]{2,1,0:T(8,128)(2,1)S(1)}, bf16[2,64,256]{2,1,0:T(8,128)(2,1)S(1)}, u32[]{:S(2)}, u32[]{:S(2)}) collective-permute-start(bf16[2,64,256]{2,1,0:T(8,128)(2,1)S(1)} %dynamic-slice_bitcast_fusion.3), channel_id=1, source_target_pairs={{0,1},{1,0},{2,3},{3,2},{4,5},{5,4},{6,7},{7,6},{8,9},{9,8},{10,11... | collective-permute-start | bytes 196616 | tf_op jit(solution)/shard_map/ppermute | solution.py:179
  127.3 8.1 %collective-permute-start.18 = (bf16[64,4096]{1,0:T(8,128)(2,1)S(1)}, bf16[64,4096]{1,0:T(8,128)(2,1)S(1)}, u32[]{:S(2)}, u32[]{:S(2)}) collective-permute-start(bf16[64,4096]{1,0:T(8,128)(2,1)S(1)} %shard_map.101.refs_0_), channel_id=1, source_target_pairs={{1,3},{5,7},{9,11},{13,15},{17,19},{21,23},{25,27},{29,31},{33,35}... | collective-permute-start | bytes 1572872 | tf_op jit(solution)/shard_map/ppermute | solution.py:293
  132.7 9.3 %collective-permute-start.17 = (bf16[64,4096]{1,0:T(8,128)(2,1)S(1)}, bf16[64,4096]{1,0:T(8,128)(2,1)S(1)}, u32[]{:S(2)}, u32[]{:S(2)}) collective-permute-start(bf16[64,4096]{1,0:T(8,128)(2,1)S(1)} %shard_map.102.refs_2_), channel_id=1, source_target_pairs={{0,2},{4,6},{8,10},{12,14},{16,18},{20,22},{24,26},{28,30},{32,34}... | collective-permute-start | bytes 1572872 | tf_op jit(solution)/shard_map/ppermute | solution.py:295
  142.7 0.7 collective-permute-start.19
  144.1 19.1 %collective-permute-start.20 = (bf16[64,4096]{1,0:T(8,128)(2,1)S(1)}, bf16[64,4096]{1,0:T(8,128)(2,1)S(1)}, u32[]{:S(2)}, u32[]{:S(2)}) collective-permute-start(bf16[64,4096]{1,0:T(8,128)(2,1)S(1)} %shard_map.105), channel_id=1, source_target_pairs={{2,0},{6,4},{10,8},{14,12},{18,16},{22,20},{26,24},{30,28},{34,32}... | collective-permute-start | bytes 1572872 | tf_op jit(solution)/shard_map/ppermute | solution.py:300

commit v7 on v6

--- a/solution.py
+++ b/solution.py
@@ -10,7 +10,7 @@
 from jax.sharding import PartitionSpec as P
 
 epsilon = 1e-06
-VMEM_LIMIT = 48 * 2**20
+VMEM_LIMIT = 24 * 2**20
 SECTIONS = 4
 
 
@@ -21,18 +21,13 @@
 
 def layer_kernel(slot, arrivals, choosing, section_ref, first_seen_ref, *refs):
     states = refs[:arrivals]
-    rows_ref, weights_ref, out_ref, weights, sems = refs[arrivals:]
+    rows_ref, weights, out_ref = refs[arrivals:]
     rows, width = out_ref.shape
     columns = weights.shape[1]
     head_size = rows_ref.shape[2] // 2
     heads = columns // head_size
-    pieces = sems.shape[0]
-    depth = weights.shape[0] // pieces
+    depth = min(width, 2 * columns)
     active, batch, chosen = slot(section_ref[0])
-
-    def fetch(piece):
-        rows_of = pl.ds(piece * depth, depth)
-        return pltpu.make_async_copy(weights_ref.at[rows_of, :], weights.at[rows_of, :], sems.at[piece])
 
     def state(start, size):
         held = states[0][:, start : start + size]
@@ -42,11 +37,8 @@
 
     @pl.when(active)
     def _():
-        for piece in range(pieces):
-            fetch(piece).start()
         query_sums = jnp.zeros((rows, columns), jnp.float32)
         for piece in range(width // depth):
-            fetch(piece).wait()
             start = piece * depth
             query_sums += jnp.dot(
                 state(start, depth), weights[start : start + depth], preferred_element_type=jnp.float32
@@ -72,8 +64,6 @@
         positions = lax.broadcasted_iota(jnp.int32, (rows, 1), 0)
         seen = (positions >= first_seen_ref[batch]).astype(jnp.float32)
         for start in range(0, width, columns):
-            if start % depth == 0:
-                fetch((width + start) // depth).wait()
             block = weights[width + start : width + start + columns]
             update = jnp.dot(attended, block, preferred_element_type=jnp.float32)
             result = state(start, columns).astype(jnp.float32) + seen * update
@@ -86,25 +76,20 @@
             out_ref[...] = states[index][...]
 
 
-def stack_kernel(w_query_ref, w_out_ref, out_ref, held, in_sems, out_sems):
+def stack_kernel(w_query_ref, w_out_ref, out_ref, sems):
     width, columns = w_query_ref.shape
-    pieces = in_sems.shape[0]
-    arriving, leaving = [], []
-    for piece in range(pieces):
+    arriving = []
+    for piece in range(sems.shape[0]):
         rows = pl.ds(piece * columns, columns)
         below = piece * columns - width
         if below < 0:
             source = w_query_ref.at[rows, :]
         else:
             source = w_out_ref.at[:, pl.ds(below, columns)]
-        arriving.append(pltpu.make_async_copy(source, held.at[rows, :], in_sems.at[piece]))
-        leaving.append(pltpu.make_async_copy(held.at[rows, :], out_ref.at[rows, :], out_sems.at[piece]))
+        arriving.append(pltpu.make_async_copy(source, out_ref.at[rows, :], sems.at[piece]))
     for copy in arriving:
         copy.start()
-    for piece in range(pieces):
-        arriving[piece].wait()
-        leaving[piece].start()
-    for copy in leaving:
+    for copy in arriving:
         copy.wait()
 
 
@@ -114,13 +99,9 @@
         stack_kernel,
         out_shape=jax.ShapeDtypeStruct((2 * width, columns), w_query.dtype),
         in_specs=[pl.BlockSpec(memory_space=pl.ANY)] * 2,
-        out_specs=pl.BlockSpec(memory_space=pl.ANY),
-        scratch_shapes=[
-            pltpu.VMEM((2 * width, columns), w_query.dtype),
-            pltpu.SemaphoreType.DMA((2 * width // columns,)),
-            pltpu.SemaphoreType.DMA((2 * width // columns,)),
-        ],
-        compiler_params=pltpu.CompilerParams(vmem_limit_bytes=60 * 2**20),
+        out_specs=pl.BlockSpec(memory_space=pltpu.VMEM),
+        scratch_shapes=[pltpu.SemaphoreType.DMA((2 * width // columns,))],
+        compiler_params=pltpu.CompilerParams(vmem_limit_bytes=VMEM_LIMIT),
         cost_estimate=pl.CostEstimate(
             flops=0, bytes_accessed=8 * width * columns, transcendentals=0
         ),
@@ -158,13 +139,8 @@
         functools.partial(layer_kernel, slot, len(states), choosing),
         out_shape=jax.ShapeDtypeStruct((rows, width), states[0].dtype),
         in_specs=[smem] * 2
-        + [vmem] * (len(states) + 1)
-        + [pl.BlockSpec(memory_space=pl.ANY)],
+        + [vmem] * (len(states) + 2),
         out_specs=vmem,
-        scratch_shapes=[
-            pltpu.VMEM(weights.shape, weights.dtype),
-            pltpu.SemaphoreType.DMA((2 * max(1, width // (2 * columns)),)),
-        ],
         compiler_params=pltpu.CompilerParams(vmem_limit_bytes=VMEM_LIMIT),
         cost_estimate=pl.CostEstimate(
             flops=4 * rows * width * columns,

time: 165 us -> 169 us (1.024)
  the two profiles are of different devices: /device:TPU:16 before, /device:TPU:32 now
where the time goes in v7:
time: 169 us; the launch traced here: 168 us
  starting transfers between devices  87.8 us (52%)
  waiting for transfers between devices  43 us (25%)
  Pallas kernels  25.6 us (15%)
  local copies, waits for them, and re-layouts  5.66 us (3%)
  other arithmetic  3.47 us (2%)
    ppermute x17, starting transfers between devices, exchanged(): return lax.ppermute(block, axis, [(i, i ^ distance) for i in devices])  82.8 us
    ppermute x17, waiting for transfers between devices, exchanged(): return lax.ppermute(block, axis, [(i, i ^ distance) for i in devices])  26.1 us
    pallas_call x5, Pallas kernels, layer(): pl.pallas_call(functools.partial(layer_kernel, slot, len(states), choosin...  21.2 us
    ppermute x1, waiting for transfers between devices, local(): home_even = lax.ppermute(fourth, 'pipe', [(2, 0)])  13.7 us
    unnamed x12, local copies, waits for them, and re-layouts  4.4 us
    pallas_call x1, Pallas kernels, stacked_weights(): pl.pallas_call(stack_kernel, out_shape=jax.ShapeDtypeStruct((2 * width, c...  4.37 us
  transfers between devices with their start and end apart: 21, of which 10 were waited for; matrix products, arithmetic and copies ran while one was open for 1% of the time, Pallas kernels for 11%

profile of v7, /device:TPU:32, one launch (start us, length us, event | category | flops | bytes accessed | tf_op | source)
XLA Modules:
  0.0 167.6 jit_solution(9937053171786055473)
XLA Ops:
  0.0 0.7 maximum_bitcast_fusion.1
  0.7 5.1 %collective-permute-start = (bf16[1,16,256]{2,1,0:T(8,128)(2,1)S(1)}, bf16[1,16,256]{2,1,0:T(8,128)(2,1)S(1)}, u32[]{:S(2)}, u32[]{:S(2)}) collective-permute-start(bf16[1,16,256]{2,1,0:T(8,128)(2,1)S(1)} %maximum_bitcast_fusion.1), channel_id=1, source_target_pairs={{0,4},{4,0},{1,5},{5,1},{2,6},{6,2},{3,7},{7,3},{8,12},{12,8},{9,1... | collective-permute-start | bytes 24584 | tf_op jit(solution)/shard_map/ppermute | solution.py:155
  5.9 1.9 %collective-permute-done = bf16[1,16,256]{2,1,0:T(8,128)(2,1)S(1)} collective-permute-done((bf16[1,16,256]{2,1,0:T(8,128)(2,1)S(1)}, bf16[1,16,256]{2,1,0:T(8,128)(2,1)S(1)}, u32[]{:S(2)}, u32[]{:S(2)}) %collective-permute-start) | collective-permute-done | bytes 8224 | tf_op jit(solution)/shard_map/ppermute | solution.py:155
  7.7 0.7 select_bitcast_fusion.20
  8.5 15.7 %collective-permute-start.3 = (bf16[1,2,16,256]{3,2,1,0:T(8,128)(2,1)S(1)}, bf16[1,2,16,256]{3,2,1,0:T(8,128)(2,1)S(1)}, u32[]{:S(2)}, u32[]{:S(2)}) collective-permute-start(bf16[1,2,16,256]{3,2,1,0:T(8,128)(2,1)S(1)} %pad_maximum_fusion.7), channel_id=1, source_target_pairs={{0,64},{8,72},{16,80},{24,88},{32,96},{40,104},{48,112},{56,120},{... | collective-permute-start | bytes 49160 | tf_op jit(solution)/shard_map/ppermute | solution.py:155
  24.2 18.5 %collective-permute-start.2 = (bf16[1,2,16,256]{3,2,1,0:T(8,128)(2,1)S(1)}, bf16[1,2,16,256]{3,2,1,0:T(8,128)(2,1)S(1)}, u32[]{:S(2)}, u32[]{:S(2)}) collective-permute-start(bf16[1,2,16,256]{3,2,1,0:T(8,128)(2,1)S(1)} %pad_maximum_fusion.7), channel_id=1, source_target_pairs={{0,128},{8,136},{16,144},{24,152},{32,160},{40,168},{48,176},{56,1... | collective-permute-start | bytes 49160 | tf_op jit(solution)/shard_map/ppermute | solution.py:155
  42.7 1.9 %collective-permute-start.1 = (bf16[1,2,16,256]{3,2,1,0:T(8,128)(2,1)S(1)}, bf16[1,2,16,256]{3,2,1,0:T(8,128)(2,1)S(1)}, u32[]{:S(2)}, u32[]{:S(2)}) collective-permute-start(bf16[1,2,16,256]{3,2,1,0:T(8,128)(2,1)S(1)} %pad_maximum_fusion.7), channel_id=1, source_target_pairs={{0,192},{8,200},{16,208},{24,216},{32,224},{40,232},{48,240},{56,2... | collective-permute-start | bytes 49160 | tf_op jit(solution)/shard_map/ppermute | solution.py:155
  44.6 1.1 constant_dynamic-slice_fusion
  45.7 4.7 %collective-permute-start.6 = (bf16[4,16,1024]{2,1,0:T(8,128)(2,1)S(1)}, bf16[4,16,1024]{2,1,0:T(8,128)(2,1)S(1)}, u32[]{:S(2)}, u32[]{:S(2)}) collective-permute-start(bf16[4,16,1024]{2,1,0:T(8,128)(2,1)S(1)} %get-tuple-element.48), channel_id=1, source_target_pairs={{0,768},{256,512},{512,256},{768,0},{1,769},{257,513},{513,257},{7... | collective-permute-start | bytes 393224 | tf_op jit(solution)/shard_map/ppermute | solution.py:155
  50.4 2.7 %collective-permute-start.5 = (bf16[4,16,1024]{2,1,0:T(8,128)(2,1)S(1)}, bf16[4,16,1024]{2,1,0:T(8,128)(2,1)S(1)}, u32[]{:S(2)}, u32[]{:S(2)}) collective-permute-start(bf16[4,16,1024]{2,1,0:T(8,128)(2,1)S(1)} %get-tuple-element.49), channel_id=1, source_target_pairs={{0,512},{256,768},{512,0},{768,256},{1,513},{257,769},{513,1},{769... | collective-permute-start | bytes 393224 | tf_op jit(solution)/shard_map/ppermute | solution.py:155
  53.1 0.0 collective-permute-done.3
  53.1 2.4 %collective-permute-start.4 = (bf16[4,16,1024]{2,1,0:T(8,128)(2,1)S(1)}, bf16[4,16,1024]{2,1,0:T(8,128)(2,1)S(1)}, u32[]{:S(2)}, u32[]{:S(2)}) collective-permute-start(bf16[4,16,1024]{2,1,0:T(8,128)(2,1)S(1)} %get-tuple-element.50), channel_id=1, source_target_pairs={{0,256},{256,0},{512,768},{768,512},{1,257},{257,1},{513,769},{769... | collective-permute-start | bytes 393224 | tf_op jit(solution)/shard_map/ppermute | solution.py:155
  55.6 1.6 collective-permute-done.1
  57.2 2.3 %collective-permute-done.5 = bf16[4,16,1024]{2,1,0:T(8,128)(2,1)S(1)} collective-permute-done((bf16[4,16,1024]{2,1,0:T(8,128)(2,1)S(1)}, bf16[4,16,1024]{2,1,0:T(8,128)(2,1)S(1)}, u32[]{:S(2)}, u32[]{:S(2)}) %collective-permute-start.5) | collective-permute-done | bytes 131104 | tf_op jit(solution)/shard_map/ppermute | solution.py:155
  59.5 0.5 collective-permute-done.4
  60.0 0.1 select_bitcast_fusion.12
  60.1 0.1 pad_maximum_fusion.2
  60.1 3.5 %collective-permute-start.8 = (bf16[4,4,16,1024]{3,2,1,0:T(8,128)(2,1)S(1)}, bf16[4,4,16,1024]{3,2,1,0:T(8,128)(2,1)S(1)}, u32[]{:S(2)}, u32[]{:S(2)}) collective-permute-start(bf16[4,4,16,1024]{3,2,1,0:T(8,128)(2,1)S(1)} %pad_maximum_fusion.2), channel_id=1, source_target_pairs={{0,2},{1,3},{2,0},{3,1},{4,6},{5,7},{6,4},{7,5},{8,10},{9,11},{10,... | collective-permute-start | bytes 1572872 | tf_op jit(solution)/shard_map/ppermute | solution.py:155
  63.6 4.3 %collective-permute-start.7 = (bf16[4,2,16,256]{3,2,1,0:T(8,128)(2,1)S(1)}, bf16[4,2,16,256]{3,2,1,0:T(8,128)(2,1)S(1)}, u32[]{:S(2)}, u32[]{:S(2)}) collective-permute-start(bf16[4,2,16,256]{3,2,1,0:T(8,128)(2,1)S(1)} %maximum_bitcast_fusion), channel_id=1, source_target_pairs={{0,32},{8,40},{16,48},{24,56},{32,0},{40,8},{48,16},{56,24},{64,96... | collective-permute-start | bytes 196616 | tf_op jit(solution)/shard_map/ppermute | solution.py:155
  67.9 7.2 %collective-permute-done.7 = bf16[4,2,16,256]{3,2,1,0:T(8,128)(2,1)S(1)} collective-permute-done((bf16[4,2,16,256]{3,2,1,0:T(8,128)(2,1)S(1)}, bf16[4,2,16,256]{3,2,1,0:T(8,128)(2,1)S(1)}, u32[]{:S(2)}, u32[]{:S(2)}) %collective-permute-start.7) | collective-permute-done | bytes 65568 | tf_op jit(solution)/shard_map/ppermute | solution.py:155
  75.1 0.0 collective-permute-done.8
  75.2 0.1 select_bitcast_fusion.4
  75.3 0.1 pad_maximum_fusion.1
  75.4 1.9 %collective-permute-start.10 = (bf16[2,4,4,16,1024]{4,3,2,1,0:T(8,128)(2,1)S(1)}, bf16[2,4,4,16,1024]{4,3,2,1,0:T(8,128)(2,1)S(1)}, u32[]{:S(2)}, u32[]{:S(2)}) collective-permute-start(bf16[2,4,4,16,1024]{4,3,2,1,0:T(8,128)(2,1)S(1)} %pad_maximum_fusion.1), channel_id=1, source_target_pairs={{0,1},{1,0},{2,3},{3,2},{4,5},{5,4},{6,7},{7,6},{8,9},{9,8},{10,11... | collective-permute-start | bytes 3145736 | tf_op jit(solution)/shard_map/ppermute | solution.py:155
  77.3 2.2 %collective-permute-start.9 = (bf16[8,2,16,256]{3,2,1,0:T(8,128)(2,1)S(1)}, bf16[8,2,16,256]{3,2,1,0:T(8,128)(2,1)S(1)}, u32[]{:S(2)}, u32[]{:S(2)}) collective-permute-start(bf16[8,2,16,256]{3,2,1,0:T(8,128)(2,1)S(1)} %bitcast.118), channel_id=1, source_target_pairs={{0,16},{8,24},{16,0},{24,8},{32,48},{40,56},{48,32},{56,40},{64,80... | collective-permute-start | bytes 393224 | tf_op jit(solution)/shard_map/ppermute | solution.py:155
  79.5 6.6 %collective-permute-done.9 = bf16[8,2,16,256]{3,2,1,0:T(8,128)(2,1)S(1)} collective-permute-done((bf16[8,2,16,256]{3,2,1,0:T(8,128)(2,1)S(1)}, bf16[8,2,16,256]{3,2,1,0:T(8,128)(2,1)S(1)}, u32[]{:S(2)}, u32[]{:S(2)}) %collective-permute-start.9) | collective-permute-done | bytes 131104 | tf_op jit(solution)/shard_map/ppermute | solution.py:155
  86.2 0.0 collective-permute-done.10
  86.2 0.1 select_bitcast_fusion.1
  86.3 0.2 pad_maximum_fusion
  86.5 6.1 %collective-permute-start.11 = (bf16[16,2,16,256]{3,2,1,0:T(8,128)(2,1)S(1)}, bf16[16,2,16,256]{3,2,1,0:T(8,128)(2,1)S(1)}, u32[]{:S(2)}, u32[]{:S(2)}) collective-permute-start(bf16[16,2,16,256]{3,2,1,0:T(8,128)(2,1)S(1)} %bitcast.116), channel_id=1, source_target_pairs={{0,8},{8,0},{16,24},{24,16},{32,40},{40,32},{48,56},{56,48},{64,72... | collective-permute-start | bytes 786440 | tf_op jit(solution)/shard_map/ppermute | solution.py:155
  92.6 0.0 copy-start
  92.6 2.2 %copy-done = bf16[1,4096,512]{2,1,0:T(8,128)(2,1)S(1)} copy-done((bf16[1,4096,512]{2,1,0:T(8,128)(2,1)S(1)}, bf16[1,4096,512]{2,1,0:T(8,128)(2,1)}, u32[]{:S(2)}) %copy-start) | copy-done | bytes 4194328
  94.8 2.2 %copy-done.1 = bf16[1,512,4096]{2,1,0:T(8,128)(2,1)S(1)} copy-done((bf16[1,512,4096]{2,1,0:T(8,128)(2,1)S(1)}, bf16[1,512,4096]{2,1,0:T(8,128)(2,1)}, u32[]{:S(2)}) %copy-start.1) | copy-done | bytes 4194328
  97.0 4.4 %shard_map.100.refs_2_.refs_3_ = bf16[8192,512]{1,0:T(8,128)(2,1)} custom-call(bf16[4096,512]{1,0:T(8,128)(2,1)S(1)} %bitcast.103, bf16[512,4096]{1,0:T(8,128)(2,1)S(1)} %bitcast.104), custom_call_target="tpu_custom_call" | custom-call | bytes 16777216 | tf_op jit(solution)/shard_map/pallas_call | solution.py:98
  101.5 0.1 pad_maximum_fusion.3
  101.6 1.9 %collective-permute-start.16 = (bf16[8192,512]{1,0:T(8,128)(2,1)}, bf16[8192,512]{1,0:T(8,128)(2,1)}, u32[]{:S(2)}, u32[]{:S(2)}) collective-permute-start(bf16[8192,512]{1,0:T(8,128)(2,1)} %shard_map.100.refs_2_.refs_3_), channel_id=1, source_target_pairs={{0,1},{1,0},{2,3},{3,2},{4,5},{5,4},{6,7},{7,6},{8,9},{9,8},{10,11... | collective-permute-start | bytes 25165832 | tf_op jit(solution)/shard_map/ppermute | solution.py:155
  104.2 0.0 copy-start.4
  104.2 0.0 copy-start.5
  104.2 0.7 fusion.4
  105.0 0.0 copy-start.2
  105.0 0.0 copy-start.3
  105.0 2.7 %collective-permute-start.12 = (bf16[4,4,16,256]{3,2,1,0:T(8,128)(2,1)S(1)}, bf16[4,4,16,256]{3,2,1,0:T(8,128)(2,1)S(1)}, u32[]{:S(2)}, u32[]{:S(2)}) collective-permute-start(bf16[4,4,16,256]{3,2,1,0:T(8,128)(2,1)S(1)} %get-tuple-element.39), channel_id=1, source_target_pairs={{0,256},{256,0},{512,768},{768,512},{1,257},{257,1},{513,769},{769... | collective-permute-start | bytes 393224 | tf_op jit(solution)/shard_map/ppermute | solution.py:155
  107.7 4.7 %collective-permute-start.14 = (bf16[4,4,16,256]{3,2,1,0:T(8,128)(2,1)S(1)}, bf16[4,4,16,256]{3,2,1,0:T(8,128)(2,1)S(1)}, u32[]{:S(2)}, u32[]{:S(2)}) collective-permute-start(bf16[4,4,16,256]{3,2,1,0:T(8,128)(2,1)S(1)} %get-tuple-element.40), channel_id=1, source_target_pairs={{0,768},{256,512},{512,256},{768,0},{1,769},{257,513},{513,257},{7... | collective-permute-start | bytes 393224 | tf_op jit(solution)/shard_map/ppermute | solution.py:155
  112.4 2.6 %collective-permute-start.13 = (bf16[4,4,16,256]{3,2,1,0:T(8,128)(2,1)S(1)}, bf16[4,4,16,256]{3,2,1,0:T(8,128)(2,1)S(1)}, u32[]{:S(2)}, u32[]{:S(2)}) collective-permute-start(bf16[4,4,16,256]{3,2,1,0:T(8,128)(2,1)S(1)} %get-tuple-element.41), channel_id=1, source_target_pairs={{0,512},{256,768},{512,0},{768,256},{1,513},{257,769},{513,1},{769... | collective-permute-start | bytes 393224 | tf_op jit(solution)/shard_map/ppermute | solution.py:155
  115.0 3.3 %collective-permute-done.14 = bf16[4,4,16,256]{3,2,1,0:T(8,128)(2,1)S(1)} collective-permute-done((bf16[4,4,16,256]{3,2,1,0:T(8,128)(2,1)S(1)}, bf16[4,4,16,256]{3,2,1,0:T(8,128)(2,1)S(1)}, u32[]{:S(2)}, u32[]{:S(2)}) %collective-permute-start.14) | collective-permute-done | bytes 131104 | tf_op jit(solution)/shard_map/ppermute | solution.py:155
  118.3 2.8 %collective-permute-done.13 = bf16[4,4,16,256]{3,2,1,0:T(8,128)(2,1)S(1)} collective-permute-done((bf16[4,4,16,256]{3,2,1,0:T(8,128)(2,1)S(1)}, bf16[4,4,16,256]{3,2,1,0:T(8,128)(2,1)S(1)}, u32[]{:S(2)}, u32[]{:S(2)}) %collective-permute-start.13) | collective-permute-done | bytes 131104 | tf_op jit(solution)/shard_map/ppermute | solution.py:155
  121.1 0.1 fusion.2
  121.2 0.1 multiply_reduce_fusion
  121.3 0.1 multiply_convert_fusion
  121.5 1.9 %collective-permute-start.15 = (bf16[2,64,256]{2,1,0:T(8,128)(2,1)S(1)}, bf16[2,64,256]{2,1,0:T(8,128)(2,1)S(1)}, u32[]{:S(2)}, u32[]{:S(2)}) collective-permute-start(bf16[2,64,256]{2,1,0:T(8,128)(2,1)S(1)} %dynamic-slice_bitcast_fusion.3), channel_id=1, source_target_pairs={{0,1},{1,0},{2,3},{3,2},{4,5},{5,4},{6,7},{7,6},{8,9},{9,8},{10,11... | collective-permute-start | bytes 196616 | tf_op jit(solution)/shard_map/ppermute | solution.py:155
  123.5 5.5 %shard_map.101.refs_0_ = bf16[64,4096]{1,0:T(8,128)(2,1)S(1)} custom-call(s32[1]{0:T(128)} %bitcast.section_ref, s32[4]{0:T(128)S(1)} %bitcast.107, bf16[64,4096]{1,0:T(8,128)(2,1)S(1)} %bitcast.106, bf16[4,64,256]{2,1,0:T(8,128)(2,1)S(1)} %pad_maximum_fusion.6.refs_1_.refs_2_, bf16[8192,512]{1,0:T(8,128)(2,1)} %shard_map.100.refs_2_.refs_3_), custom_call_target="tpu_custom_call" | custom-call | flops 536870912 | bytes 8388608 | tf_op jit(solution)/shard_map/pallas_call | solution.py:138
  128.9 0.7 collective-permute-start.18
  129.6 5.5 %shard_map.102.refs_2_ = bf16[64,4096]{1,0:T(8,128)(2,1)S(1)} custom-call(s32[1]{0:T(128)} %bitcast.section_ref, s32[4]{0:T(128)S(1)} %bitcast.108, bf16[64,4096]{1,0:T(8,128)(2,1)S(1)} %shard_map.101.refs_0_, bf16[2,64,256]{2,1,0:T(8,128)(2,1)S(1)} %collective-permute-done.15.refs_1_.refs_3_, bf16[8192,512]{1,0:T(8,128)(2,1)} %collective-permute-done.16.refs_2_.refs_4_), custom_call_target="tpu_custom_call" | custom-call | flops 536870912 | bytes 8388608 | tf_op jit(solution)/shard_map/pallas_call | solution.py:138
  135.1 2.4 %collective-permute-start.17 = (bf16[64,4096]{1,0:T(8,128)(2,1)S(1)}, bf16[64,4096]{1,0:T(8,128)(2,1)S(1)}, u32[]{:S(2)}, u32[]{:S(2)}) collective-permute-start(bf16[64,4096]{1,0:T(8,128)(2,1)S(1)} %shard_map.102.refs_2_), channel_id=1, source_target_pairs={{0,2},{4,6},{8,10},{12,14},{16,18},{20,22},{24,26},{28,30},{32,34}... | collective-permute-start | bytes 1572872 | tf_op jit(solution)/shard_map/ppermute | solution.py:271
  137.5 0.0 collective-permute-done.18.refs_0_
  137.5 3.4 %shard_map.103.refs_1_ = bf16[64,4096]{1,0:T(8,128)(2,1)S(1)} custom-call(s32[1]{0:T(128)} %bitcast.section_ref, s32[4]{0:T(128)S(1)} %bitcast.109, bf16[64,4096]{1,0:T(8,128)(2,1)S(1)} %collective-permute-done.18.refs_0_, bf16[2,64,256]{2,1,0:T(8,128)(2,1)S(1)} %collective-permute-done.15.refs_1_.refs_3_, ...), custom_call_target="tpu_custom_call" | custom-call | flops 536870912 | bytes 8388608 | tf_op jit(solution)/shard_map/pallas_call | solution.py:138
  141.0 3.2 %collective-permute-done.17.refs_0_ = bf16[64,4096]{1,0:T(8,128)(2,1)S(1)} collective-permute-done((bf16[64,4096]{1,0:T(8,128)(2,1)S(1)}, bf16[64,4096]{1,0:T(8,128)(2,1)S(1)}, u32[]{:S(2)}, u32[]{:S(2)}) %collective-permute-start.17) | collective-permute-done | bytes 524320 | tf_op jit(solution)/shard_map/ppermute | solution.py:271
  144.2 3.4 %shard_map.104.refs_0_ = bf16[64,4096]{1,0:T(8,128)(2,1)S(1)} custom-call(s32[1]{0:T(128)} %bitcast.section_ref, s32[4]{0:T(128)S(1)} %bitcast.110, bf16[64,4096]{1,0:T(8,128)(2,1)S(1)} %collective-permute-done.17.refs_0_, bf16[64,4096]{1,0:T(8,128)(2,1)S(1)} %shard_map.103.refs_1_, bf16[4,64,256]{2,1,0:T(8,128)(2,1)S(1)} %pad_maximum_fusion.6.refs_1_.refs_2_, ...), custom_call_target="tpu_custom_call" | custom-call | flops 536870912 | bytes 8388608 | tf_op jit(solution)/shard_map/pallas_call | solution.py:138
  147.6 0.7 collective-permute-start.19
  148.3 0.0 collective-permute-done.19.refs_1_
  148.3 3.4 %shard_map.105 = bf16[64,4096]{1,0:T(8,128)(2,1)S(1)} custom-call(s32[1]{0:T(128)} %bitcast.section_ref, s32[4]{0:T(128)S(1)} %bitcast.111, bf16[64,4096]{1,0:T(8,128)(2,1)S(1)} %shard_map.104.refs_0_, bf16[64,4096]{1,0:T(8,128)(2,1)S(1)} %collective-permute-done.19.refs_1_, bf16[64,4096]{1,0:T(8,128)(2,1)S(1)} %shard_map.102.refs_2_, ...), custom_call_target="tpu_custom_call" | custom-call | flops 536870912 | bytes 8388608 | tf_op jit(solution)/shard_map/pallas_call | solution.py:138
  151.8 1.3 collective-permute-start.20
  153.1 13.7 %collective-permute-done.20 = bf16[64,4096]{1,0:T(8,128)(2,1)S(1)} collective-permute-done((bf16[64,4096]{1,0:T(8,128)(2,1)S(1)}, bf16[64,4096]{1,0:T(8,128)(2,1)S(1)}, u32[]{:S(2)}, u32[]{:S(2)}) %collective-permute-start.20) | collective-permute-done | bytes 524320 | tf_op jit(solution)/shard_map/ppermute | solution.py:276
  166.8 0.9 select_bitcast_fusion.2
  (27 shorter events, 0.3 us)
Async XLA Ops:
  0.7 7.0 %collective-permute-start = (bf16[1,16,256]{2,1,0:T(8,128)(2,1)S(1)}, bf16[1,16,256]{2,1,0:T(8,128)(2,1)S(1)}, u32[]{:S(2)}, u32[]{:S(2)}) collective-permute-start(bf16[1,16,256]{2,1,0:T(8,128)(2,1)S(1)} %maximum_bitcast_fusion.1), channel_id=1, source_target_pairs={{0,4},{4,0},{1,5},{5,1},{2,6},{6,2},{3,7},{7,3},{8,12},{12,8},{9,1... | collective-permute-start | bytes 24584 | tf_op jit(solution)/shard_map/ppermute | solution.py:155
  8.5 44.7 %collective-permute-start.3 = (bf16[1,2,16,256]{3,2,1,0:T(8,128)(2,1)S(1)}, bf16[1,2,16,256]{3,2,1,0:T(8,128)(2,1)S(1)}, u32[]{:S(2)}, u32[]{:S(2)}) collective-permute-start(bf16[1,2,16,256]{3,2,1,0:T(8,128)(2,1)S(1)} %pad_maximum_fusion.7), channel_id=1, source_target_pairs={{0,64},{8,72},{16,80},{24,88},{32,96},{40,104},{48,112},{56,120},{... | collective-permute-start | bytes 49160 | tf_op jit(solution)/shard_map/ppermute | solution.py:155
  24.2 31.4 %collective-permute-start.2 = (bf16[1,2,16,256]{3,2,1,0:T(8,128)(2,1)S(1)}, bf16[1,2,16,256]{3,2,1,0:T(8,128)(2,1)S(1)}, u32[]{:S(2)}, u32[]{:S(2)}) collective-permute-start(bf16[1,2,16,256]{3,2,1,0:T(8,128)(2,1)S(1)} %pad_maximum_fusion.7), channel_id=1, source_target_pairs={{0,128},{8,136},{16,144},{24,152},{32,160},{40,168},{48,176},{56,1... | collective-permute-start | bytes 49160 | tf_op jit(solution)/shard_map/ppermute | solution.py:155
  42.7 14.5 %collective-permute-start.1 = (bf16[1,2,16,256]{3,2,1,0:T(8,128)(2,1)S(1)}, bf16[1,2,16,256]{3,2,1,0:T(8,128)(2,1)S(1)}, u32[]{:S(2)}, u32[]{:S(2)}) collective-permute-start(bf16[1,2,16,256]{3,2,1,0:T(8,128)(2,1)S(1)} %pad_maximum_fusion.7), channel_id=1, source_target_pairs={{0,192},{8,200},{16,208},{24,216},{32,224},{40,232},{48,240},{56,2... | collective-permute-start | bytes 49160 | tf_op jit(solution)/shard_map/ppermute | solution.py:155
  45.7 11.5 %collective-permute-start.6 = (bf16[4,16,1024]{2,1,0:T(8,128)(2,1)S(1)}, bf16[4,16,1024]{2,1,0:T(8,128)(2,1)S(1)}, u32[]{:S(2)}, u32[]{:S(2)}) collective-permute-start(bf16[4,16,1024]{2,1,0:T(8,128)(2,1)S(1)} %get-tuple-element.48), channel_id=1, source_target_pairs={{0,768},{256,512},{512,256},{768,0},{1,769},{257,513},{513,257},{7... | collective-permute-start | bytes 393224 | tf_op jit(solution)/shard_map/ppermute | solution.py:155
  50.4 9.1 %collective-permute-start.5 = (bf16[4,16,1024]{2,1,0:T(8,128)(2,1)S(1)}, bf16[4,16,1024]{2,1,0:T(8,128)(2,1)S(1)}, u32[]{:S(2)}, u32[]{:S(2)}) collective-permute-start(bf16[4,16,1024]{2,1,0:T(8,128)(2,1)S(1)} %get-tuple-element.49), channel_id=1, source_target_pairs={{0,512},{256,768},{512,0},{768,256},{1,513},{257,769},{513,1},{769... | collective-permute-start | bytes 393224 | tf_op jit(solution)/shard_map/ppermute | solution.py:155
  53.1 6.9 %collective-permute-start.4 = (bf16[4,16,1024]{2,1,0:T(8,128)(2,1)S(1)}, bf16[4,16,1024]{2,1,0:T(8,128)(2,1)S(1)}, u32[]{:S(2)}, u32[]{:S(2)}) collective-permute-start(bf16[4,16,1024]{2,1,0:T(8,128)(2,1)S(1)} %get-tuple-element.50), channel_id=1, source_target_pairs={{0,256},{256,0},{512,768},{768,512},{1,257},{257,1},{513,769},{769... | collective-permute-start | bytes 393224 | tf_op jit(solution)/shard_map/ppermute | solution.py:155
  60.1 15.0 %collective-permute-start.8 = (bf16[4,4,16,1024]{3,2,1,0:T(8,128)(2,1)S(1)}, bf16[4,4,16,1024]{3,2,1,0:T(8,128)(2,1)S(1)}, u32[]{:S(2)}, u32[]{:S(2)}) collective-permute-start(bf16[4,4,16,1024]{3,2,1,0:T(8,128)(2,1)S(1)} %pad_maximum_fusion.2), channel_id=1, source_target_pairs={{0,2},{1,3},{2,0},{3,1},{4,6},{5,7},{6,4},{7,5},{8,10},{9,11},{10,... | collective-permute-start | bytes 1572872 | tf_op jit(solution)/shard_map/ppermute | solution.py:155
  63.6 11.5 %collective-permute-start.7 = (bf16[4,2,16,256]{3,2,1,0:T(8,128)(2,1)S(1)}, bf16[4,2,16,256]{3,2,1,0:T(8,128)(2,1)S(1)}, u32[]{:S(2)}, u32[]{:S(2)}) collective-permute-start(bf16[4,2,16,256]{3,2,1,0:T(8,128)(2,1)S(1)} %maximum_bitcast_fusion), channel_id=1, source_target_pairs={{0,32},{8,40},{16,48},{24,56},{32,0},{40,8},{48,16},{56,24},{64,96... | collective-permute-start | bytes 196616 | tf_op jit(solution)/shard_map/ppermute | solution.py:155
  75.4 10.8 %collective-permute-start.10 = (bf16[2,4,4,16,1024]{4,3,2,1,0:T(8,128)(2,1)S(1)}, bf16[2,4,4,16,1024]{4,3,2,1,0:T(8,128)(2,1)S(1)}, u32[]{:S(2)}, u32[]{:S(2)}) collective-permute-start(bf16[2,4,4,16,1024]{4,3,2,1,0:T(8,128)(2,1)S(1)} %pad_maximum_fusion.1), channel_id=1, source_target_pairs={{0,1},{1,0},{2,3},{3,2},{4,5},{5,4},{6,7},{7,6},{8,9},{9,8},{10,11... | collective-permute-start | bytes 3145736 | tf_op jit(solution)/shard_map/ppermute | solution.py:155
  77.3 8.8 %collective-permute-start.9 = (bf16[8,2,16,256]{3,2,1,0:T(8,128)(2,1)S(1)}, bf16[8,2,16,256]{3,2,1,0:T(8,128)(2,1)S(1)}, u32[]{:S(2)}, u32[]{:S(2)}) collective-permute-start(bf16[8,2,16,256]{3,2,1,0:T(8,128)(2,1)S(1)} %bitcast.118), channel_id=1, source_target_pairs={{0,16},{8,24},{16,0},{24,8},{32,48},{40,56},{48,32},{56,40},{64,80... | collective-permute-start | bytes 393224 | tf_op jit(solution)/shard_map/ppermute | solution.py:155
  86.5 14.9 %collective-permute-start.11 = (bf16[16,2,16,256]{3,2,1,0:T(8,128)(2,1)S(1)}, bf16[16,2,16,256]{3,2,1,0:T(8,128)(2,1)S(1)}, u32[]{:S(2)}, u32[]{:S(2)}) collective-permute-start(bf16[16,2,16,256]{3,2,1,0:T(8,128)(2,1)S(1)} %bitcast.116), channel_id=1, source_target_pairs={{0,8},{8,0},{16,24},{24,16},{32,40},{40,32},{48,56},{56,48},{64,72... | collective-permute-start | bytes 786440 | tf_op jit(solution)/shard_map/ppermute | solution.py:155
  92.6 2.2 %copy-start = (bf16[1,4096,512]{2,1,0:T(8,128)(2,1)S(1)}, bf16[1,4096,512]{2,1,0:T(8,128)(2,1)}, u32[]{:S(2)}) copy-start(bf16[1,4096,512]{2,1,0:T(8,128)(2,1)} %param.13) | copy-start | bytes 12582916
  94.8 2.2 %copy-start.1 = (bf16[1,512,4096]{2,1,0:T(8,128)(2,1)S(1)}, bf16[1,512,4096]{2,1,0:T(8,128)(2,1)}, u32[]{:S(2)}) copy-start(bf16[1,512,4096]{2,1,0:T(8,128)(2,1)} %param.16) | copy-start | bytes 12582916
  101.6 28.1 %collective-permute-start.16 = (bf16[8192,512]{1,0:T(8,128)(2,1)}, bf16[8192,512]{1,0:T(8,128)(2,1)}, u32[]{:S(2)}, u32[]{:S(2)}) collective-permute-start(bf16[8192,512]{1,0:T(8,128)(2,1)} %shard_map.100.refs_2_.refs_3_), channel_id=1, source_target_pairs={{0,1},{1,0},{2,3},{3,2},{4,5},{5,4},{6,7},{7,6},{8,9},{9,8},{10,11... | collective-permute-start | bytes 25165832 | tf_op jit(solution)/shard_map/ppermute | solution.py:155
  104.2 10.8 %copy-start.4 = (f32[1,128]{1,0:T(1,128)S(1)}, f32[1,128]{1,0:T(1,128)}, u32[]{:S(2)}) copy-start(f32[1,128]{1,0:T(1,128)} %param.18) | copy-start | bytes 1540
  104.2 10.8 %copy-start.5 = (f32[1,128]{1,0:T(1,128)S(1)}, f32[1,128]{1,0:T(1,128)}, u32[]{:S(2)}) copy-start(f32[1,128]{1,0:T(1,128)} %param.17) | copy-start | bytes 1540
  105.0 18.5 %copy-start.2 = (bf16[1,64,4096]{2,1,0:T(8,128)(2,1)S(1)}, bf16[1,64,4096]{2,1,0:T(8,128)(2,1)}, u32[]{:S(2)}) copy-start(bf16[1,64,4096]{2,1,0:T(8,128)(2,1)} %param.10) | copy-start | bytes 1572868
  105.0 18.5 %copy-start.3 = (s32[4,1]{0,1:T(1,128)S(1)}, s32[4,1]{0,1:T(1,128)}, u32[]{:S(2)}) copy-start(s32[4,1]{0,1:T(1,128)} %param.12) | copy-start | bytes 52
  105.0 10.0 %collective-permute-start.12 = (bf16[4,4,16,256]{3,2,1,0:T(8,128)(2,1)S(1)}, bf16[4,4,16,256]{3,2,1,0:T(8,128)(2,1)S(1)}, u32[]{:S(2)}, u32[]{:S(2)}) collective-permute-start(bf16[4,4,16,256]{3,2,1,0:T(8,128)(2,1)S(1)} %get-tuple-element.39), channel_id=1, source_target_pairs={{0,256},{256,0},{512,768},{768,512},{1,257},{257,1},{513,769},{769... | collective-permute-start | bytes 393224 | tf_op jit(solution)/shard_map/ppermute | solution.py:155
  107.7 10.6 %collective-permute-start.14 = (bf16[4,4,16,256]{3,2,1,0:T(8,128)(2,1)S(1)}, bf16[4,4,16,256]{3,2,1,0:T(8,128)(2,1)S(1)}, u32[]{:S(2)}, u32[]{:S(2)}) collective-permute-start(bf16[4,4,16,256]{3,2,1,0:T(8,128)(2,1)S(1)} %get-tuple-element.40), channel_id=1, source_target_pairs={{0,768},{256,512},{512,256},{768,0},{1,769},{257,513},{513,257},{7... | collective-permute-start | bytes 393224 | tf_op jit(solution)/shard_map/ppermute | solution.py:155
  112.4 8.7 %collective-permute-start.13 = (bf16[4,4,16,256]{3,2,1,0:T(8,128)(2,1)S(1)}, bf16[4,4,16,256]{3,2,1,0:T(8,128)(2,1)S(1)}, u32[]{:S(2)}, u32[]{:S(2)}) collective-permute-start(bf16[4,4,16,256]{3,2,1,0:T(8,128)(2,1)S(1)} %get-tuple-element.41), channel_id=1, source_target_pairs={{0,512},{256,768},{512,0},{768,256},{1,513},{257,769},{513,1},{769... | collective-permute-start | bytes 393224 | tf_op jit(solution)/shard_map/ppermute | solution.py:155
  121.5 8.1 %collective-permute-start.15 = (bf16[2,64,256]{2,1,0:T(8,128)(2,1)S(1)}, bf16[2,64,256]{2,1,0:T(8,128)(2,1)S(1)}, u32[]{:S(2)}, u32[]{:S(2)}) collective-permute-start(bf16[2,64,256]{2,1,0:T(8,128)(2,1)S(1)} %dynamic-slice_bitcast_fusion.3), channel_id=1, source_target_pairs={{0,1},{1,0},{2,3},{3,2},{4,5},{5,4},{6,7},{7,6},{8,9},{9,8},{10,11... | collective-permute-start | bytes 196616 | tf_op jit(solution)/shard_map/ppermute | solution.py:155
  128.9 8.6 %collective-permute-start.18 = (bf16[64,4096]{1,0:T(8,128)(2,1)S(1)}, bf16[64,4096]{1,0:T(8,128)(2,1)S(1)}, u32[]{:S(2)}, u32[]{:S(2)}) collective-permute-start(bf16[64,4096]{1,0:T(8,128)(2,1)S(1)} %shard_map.101.refs_0_), channel_id=1, source_target_pairs={{1,3},{5,7},{9,11},{13,15},{17,19},{21,23},{25,27},{29,31},{33,35}... | collective-permute-start | bytes 1572872 | tf_op jit(solution)/shard_map/ppermute | solution.py:269
  135.1 9.0 %collective-permute-start.17 = (bf16[64,4096]{1,0:T(8,128)(2,1)S(1)}, bf16[64,4096]{1,0:T(8,128)(2,1)S(1)}, u32[]{:S(2)}, u32[]{:S(2)}) collective-permute-start(bf16[64,4096]{1,0:T(8,128)(2,1)S(1)} %shard_map.102.refs_2_), channel_id=1, source_target_pairs={{0,2},{4,6},{8,10},{12,14},{16,18},{20,22},{24,26},{28,30},{32,34}... | collective-permute-start | bytes 1572872 | tf_op jit(solution)/shard_map/ppermute | solution.py:271
  147.6 0.7 collective-permute-start.19
  151.8 15.0 %collective-permute-start.20 = (bf16[64,4096]{1,0:T(8,128)(2,1)S(1)}, bf16[64,4096]{1,0:T(8,128)(2,1)S(1)}, u32[]{:S(2)}, u32[]{:S(2)}) collective-permute-start(bf16[64,4096]{1,0:T(8,128)(2,1)S(1)} %shard_map.105), channel_id=1, source_target_pairs={{2,0},{6,4},{10,8},{14,12},{18,16},{22,20},{26,24},{30,28},{34,32}... | collective-permute-start | bytes 1572872 | tf_op jit(solution)/shard_map/ppermute | solution.py:276

commit v8 on v6

--- a/solution.py
+++ b/solution.py
@@ -19,9 +19,9 @@
     return projected * lax.rsqrt(mean_square + epsilon)
 
 
-def layer_kernel(slot, arrivals, choosing, section_ref, first_seen_ref, *refs):
+def layer_kernel(slot, arrivals, choosing, given, section_ref, first_seen_ref, *refs):
     states = refs[:arrivals]
-    rows_ref, weights_ref, out_ref, weights, sems = refs[arrivals:]
+    rows_ref, weights_ref, *sums_ref, out_ref, weights, sems = refs[arrivals:]
     rows, width = out_ref.shape
     columns = weights.shape[1]
     head_size = rows_ref.shape[2] // 2
@@ -42,10 +42,10 @@
 
     @pl.when(active)
     def _():
-        for piece in range(pieces):
+        for piece in range(width // depth if given else 0, pieces):
             fetch(piece).start()
-        query_sums = jnp.zeros((rows, columns), jnp.float32)
-        for piece in range(width // depth):
+        query_sums = sums_ref[0][...] if given else jnp.zeros((rows, columns), jnp.float32)
+        for piece in range(0 if given else width // depth):
             fetch(piece).wait()
             start = piece * depth
             query_sums += jnp.dot(
@@ -149,17 +149,18 @@
     return section == 2, jnp.int32(0), kept
 
 
-def layer(slot, section, first_seen, states, rows_by_batch, weights, choosing=1):
+def layer(slot, section, first_seen, states, rows_by_batch, weights, choosing=1, sums=()):
     rows, width = states[0].shape
     columns = weights.shape[1]
     smem = pl.BlockSpec(memory_space=pltpu.SMEM)
     vmem = pl.BlockSpec(memory_space=pltpu.VMEM)
     return pl.pallas_call(
-        functools.partial(layer_kernel, slot, len(states), choosing),
+        functools.partial(layer_kernel, slot, len(states), choosing, len(sums) == 1),
         out_shape=jax.ShapeDtypeStruct((rows, width), states[0].dtype),
         in_specs=[smem] * 2
         + [vmem] * (len(states) + 1)
-        + [pl.BlockSpec(memory_space=pl.ANY)],
+        + [pl.BlockSpec(memory_space=pl.ANY)]
+        + [vmem] * len(sums),
         out_specs=vmem,
         scratch_shapes=[
             pltpu.VMEM(weights.shape, weights.dtype),
@@ -171,7 +172,7 @@
             bytes_accessed=4 * width * columns,
             transcendentals=rows * columns,
         ),
-    )(section, first_seen, *states, rows_by_batch, weights)
+    )(section, first_seen, *states, rows_by_batch, weights, *sums)
 
 
 def exchanged(block, axis, distance):
@@ -253,6 +254,7 @@
     known = joined(known, "z", distance)
     known, halves, w_query, w_out = lax.optimization_barrier((known, halves, w_query, w_out))
     pictures = doubled(halves, "pipe", 1, 1)
+    query_sums = jnp.dot(text_states[0], w_query[0], preferred_element_type=jnp.float32)
     own_weights = stacked_weights(w_query[0], w_out[0])
     distance //= 2
     known = joined(known, "z", distance)
@@ -273,6 +275,7 @@
     for distance in range(1, parts):
         block = lax.dynamic_index_in_dim(rounded, own ^ distance, 1, keepdims=False)
         total = total + exchanged(block, "x", distance).astype(jnp.float32)
+    total, query_sums = lax.optimization_barrier((total, query_sums))
     total = jnp.swapaxes(total, 0, 1)
     total = total.reshape(total.shape[0], -1, 2 * head_size)
     key_scale = key_gain * query_gain
@@ -289,7 +292,7 @@
     run = functools.partial(layer, section=section, first_seen=first_seen)
     own = dict(rows_by_batch=own_rows, weights=own_weights)
     near = dict(rows_by_batch=near_rows, weights=near_weights)
-    first = run(slot_own, states=(text_states[0],), **own)
+    first = run(slot_own, states=(text_states[0],), sums=(query_sums,), **own)
     from_odd = lax.ppermute(first, "pipe", [(1, 3)])
     second = run(slot_second, states=(first,), **near)
     from_even = lax.ppermute(second, "pipe", [(0, 2)])

time: 165 us -> 163 us (0.988)
  transfers between devices with their start and end apart: 21 -> 21, of which waited for: 11 -> 11; matrix products, arithmetic and copies ran while one was open for 1% -> 2% of each run, Pallas kernels for 10% -> 9%
where the time goes in v8:
time: 163 us; the launch traced here: 162 us
  starting transfers between devices  84.8 us (52%)
  waiting for transfers between devices  53.5 us (33%)
  Pallas kernels  16.5 us (10%)
  other arithmetic  3.47 us (2%)
    ppermute x17, starting transfers between devices, exchanged(): return lax.ppermute(block, axis, [(i, i ^ distance) for i in devices])  79.4 us
    ppermute x17, waiting for transfers between devices, exchanged(): return lax.ppermute(block, axis, [(i, i ^ distance) for i in devices])  29.7 us
    ppermute x1, waiting for transfers between devices, local(): home_even = lax.ppermute(fourth, 'pipe', [(2, 0)])  17.8 us
    pallas_call x5, Pallas kernels, layer(): pl.pallas_call(functools.partial(layer_kernel, slot, len(states), choosin...  9.79 us
    pallas_call x1, Pallas kernels, stacked_weights(): pl.pallas_call(stack_kernel, out_shape=jax.ShapeDtypeStruct((2 * width, c...  6.69 us
    ppermute x1, waiting for transfers between devices, local(): from_even = lax.ppermute(second, 'pipe', [(0, 2)])  5.98 us
  transfers between devices with their start and end apart: 21, of which 11 were waited for; matrix products, arithmetic and copies ran while one was open for 2% of the time, Pallas kernels for 9%

profile of v8, /device:TPU:16, one launch (start us, length us, event | category | flops | bytes accessed | tf_op | source)
XLA Modules:
  0.0 162.4 jit_solution(4094898232825998362)
XLA Ops:
  0.0 0.7 maximum_bitcast_fusion.1
  0.7 14.9 %collective-permute-start = (bf16[1,16,256]{2,1,0:T(8,128)(2,1)S(1)}, bf16[1,16,256]{2,1,0:T(8,128)(2,1)S(1)}, u32[]{:S(2)}, u32[]{:S(2)}) collective-permute-start(bf16[1,16,256]{2,1,0:T(8,128)(2,1)S(1)} %maximum_bitcast_fusion.1), channel_id=1, source_target_pairs={{0,4},{4,0},{1,5},{5,1},{2,6},{6,2},{3,7},{7,3},{8,12},{12,8},{9,1... | collective-permute-start | bytes 24584 | tf_op jit(solution)/shard_map/ppermute | solution.py:180
  15.6 1.6 collective-permute-done
  17.2 0.7 select_bitcast_fusion.20
  17.9 6.2 %collective-permute-start.3 = (bf16[1,2,16,256]{3,2,1,0:T(8,128)(2,1)S(1)}, bf16[1,2,16,256]{3,2,1,0:T(8,128)(2,1)S(1)}, u32[]{:S(2)}, u32[]{:S(2)}) collective-permute-start(bf16[1,2,16,256]{3,2,1,0:T(8,128)(2,1)S(1)} %pad_maximum_fusion.7), channel_id=1, source_target_pairs={{0,64},{8,72},{16,80},{24,88},{32,96},{40,104},{48,112},{56,120},{... | collective-permute-start | bytes 49160 | tf_op jit(solution)/shard_map/ppermute | solution.py:180
  24.2 19.4 %collective-permute-start.2 = (bf16[1,2,16,256]{3,2,1,0:T(8,128)(2,1)S(1)}, bf16[1,2,16,256]{3,2,1,0:T(8,128)(2,1)S(1)}, u32[]{:S(2)}, u32[]{:S(2)}) collective-permute-start(bf16[1,2,16,256]{3,2,1,0:T(8,128)(2,1)S(1)} %pad_maximum_fusion.7), channel_id=1, source_target_pairs={{0,128},{8,136},{16,144},{24,152},{32,160},{40,168},{48,176},{56,1... | collective-permute-start | bytes 49160 | tf_op jit(solution)/shard_map/ppermute | solution.py:180
  43.6 1.9 %collective-permute-start.1 = (bf16[1,2,16,256]{3,2,1,0:T(8,128)(2,1)S(1)}, bf16[1,2,16,256]{3,2,1,0:T(8,128)(2,1)S(1)}, u32[]{:S(2)}, u32[]{:S(2)}) collective-permute-start(bf16[1,2,16,256]{3,2,1,0:T(8,128)(2,1)S(1)} %pad_maximum_fusion.7), channel_id=1, source_target_pairs={{0,192},{8,200},{16,208},{24,216},{32,224},{40,232},{48,240},{56,2... | collective-permute-start | bytes 49160 | tf_op jit(solution)/shard_map/ppermute | solution.py:180
  45.5 1.1 constant_dynamic-slice_fusion
  46.6 4.7 %collective-permute-start.6 = (bf16[4,16,1024]{2,1,0:T(8,128)(2,1)S(1)}, bf16[4,16,1024]{2,1,0:T(8,128)(2,1)S(1)}, u32[]{:S(2)}, u32[]{:S(2)}) collective-permute-start(bf16[4,16,1024]{2,1,0:T(8,128)(2,1)S(1)} %get-tuple-element.52), channel_id=1, source_target_pairs={{0,768},{256,512},{512,256},{768,0},{1,769},{257,513},{513,257},{7... | collective-permute-start | bytes 393224 | tf_op jit(solution)/shard_map/ppermute | solution.py:180
  51.3 2.7 %collective-permute-start.5 = (bf16[4,16,1024]{2,1,0:T(8,128)(2,1)S(1)}, bf16[4,16,1024]{2,1,0:T(8,128)(2,1)S(1)}, u32[]{:S(2)}, u32[]{:S(2)}) collective-permute-start(bf16[4,16,1024]{2,1,0:T(8,128)(2,1)S(1)} %get-tuple-element.53), channel_id=1, source_target_pairs={{0,512},{256,768},{512,0},{768,256},{1,513},{257,769},{513,1},{769... | collective-permute-start | bytes 393224 | tf_op jit(solution)/shard_map/ppermute | solution.py:180
  54.0 0.0 collective-permute-done.3
  54.0 2.4 %collective-permute-start.4 = (bf16[4,16,1024]{2,1,0:T(8,128)(2,1)S(1)}, bf16[4,16,1024]{2,1,0:T(8,128)(2,1)S(1)}, u32[]{:S(2)}, u32[]{:S(2)}) collective-permute-start(bf16[4,16,1024]{2,1,0:T(8,128)(2,1)S(1)} %get-tuple-element.54), channel_id=1, source_target_pairs={{0,256},{256,0},{512,768},{768,512},{1,257},{257,1},{513,769},{769... | collective-permute-start | bytes 393224 | tf_op jit(solution)/shard_map/ppermute | solution.py:180
  56.5 0.0 collective-permute-done.2
  56.5 1.6 collective-permute-done.1
  58.1 0.0 collective-permute-done.6
  58.1 2.3 %collective-permute-done.5 = bf16[4,16,1024]{2,1,0:T(8,128)(2,1)S(1)} collective-permute-done((bf16[4,16,1024]{2,1,0:T(8,128)(2,1)S(1)}, bf16[4,16,1024]{2,1,0:T(8,128)(2,1)S(1)}, u32[]{:S(2)}, u32[]{:S(2)}) %collective-permute-start.5) | collective-permute-done | bytes 131104 | tf_op jit(solution)/shard_map/ppermute | solution.py:180
  60.4 0.5 collective-permute-done.4
  60.9 0.1 select_bitcast_fusion.12
  61.0 0.1 pad_maximum_fusion.2
  61.0 3.2 %collective-permute-start.8 = (bf16[4,4,16,1024]{3,2,1,0:T(8,128)(2,1)S(1)}, bf16[4,4,16,1024]{3,2,1,0:T(8,128)(2,1)S(1)}, u32[]{:S(2)}, u32[]{:S(2)}) collective-permute-start(bf16[4,4,16,1024]{3,2,1,0:T(8,128)(2,1)S(1)} %pad_maximum_fusion.2), channel_id=1, source_target_pairs={{0,2},{1,3},{2,0},{3,1},{4,6},{5,7},{6,4},{7,5},{8,10},{9,11},{10,... | collective-permute-start | bytes 1572872 | tf_op jit(solution)/shard_map/ppermute | solution.py:180
  64.2 4.3 %collective-permute-start.7 = (bf16[4,2,16,256]{3,2,1,0:T(8,128)(2,1)S(1)}, bf16[4,2,16,256]{3,2,1,0:T(8,128)(2,1)S(1)}, u32[]{:S(2)}, u32[]{:S(2)}) collective-permute-start(bf16[4,2,16,256]{3,2,1,0:T(8,128)(2,1)S(1)} %maximum_bitcast_fusion), channel_id=1, source_target_pairs={{0,32},{8,40},{16,48},{24,56},{32,0},{40,8},{48,16},{56,24},{64,96... | collective-permute-start | bytes 196616 | tf_op jit(solution)/shard_map/ppermute | solution.py:180
  68.6 7.9 %collective-permute-done.7 = bf16[4,2,16,256]{3,2,1,0:T(8,128)(2,1)S(1)} collective-permute-done((bf16[4,2,16,256]{3,2,1,0:T(8,128)(2,1)S(1)}, bf16[4,2,16,256]{3,2,1,0:T(8,128)(2,1)S(1)}, u32[]{:S(2)}, u32[]{:S(2)}) %collective-permute-start.7) | collective-permute-done | bytes 65568 | tf_op jit(solution)/shard_map/ppermute | solution.py:180
  76.5 0.0 collective-permute-done.8
  76.5 0.1 select_bitcast_fusion.4
  76.6 0.1 pad_maximum_fusion.1
  76.7 1.9 %collective-permute-start.10 = (bf16[2,4,4,16,1024]{4,3,2,1,0:T(8,128)(2,1)S(1)}, bf16[2,4,4,16,1024]{4,3,2,1,0:T(8,128)(2,1)S(1)}, u32[]{:S(2)}, u32[]{:S(2)}) collective-permute-start(bf16[2,4,4,16,1024]{4,3,2,1,0:T(8,128)(2,1)S(1)} %pad_maximum_fusion.1), channel_id=1, source_target_pairs={{0,1},{1,0},{2,3},{3,2},{4,5},{5,4},{6,7},{7,6},{8,9},{9,8},{10,11... | collective-permute-start | bytes 3145736 | tf_op jit(solution)/shard_map/ppermute | solution.py:180
  78.6 2.1 %collective-permute-start.9 = (bf16[8,2,16,256]{3,2,1,0:T(8,128)(2,1)S(1)}, bf16[8,2,16,256]{3,2,1,0:T(8,128)(2,1)S(1)}, u32[]{:S(2)}, u32[]{:S(2)}) collective-permute-start(bf16[8,2,16,256]{3,2,1,0:T(8,128)(2,1)S(1)} %bitcast.122), channel_id=1, source_target_pairs={{0,16},{8,24},{16,0},{24,8},{32,48},{40,56},{48,32},{56,40},{64,80... | collective-permute-start | bytes 393224 | tf_op jit(solution)/shard_map/ppermute | solution.py:180
  80.7 9.2 %collective-permute-done.9 = bf16[8,2,16,256]{3,2,1,0:T(8,128)(2,1)S(1)} collective-permute-done((bf16[8,2,16,256]{3,2,1,0:T(8,128)(2,1)S(1)}, bf16[8,2,16,256]{3,2,1,0:T(8,128)(2,1)S(1)}, u32[]{:S(2)}, u32[]{:S(2)}) %collective-permute-start.9) | collective-permute-done | bytes 131104 | tf_op jit(solution)/shard_map/ppermute | solution.py:180
  90.0 0.1 select_bitcast_fusion.1
  90.1 0.2 pad_maximum_fusion
  90.3 1.9 %collective-permute-start.11 = (bf16[16,2,16,256]{3,2,1,0:T(8,128)(2,1)S(1)}, bf16[16,2,16,256]{3,2,1,0:T(8,128)(2,1)S(1)}, u32[]{:S(2)}, u32[]{:S(2)}) collective-permute-start(bf16[16,2,16,256]{3,2,1,0:T(8,128)(2,1)S(1)} %bitcast.120), channel_id=1, source_target_pairs={{0,8},{8,0},{16,24},{24,16},{32,40},{40,32},{48,56},{56,48},{64,72... | collective-permute-start | bytes 786440 | tf_op jit(solution)/shard_map/ppermute | solution.py:180
  92.2 0.0 copy-start.3
  92.3 0.0 copy-start.4
  92.3 6.7 %shard_map.100.refs_2_.refs_3_ = bf16[8192,512]{1,0:T(8,128)(2,1)} custom-call(bf16[4096,512]{1,0:T(8,128)(2,1)} %bitcast.113, bf16[512,4096]{1,0:T(8,128)(2,1)} %bitcast.115), custom_call_target="tpu_custom_call" | custom-call | bytes 16777216 | tf_op jit(solution)/shard_map/pallas_call | solution.py:113
  99.0 0.0 copy-start
  99.0 1.5 collective-permute-done.11
  100.5 0.1 pad_maximum_fusion.3
  100.6 1.9 %collective-permute-start.16 = (bf16[8192,512]{1,0:T(8,128)(2,1)}, bf16[8192,512]{1,0:T(8,128)(2,1)}, u32[]{:S(2)}, u32[]{:S(2)}) collective-permute-start(bf16[8192,512]{1,0:T(8,128)(2,1)} %shard_map.100.refs_2_.refs_3_), channel_id=1, source_target_pairs={{0,1},{1,0},{2,3},{3,2},{4,5},{5,4},{6,7},{7,6},{8,9},{9,8},{10,11... | collective-permute-start | bytes 25165832 | tf_op jit(solution)/shard_map/ppermute | solution.py:180
  103.3 0.0 copy-start.2
  103.3 0.7 fusion.5
  104.1 0.0 copy-start.1
  104.1 2.7 %collective-permute-start.12 = (bf16[4,4,16,256]{3,2,1,0:T(8,128)(2,1)S(1)}, bf16[4,4,16,256]{3,2,1,0:T(8,128)(2,1)S(1)}, u32[]{:S(2)}, u32[]{:S(2)}) collective-permute-start(bf16[4,4,16,256]{3,2,1,0:T(8,128)(2,1)S(1)} %get-tuple-element.43), channel_id=1, source_target_pairs={{0,256},{256,0},{512,768},{768,512},{1,257},{257,1},{513,769},{769... | collective-permute-start | bytes 393224 | tf_op jit(solution)/shard_map/ppermute | solution.py:180
  106.8 4.7 %collective-permute-start.14 = (bf16[4,4,16,256]{3,2,1,0:T(8,128)(2,1)S(1)}, bf16[4,4,16,256]{3,2,1,0:T(8,128)(2,1)S(1)}, u32[]{:S(2)}, u32[]{:S(2)}) collective-permute-start(bf16[4,4,16,256]{3,2,1,0:T(8,128)(2,1)S(1)} %get-tuple-element.44), channel_id=1, source_target_pairs={{0,768},{256,512},{512,256},{768,0},{1,769},{257,513},{513,257},{7... | collective-permute-start | bytes 393224 | tf_op jit(solution)/shard_map/ppermute | solution.py:180
  111.5 2.6 %collective-permute-start.13 = (bf16[4,4,16,256]{3,2,1,0:T(8,128)(2,1)S(1)}, bf16[4,4,16,256]{3,2,1,0:T(8,128)(2,1)S(1)}, u32[]{:S(2)}, u32[]{:S(2)}) collective-permute-start(bf16[4,4,16,256]{3,2,1,0:T(8,128)(2,1)S(1)} %get-tuple-element.45), channel_id=1, source_target_pairs={{0,512},{256,768},{512,0},{768,256},{1,513},{257,769},{513,1},{769... | collective-permute-start | bytes 393224 | tf_op jit(solution)/shard_map/ppermute | solution.py:180
  114.1 0.8 convolution_bitcast_fusion.refs_3_
  114.9 0.0 collective-permute-done.12
  115.0 2.5 %collective-permute-done.14 = bf16[4,4,16,256]{3,2,1,0:T(8,128)(2,1)S(1)} collective-permute-done((bf16[4,4,16,256]{3,2,1,0:T(8,128)(2,1)S(1)}, bf16[4,4,16,256]{3,2,1,0:T(8,128)(2,1)S(1)}, u32[]{:S(2)}, u32[]{:S(2)}) %collective-permute-start.14) | collective-permute-done | bytes 131104 | tf_op jit(solution)/shard_map/ppermute | solution.py:180
  117.4 2.8 %collective-permute-done.13 = bf16[4,4,16,256]{3,2,1,0:T(8,128)(2,1)S(1)} collective-permute-done((bf16[4,4,16,256]{3,2,1,0:T(8,128)(2,1)S(1)}, bf16[4,4,16,256]{3,2,1,0:T(8,128)(2,1)S(1)}, u32[]{:S(2)}, u32[]{:S(2)}) %collective-permute-start.13) | collective-permute-done | bytes 131104 | tf_op jit(solution)/shard_map/ppermute | solution.py:180
  120.2 0.1 fusion.1
  120.3 0.1 multiply_reduce_fusion
  120.4 0.1 multiply_convert_fusion
  120.6 1.9 %collective-permute-start.15 = (bf16[2,64,256]{2,1,0:T(8,128)(2,1)S(1)}, bf16[2,64,256]{2,1,0:T(8,128)(2,1)S(1)}, u32[]{:S(2)}, u32[]{:S(2)}) collective-permute-start(bf16[2,64,256]{2,1,0:T(8,128)(2,1)S(1)} %dynamic-slice_bitcast_fusion.3), channel_id=1, source_target_pairs={{0,1},{1,0},{2,3},{3,2},{4,5},{5,4},{6,7},{7,6},{8,9},{9,8},{10,11... | collective-permute-start | bytes 196616 | tf_op jit(solution)/shard_map/ppermute | solution.py:180
  122.5 3.1 %shard_map.101.refs_0_ = bf16[64,4096]{1,0:T(8,128)(2,1)S(1)} custom-call(s32[1]{0:T(128)} %bitcast.section_ref, s32[4]{0:T(128)S(1)} %bitcast.108, bf16[64,4096]{1,0:T(8,128)(2,1)S(1)} %bitcast.106, bf16[4,64,256]{2,1,0:T(8,128)(2,1)S(1)} %pad_maximum_fusion.6.refs_1_.refs_2_, bf16[8192,512]{1,0:T(8,128)(2,1)} %shard_map.100.refs_2_.refs_3_, ...), custom_call_target="tpu_custom_call" | custom-call | flops 536870912 | bytes 8388608 | tf_op jit(solution)/shard_map/pallas_call | solution.py:157
  125.6 0.7 collective-permute-start.18
  126.3 4.7 %shard_map.102.refs_2_ = bf16[64,4096]{1,0:T(8,128)(2,1)S(1)} custom-call(s32[1]{0:T(128)} %bitcast.section_ref, s32[4]{0:T(128)S(1)} %bitcast.109, bf16[64,4096]{1,0:T(8,128)(2,1)S(1)} %shard_map.101.refs_0_, bf16[2,64,256]{2,1,0:T(8,128)(2,1)S(1)} %collective-permute-done.15.refs_1_.refs_3_, bf16[8192,512]{1,0:T(8,128)(2,1)} %collective-permute-done.16.refs_2_.refs_4_), custom_call_target="tpu_custom_call" | custom-call | flops 536870912 | bytes 8388608 | tf_op jit(solution)/shard_map/pallas_call | solution.py:157
  131.1 2.7 %collective-permute-start.17 = (bf16[64,4096]{1,0:T(8,128)(2,1)S(1)}, bf16[64,4096]{1,0:T(8,128)(2,1)S(1)}, u32[]{:S(2)}, u32[]{:S(2)}) collective-permute-start(bf16[64,4096]{1,0:T(8,128)(2,1)S(1)} %shard_map.102.refs_2_), channel_id=1, source_target_pairs={{0,2},{4,6},{8,10},{12,14},{16,18},{20,22},{24,26},{28,30},{32,34}... | collective-permute-start | bytes 1572872 | tf_op jit(solution)/shard_map/ppermute | solution.py:298
  133.8 0.7 shard_map.103.refs_1_
  134.4 6.0 %collective-permute-done.17.refs_0_ = bf16[64,4096]{1,0:T(8,128)(2,1)S(1)} collective-permute-done((bf16[64,4096]{1,0:T(8,128)(2,1)S(1)}, bf16[64,4096]{1,0:T(8,128)(2,1)S(1)}, u32[]{:S(2)}, u32[]{:S(2)}) %collective-permute-start.17) | collective-permute-done | bytes 524320 | tf_op jit(solution)/shard_map/ppermute | solution.py:298
  140.4 0.7 shard_map.104.refs_0_
  141.1 0.7 collective-permute-start.19
  141.8 0.7 shard_map.105
  142.5 1.3 collective-permute-start.20
  143.8 17.8 %collective-permute-done.20 = bf16[64,4096]{1,0:T(8,128)(2,1)S(1)} collective-permute-done((bf16[64,4096]{1,0:T(8,128)(2,1)S(1)}, bf16[64,4096]{1,0:T(8,128)(2,1)S(1)}, u32[]{:S(2)}, u32[]{:S(2)}) %collective-permute-start.20) | collective-permute-done | bytes 524320 | tf_op jit(solution)/shard_map/ppermute | solution.py:303
  161.5 0.9 select_bitcast_fusion.2
  (26 shorter events, 0.3 us)
Async XLA Ops:
  0.7 16.5 %collective-permute-start = (bf16[1,16,256]{2,1,0:T(8,128)(2,1)S(1)}, bf16[1,16,256]{2,1,0:T(8,128)(2,1)S(1)}, u32[]{:S(2)}, u32[]{:S(2)}) collective-permute-start(bf16[1,16,256]{2,1,0:T(8,128)(2,1)S(1)} %maximum_bitcast_fusion.1), channel_id=1, source_target_pairs={{0,4},{4,0},{1,5},{5,1},{2,6},{6,2},{3,7},{7,3},{8,12},{12,8},{9,1... | collective-permute-start | bytes 24584 | tf_op jit(solution)/shard_map/ppermute | solution.py:180
  17.9 36.1 %collective-permute-start.3 = (bf16[1,2,16,256]{3,2,1,0:T(8,128)(2,1)S(1)}, bf16[1,2,16,256]{3,2,1,0:T(8,128)(2,1)S(1)}, u32[]{:S(2)}, u32[]{:S(2)}) collective-permute-start(bf16[1,2,16,256]{3,2,1,0:T(8,128)(2,1)S(1)} %pad_maximum_fusion.7), channel_id=1, source_target_pairs={{0,64},{8,72},{16,80},{24,88},{32,96},{40,104},{48,112},{56,120},{... | collective-permute-start | bytes 49160 | tf_op jit(solution)/shard_map/ppermute | solution.py:180
  24.2 32.3 %collective-permute-start.2 = (bf16[1,2,16,256]{3,2,1,0:T(8,128)(2,1)S(1)}, bf16[1,2,16,256]{3,2,1,0:T(8,128)(2,1)S(1)}, u32[]{:S(2)}, u32[]{:S(2)}) collective-permute-start(bf16[1,2,16,256]{3,2,1,0:T(8,128)(2,1)S(1)} %pad_maximum_fusion.7), channel_id=1, source_target_pairs={{0,128},{8,136},{16,144},{24,152},{32,160},{40,168},{48,176},{56,1... | collective-permute-start | bytes 49160 | tf_op jit(solution)/shard_map/ppermute | solution.py:180
  43.6 14.5 %collective-permute-start.1 = (bf16[1,2,16,256]{3,2,1,0:T(8,128)(2,1)S(1)}, bf16[1,2,16,256]{3,2,1,0:T(8,128)(2,1)S(1)}, u32[]{:S(2)}, u32[]{:S(2)}) collective-permute-start(bf16[1,2,16,256]{3,2,1,0:T(8,128)(2,1)S(1)} %pad_maximum_fusion.7), channel_id=1, source_target_pairs={{0,192},{8,200},{16,208},{24,216},{32,224},{40,232},{48,240},{56,2... | collective-permute-start | bytes 49160 | tf_op jit(solution)/shard_map/ppermute | solution.py:180
  46.6 11.5 %collective-permute-start.6 = (bf16[4,16,1024]{2,1,0:T(8,128)(2,1)S(1)}, bf16[4,16,1024]{2,1,0:T(8,128)(2,1)S(1)}, u32[]{:S(2)}, u32[]{:S(2)}) collective-permute-start(bf16[4,16,1024]{2,1,0:T(8,128)(2,1)S(1)} %get-tuple-element.52), channel_id=1, source_target_pairs={{0,768},{256,512},{512,256},{768,0},{1,769},{257,513},{513,257},{7... | collective-permute-start | bytes 393224 | tf_op jit(solution)/shard_map/ppermute | solution.py:180
  51.3 9.1 %collective-permute-start.5 = (bf16[4,16,1024]{2,1,0:T(8,128)(2,1)S(1)}, bf16[4,16,1024]{2,1,0:T(8,128)(2,1)S(1)}, u32[]{:S(2)}, u32[]{:S(2)}) collective-permute-start(bf16[4,16,1024]{2,1,0:T(8,128)(2,1)S(1)} %get-tuple-element.53), channel_id=1, source_target_pairs={{0,512},{256,768},{512,0},{768,256},{1,513},{257,769},{513,1},{769... | collective-permute-start | bytes 393224 | tf_op jit(solution)/shard_map/ppermute | solution.py:180
  54.0 6.9 %collective-permute-start.4 = (bf16[4,16,1024]{2,1,0:T(8,128)(2,1)S(1)}, bf16[4,16,1024]{2,1,0:T(8,128)(2,1)S(1)}, u32[]{:S(2)}, u32[]{:S(2)}) collective-permute-start(bf16[4,16,1024]{2,1,0:T(8,128)(2,1)S(1)} %get-tuple-element.54), channel_id=1, source_target_pairs={{0,256},{256,0},{512,768},{768,512},{1,257},{257,1},{513,769},{769... | collective-permute-start | bytes 393224 | tf_op jit(solution)/shard_map/ppermute | solution.py:180
  61.0 15.4 %collective-permute-start.8 = (bf16[4,4,16,1024]{3,2,1,0:T(8,128)(2,1)S(1)}, bf16[4,4,16,1024]{3,2,1,0:T(8,128)(2,1)S(1)}, u32[]{:S(2)}, u32[]{:S(2)}) collective-permute-start(bf16[4,4,16,1024]{3,2,1,0:T(8,128)(2,1)S(1)} %pad_maximum_fusion.2), channel_id=1, source_target_pairs={{0,2},{1,3},{2,0},{3,1},{4,6},{5,7},{6,4},{7,5},{8,10},{9,11},{10,... | collective-permute-start | bytes 1572872 | tf_op jit(solution)/shard_map/ppermute | solution.py:180
  64.2 12.2 %collective-permute-start.7 = (bf16[4,2,16,256]{3,2,1,0:T(8,128)(2,1)S(1)}, bf16[4,2,16,256]{3,2,1,0:T(8,128)(2,1)S(1)}, u32[]{:S(2)}, u32[]{:S(2)}) collective-permute-start(bf16[4,2,16,256]{3,2,1,0:T(8,128)(2,1)S(1)} %maximum_bitcast_fusion), channel_id=1, source_target_pairs={{0,32},{8,40},{16,48},{24,56},{32,0},{40,8},{48,16},{56,24},{64,96... | collective-permute-start | bytes 196616 | tf_op jit(solution)/shard_map/ppermute | solution.py:180
  76.7 13.3 %collective-permute-start.10 = (bf16[2,4,4,16,1024]{4,3,2,1,0:T(8,128)(2,1)S(1)}, bf16[2,4,4,16,1024]{4,3,2,1,0:T(8,128)(2,1)S(1)}, u32[]{:S(2)}, u32[]{:S(2)}) collective-permute-start(bf16[2,4,4,16,1024]{4,3,2,1,0:T(8,128)(2,1)S(1)} %pad_maximum_fusion.1), channel_id=1, source_target_pairs={{0,1},{1,0},{2,3},{3,2},{4,5},{5,4},{6,7},{7,6},{8,9},{9,8},{10,11... | collective-permute-start | bytes 3145736 | tf_op jit(solution)/shard_map/ppermute | solution.py:180
  78.6 11.3 %collective-permute-start.9 = (bf16[8,2,16,256]{3,2,1,0:T(8,128)(2,1)S(1)}, bf16[8,2,16,256]{3,2,1,0:T(8,128)(2,1)S(1)}, u32[]{:S(2)}, u32[]{:S(2)}) collective-permute-start(bf16[8,2,16,256]{3,2,1,0:T(8,128)(2,1)S(1)} %bitcast.122), channel_id=1, source_target_pairs={{0,16},{8,24},{16,0},{24,8},{32,48},{40,56},{48,32},{56,40},{64,80... | collective-permute-start | bytes 393224 | tf_op jit(solution)/shard_map/ppermute | solution.py:180
  90.3 10.2 %collective-permute-start.11 = (bf16[16,2,16,256]{3,2,1,0:T(8,128)(2,1)S(1)}, bf16[16,2,16,256]{3,2,1,0:T(8,128)(2,1)S(1)}, u32[]{:S(2)}, u32[]{:S(2)}) collective-permute-start(bf16[16,2,16,256]{3,2,1,0:T(8,128)(2,1)S(1)} %bitcast.120), channel_id=1, source_target_pairs={{0,8},{8,0},{16,24},{24,16},{32,40},{40,32},{48,56},{56,48},{64,72... | collective-permute-start | bytes 786440 | tf_op jit(solution)/shard_map/ppermute | solution.py:180
  92.2 11.0 %copy-start.3 = (f32[1,128]{1,0:T(1,128)S(1)}, f32[1,128]{1,0:T(1,128)}, u32[]{:S(2)}) copy-start(f32[1,128]{1,0:T(1,128)} %param.18) | copy-start | bytes 1540
  92.3 11.0 %copy-start.4 = (f32[1,128]{1,0:T(1,128)S(1)}, f32[1,128]{1,0:T(1,128)}, u32[]{:S(2)}) copy-start(f32[1,128]{1,0:T(1,128)} %param.17) | copy-start | bytes 1540
  99.0 15.1 %copy-start = (bf16[1,64,4096]{2,1,0:T(8,128)(2,1)S(1)}, bf16[1,64,4096]{2,1,0:T(8,128)(2,1)}, u32[]{:S(2)}) copy-start(bf16[1,64,4096]{2,1,0:T(8,128)(2,1)} %param.10) | copy-start | bytes 1572868
  100.6 25.7 %collective-permute-start.16 = (bf16[8192,512]{1,0:T(8,128)(2,1)}, bf16[8192,512]{1,0:T(8,128)(2,1)}, u32[]{:S(2)}, u32[]{:S(2)}) collective-permute-start(bf16[8192,512]{1,0:T(8,128)(2,1)} %shard_map.100.refs_2_.refs_3_), channel_id=1, source_target_pairs={{0,1},{1,0},{2,3},{3,2},{4,5},{5,4},{6,7},{7,6},{8,9},{9,8},{10,11... | collective-permute-start | bytes 25165832 | tf_op jit(solution)/shard_map/ppermute | solution.py:180
  103.3 10.8 %copy-start.2 = (bf16[1,4096,512]{2,1,0:T(8,128)(2,1)S(1)}, bf16[1,4096,512]{2,1,0:T(8,128)(2,1)}, u32[]{:S(2)}) copy-start(bf16[1,4096,512]{2,1,0:T(8,128)(2,1)} %param.13) | copy-start | bytes 12582916
  104.1 18.5 %copy-start.1 = (s32[4,1]{0,1:T(1,128)S(1)}, s32[4,1]{0,1:T(1,128)}, u32[]{:S(2)}) copy-start(s32[4,1]{0,1:T(1,128)} %param.12) | copy-start | bytes 52
  104.1 10.8 %collective-permute-start.12 = (bf16[4,4,16,256]{3,2,1,0:T(8,128)(2,1)S(1)}, bf16[4,4,16,256]{3,2,1,0:T(8,128)(2,1)S(1)}, u32[]{:S(2)}, u32[]{:S(2)}) collective-permute-start(bf16[4,4,16,256]{3,2,1,0:T(8,128)(2,1)S(1)} %get-tuple-element.43), channel_id=1, source_target_pairs={{0,256},{256,0},{512,768},{768,512},{1,257},{257,1},{513,769},{769... | collective-permute-start | bytes 393224 | tf_op jit(solution)/shard_map/ppermute | solution.py:180
  106.8 10.6 %collective-permute-start.14 = (bf16[4,4,16,256]{3,2,1,0:T(8,128)(2,1)S(1)}, bf16[4,4,16,256]{3,2,1,0:T(8,128)(2,1)S(1)}, u32[]{:S(2)}, u32[]{:S(2)}) collective-permute-start(bf16[4,4,16,256]{3,2,1,0:T(8,128)(2,1)S(1)} %get-tuple-element.44), channel_id=1, source_target_pairs={{0,768},{256,512},{512,256},{768,0},{1,769},{257,513},{513,257},{7... | collective-permute-start | bytes 393224 | tf_op jit(solution)/shard_map/ppermute | solution.py:180
  111.5 8.7 %collective-permute-start.13 = (bf16[4,4,16,256]{3,2,1,0:T(8,128)(2,1)S(1)}, bf16[4,4,16,256]{3,2,1,0:T(8,128)(2,1)S(1)}, u32[]{:S(2)}, u32[]{:S(2)}) collective-permute-start(bf16[4,4,16,256]{3,2,1,0:T(8,128)(2,1)S(1)} %get-tuple-element.45), channel_id=1, source_target_pairs={{0,512},{256,768},{512,0},{768,256},{1,513},{257,769},{513,1},{769... | collective-permute-start | bytes 393224 | tf_op jit(solution)/shard_map/ppermute | solution.py:180
  120.6 5.7 %collective-permute-start.15 = (bf16[2,64,256]{2,1,0:T(8,128)(2,1)S(1)}, bf16[2,64,256]{2,1,0:T(8,128)(2,1)S(1)}, u32[]{:S(2)}, u32[]{:S(2)}) collective-permute-start(bf16[2,64,256]{2,1,0:T(8,128)(2,1)S(1)} %dynamic-slice_bitcast_fusion.3), channel_id=1, source_target_pairs={{0,1},{1,0},{2,3},{3,2},{4,5},{5,4},{6,7},{7,6},{8,9},{9,8},{10,11... | collective-permute-start | bytes 196616 | tf_op jit(solution)/shard_map/ppermute | solution.py:180
  125.6 8.1 %collective-permute-start.18 = (bf16[64,4096]{1,0:T(8,128)(2,1)S(1)}, bf16[64,4096]{1,0:T(8,128)(2,1)S(1)}, u32[]{:S(2)}, u32[]{:S(2)}) collective-permute-start(bf16[64,4096]{1,0:T(8,128)(2,1)S(1)} %shard_map.101.refs_0_), channel_id=1, source_target_pairs={{1,3},{5,7},{9,11},{13,15},{17,19},{21,23},{25,27},{29,31},{33,35}... | collective-permute-start | bytes 1572872 | tf_op jit(solution)/shard_map/ppermute | solution.py:296
  131.1 9.3 %collective-permute-start.17 = (bf16[64,4096]{1,0:T(8,128)(2,1)S(1)}, bf16[64,4096]{1,0:T(8,128)(2,1)S(1)}, u32[]{:S(2)}, u32[]{:S(2)}) collective-permute-start(bf16[64,4096]{1,0:T(8,128)(2,1)S(1)} %shard_map.102.refs_2_), channel_id=1, source_target_pairs={{0,2},{4,6},{8,10},{12,14},{16,18},{20,22},{24,26},{28,30},{32,34}... | collective-permute-start | bytes 1572872 | tf_op jit(solution)/shard_map/ppermute | solution.py:298
  141.1 0.7 collective-permute-start.19
  142.5 19.1 %collective-permute-start.20 = (bf16[64,4096]{1,0:T(8,128)(2,1)S(1)}, bf16[64,4096]{1,0:T(8,128)(2,1)S(1)}, u32[]{:S(2)}, u32[]{:S(2)}) collective-permute-start(bf16[64,4096]{1,0:T(8,128)(2,1)S(1)} %shard_map.105), channel_id=1, source_target_pairs={{2,0},{6,4},{10,8},{14,12},{18,16},{22,20},{26,24},{30,28},{34,32}... | collective-permute-start | bytes 1572872 | tf_op jit(solution)/shard_map/ppermute | solution.py:303
